TPU v7x, 32 devices: a whole 2x2x4 slice. The times are simulated.
32 devices in a mesh: adv: 2 (over y), imp: 16 (over z, x, core).
Axes of the slice: x: 2, y: 2, z: 4, core: 2. Of those that a mesh axis runs over, the one named last changes fastest.
Arguments:
- adv_embed: float32 [4096, 64], P(('adv', 'imp')), may hold values from -5 to 5
- imp_embed: float32 [8192, 64], P(('imp', 'adv')), may hold values from -5 to 5
- value_scale: float32 [4096], P('adv'), may hold values from 0.3 to 3
- spend_class: int32 [4096], P('adv'), may hold values from 0 to 7
- eligible: int32 [32, 64], P('adv', 'imp'), may hold values from 0 to 1, as said below
Outputs:
- bid_density: float32 [4096, 8192], P('adv', 'imp')
- prices: float32 [8192], P('imp')
- pacing: float32 [4096], P('adv')
Inputs may be any that keep to these rules, and one draw needn't show every extreme that they name: Every impression block is eligible for at least one advertiser block.
All inputs are finite; a program needn't handle non-finite values.
Results may differ from a plain program's by a relative error of at most 0.0002.
Values sent between devices are 32-bit elements; how exact they have to be, the bound alone decides.
No kernel may reach another device: no remote copies, remote signals or barrier semaphores. Data moves between devices by JAX's collectives and lax.ppermute only.
A program may use at most 64 MiB of HBM per device.

v0:
```python
import jax
import jax.numpy as jnp
from jax import lax
from jax.sharding import PartitionSpec as P

BLOCK = 128
ITERS = 2


score_gain = 0.0875


def score_block(embed_rows, imp_block):
    return (
        jnp.einsum(
            "ae,ie->ai",
            embed_rows,
            imp_block,
            precision=lax.Precision.HIGHEST,
            preferred_element_type=jnp.float32,
        )
        * score_gain
    )


def per_device(adv_embed, imp_embed, value_scale, spend_class, eligible):
    imp_block = lax.all_gather(imp_embed, "adv", axis=0, tiled=True)
    scores = score_block(lax.all_gather(adv_embed, "imp", axis=0, tiled=True), imp_block)
    adv_count = scores.shape[0]
    imp_count = scores.shape[1]
    total_advs = adv_count * lax.axis_size("adv")
    total_imps = imp_count * lax.axis_size("imp")
    mask_rows = eligible.shape[0]
    mask_cols = eligible.shape[1]
    expanded = jnp.broadcast_to(
        eligible.astype(jnp.float32)[:, None, :, None], (mask_rows, BLOCK, mask_cols, BLOCK)
    )
    blocks_mask = expanded.reshape(adv_count, imp_count)
    values = value_scale[:, None] * jnp.exp(scores) * blocks_mask
    allowance = total_imps / total_advs * jnp.exp(0.3 * spend_class.astype(jnp.float32) - 1.2)
    bid_tile = blocks_mask * allowance[:, None] / total_imps
    prices = jnp.ones((imp_count,), jnp.float32)
    pacing = jnp.ones((adv_count,), jnp.float32)
    for step in range(ITERS):
        prices = lax.psum(jnp.sum(bid_tile, axis=0), "adv")
        gain = values * bid_tile / prices[None, :]
        row_totals = jnp.sum(gain, axis=1)
        spending = lax.psum(row_totals, "imp")
        pacing = allowance / jnp.maximum(spending, allowance)
        bid_tile = pacing[:, None] * gain
    return (bid_tile * total_advs, prices, pacing)


def solution(mesh):
    in_specs = (
        P(("adv", "imp"), None),
        P(("imp", "adv"), None),
        P("adv"),
        P("adv"),
        P("adv", "imp"),
    )
    out_specs = (P("adv", "imp"), P("imp"), P("adv"))
    return jax.shard_map(
        per_device, mesh=mesh, in_specs=in_specs, out_specs=out_specs, check_vma=False
    )
```

profile of v0, /device:TPU:0, one launch (start us, length us, event | category | flops | bytes accessed | tf_op | source)
XLA Modules:
  0.0 131.1 jit_solution(4042350924673673762)
XLA Ops:
  0.6 0.0 copy-start.3
  0.6 0.7 convert_element_type.7
  1.3 0.7 exponential_multiply_fusion
  2.0 1.2 multiply_reduce_fusion
  3.2 5.9 %psum.28 = f32[512]{0:T(512)S(1)} all-reduce(f32[512]{0:T(512)S(1)} %bitcast.20), channel_id=1, replica_groups=mesh['adv'=2,'imp'=16] {'adv'}, use_global_device_ids=true, to_apply=%region_1.0 | all-reduce | flops 512 | bytes 4096 | tf_op jit(solution)/shard_map/psum | solution.py:45
  9.1 5.2 %all_gather.7 = f32[512,64]{0,1:T(8,128)S(1)} all-gather(f32[256,64]{0,1:T(8,128)} %param.6), channel_id=1, replica_groups=mesh['adv'=2,'imp'=16] {'adv'}, dimensions={0}, use_global_device_ids=true | all-gather | bytes 196608 | tf_op jit(solution)/shard_map/all_gather | solution.py:27
  14.3 23.9 %all_gather.6 = f32[2048,64]{0,1:T(8,128)S(1)} all-gather(f32[128,64]{0,1:T(8,128)} %param.5), channel_id=1, replica_groups=mesh['adv'=2,'imp'=16] {'imp'}, dimensions={0}, use_global_device_ids=true | all-gather | bytes 557056 | tf_op jit(solution)/shard_map/all_gather | solution.py:28
  38.2 0.3 broadcast_in_dim.2
  38.6 0.0 copy-done.3
  38.6 0.0 copy-start
  38.6 8.1 %fusion.5 = (f32[2048]{0:T(1024)S(1)}, f32[2048,512]{0,1:T(8,128)}, f32[2048,512]{0,1:T(8,128)}) fusion(f32[512]{0:T(512)S(1)} %psum.28, f32[2048]{0:T(1024)S(1)} %get-tuple-element.8, f32[64,8,16,128]{3,2,1,0:T(8,128)S(1)} %bitcast.19, f32[2048,64]{0,1:T(8,128)S(1)} %all_gather.6, f32[512,64]{0,1:T(8,128)S(1)} %all_gather.7, f32[2048]{0:T(1024)S(1)} %copy-done.3), kind=kOutput, calls=%fused_computation.14 | convolution fusion | flops 813692928 | bytes 13264896 | tf_op jit(solution)/shard_map/ae,ie->ai/dot_general | solution.py:15
  46.7 30.3 %psum.29 = f32[2048]{0:T(1024)S(1)} all-reduce(f32[2048]{0:T(1024)S(1)} %get-tuple-element.6), channel_id=1, replica_groups=mesh['adv'=2,'imp'=16] {'imp'}, use_global_device_ids=true, to_apply=%region_3.0 | all-reduce | flops 2048 | bytes 16384 | tf_op jit(solution)/shard_map/psum | solution.py:48
  77.0 0.0 copy-done
  77.1 2.5 %multiply_reduce_fusion.1 = f32[512]{0:T(512)S(1)} fusion(f32[2048,512]{0,1:T(8,128)} %get-tuple-element.7, f32[2048]{0:T(1024)S(1)} %maximum_divide_fusion.1), kind=kLoop, calls=%fused_computation.8 | loop fusion | flops 2096640 | bytes 4204544 | tf_op jit(solution)/shard_map/reduce_sum | solution.py:45
  79.6 4.9 %psum.30 = f32[512]{0:T(512)S(1)} all-reduce(f32[512]{0:T(512)S(1)} %multiply_reduce_fusion.1), channel_id=1, replica_groups=mesh['adv'=2,'imp'=16] {'adv'}, use_global_device_ids=true, to_apply=%region_5.0 | all-reduce | flops 512 | bytes 4096 | tf_op jit(solution)/shard_map/psum | solution.py:45
  84.6 0.0 copy-start.2
  84.6 4.3 %fusion.4 = f32[2048]{0:T(1024)S(1)} fusion(f32[512]{0:T(512)S(1)} %psum.30, f32[2048,512]{0,1:T(8,128)} %get-tuple-element.10, f32[2048,512]{0,1:T(8,128)} %get-tuple-element.7, f32[2048]{0:T(1024)S(1)} %maximum_divide_fusion.1), kind=kLoop, calls=%fused_computation.13 | loop fusion | flops 4192256 | bytes 8407040 | tf_op jit(solution)/shard_map/reduce_sum | solution.py:47
  88.9 30.0 %psum.31 = f32[2048]{0:T(1024)S(1)} all-reduce(f32[2048]{0:T(1024)S(1)} %fusion.4), channel_id=1, replica_groups=mesh['adv'=2,'imp'=16] {'imp'}, use_global_device_ids=true, to_apply=%region_7.0 | all-reduce | flops 2048 | bytes 16384 | tf_op jit(solution)/shard_map/psum | solution.py:48
  118.9 0.0 copy-done.2
  118.9 0.0 copy-start.1
  118.9 6.9 %multiply_multiply_fusion = f32[2048,512]{0,1:T(8,128)} fusion(f32[2048]{0:T(1024)S(1)} %maximum_divide_fusion, f32[512]{0:T(512)S(1)} %psum.30, f32[2048,512]{0,1:T(8,128)} %get-tuple-element.10, f32[2048,512]{0,1:T(8,128)} %get-tuple-element.7, f32[2048]{0:T(1024)S(1)} %maximum_divide_fusion.1), kind=kLoop, calls=%fused_computation.5 | loop fusion | flops 5242880 | bytes 12601344 | tf_op jit(solution)/shard_map/mul | solution.py:51
  125.8 0.0 copy-done.1
  125.8 5.3 %copy.8 = f32[2048,512]{1,0:T(8,128)} copy(f32[2048,512]{0,1:T(8,128)} %multiply_multiply_fusion) | data formatting | bytes 8388608
  (2 shorter events, 0.0 us)
Async XLA Ops:
  0.6 37.9 %copy-start.3 = (f32[2048]{0:T(1024)S(1)}, f32[2048]{0:T(1024)}, u32[]{:S(2)}) copy-start(f32[2048]{0:T(1024)} %param.7) | copy-start | bytes 24580
  38.6 38.5 %copy-start = (s32[2048]{0:T(1024)S(1)}, s32[2048]{0:T(1024)}, u32[]{:S(2)}) copy-start(s32[2048]{0:T(1024)} %param.8) | copy-start | bytes 24580
  84.6 34.4 %copy-start.2 = (f32[512]{0:T(512)}, f32[512]{0:T(512)S(1)}, u32[]{:S(2)}) copy-start(f32[512]{0:T(512)S(1)} %psum.30) | copy-start | bytes 6148
  118.9 6.9 %copy-start.1 = (f32[2048]{0:T(1024)}, f32[2048]{0:T(1024)S(1)}, u32[]{:S(2)}) copy-start(f32[2048]{0:T(1024)S(1)} %maximum_divide_fusion) | copy-start | bytes 24580
where the time goes:
time: 132 us; the launch traced here: 131 us
  blocking collectives  100 us (76%)
  other arithmetic  16.3 us (12%)
  matrix products  8.14 us (6%)
  local copies, waits for them, and re-layouts  5.69 us (4%)
    psum x2, blocking collectives, per_device(): spending = lax.psum(row_totals, 'imp')  60.3 us
    all_gather x1, blocking collectives, per_device(): lax.all_gather(adv_embed, 'imp', axis=0, tiled=True)  23.9 us
    psum x2, blocking collectives, per_device(): prices = lax.psum(jnp.sum(bid_tile, axis=0), 'adv')  10.8 us
    dot_general x1, matrix products, score_block(): jnp.einsum('ae,ie->ai', embed_rows, imp_block, precision=lax.Precision.HI...  8.14 us
    mul x1, other arithmetic, per_device(): return (bid_tile * total_advs, prices, pacing)  6.86 us
    unnamed x9, local copies, waits for them, and re-layouts  5.36 us
    all_gather x1, blocking collectives, per_device(): imp_block = lax.all_gather(imp_embed, 'adv', axis=0, tiled=True)  5.21 us
    reduce_sum x1, other arithmetic, per_device(): row_totals = jnp.sum(gain, axis=1)  4.33 us

commit v1 on v0

v1 whole, which is shorter than its diff:
```python
import math

import jax
import jax.numpy as jnp
from jax import lax
from jax.experimental import pallas as pl
from jax.experimental.pallas import tpu as pltpu
from jax.sharding import PartitionSpec as P

BLOCK = 128
ITERS = 2
SCORE_GAIN = 0.0875
LOG2E = 1.4426950408889634
OFF = 1e30
DEPTH = 208

VMEM = pl.BlockSpec(memory_space=pltpu.VMEM)
SMEM = pl.BlockSpec(memory_space=pltpu.SMEM)
PARAMS = pltpu.CompilerParams(vmem_limit_bytes=48 * 1024 * 1024)


def pieces(x):
    first = x.astype(jnp.bfloat16).astype(jnp.float32)
    rest = x - first
    second = rest.astype(jnp.bfloat16).astype(jnp.float32)
    third = (rest - second).astype(jnp.bfloat16).astype(jnp.float32)
    return first, second, third


def allowance_of(spend_class, ratio):
    return ratio * jnp.exp(0.3 * spend_class.astype(jnp.float32) - 1.2)


def prepare_kernel(ratio, imps, elig_ref, class_ref, scale_ref, imp_ref, pack_ref, extra_ref):
    spend_class = class_ref[...].astype(jnp.float32)
    allowance = allowance_of(class_ref[...], ratio) / imps
    log_scale = jnp.log(scale_ref[...]) * LOG2E + ((0.3 * spend_class - 1.2) * LOG2E + math.log2(ratio / imps))
    parts = pieces(log_scale)
    rows, cols = class_ref.shape[0], elig_ref.shape[0]
    width = imp_ref.shape[1]
    pack_ref[0:64, :] = imp_ref[...]
    ones = jnp.ones((1, BLOCK), jnp.float32)
    sums = [jnp.zeros((1, BLOCK), jnp.float32) for _ in range(cols)]
    for b in range(rows):
        masks = []
        for c in range(cols):
            flag = elig_ref[c, b].astype(jnp.float32)
            sums[c] = sums[c] + flag * allowance[b : b + 1]
            masks.append(ones * ((flag - 1.0) * OFF))
        block = masks + [p[b : b + 1] for p in parts] + [ones] * 3
        block += [jnp.zeros((16 - len(block), BLOCK), jnp.float32)]
        extra_ref[:, b * BLOCK : (b + 1) * BLOCK] = jnp.concatenate(block, axis=0)
    totals = jnp.concatenate(
        [jnp.broadcast_to(jnp.sum(s, axis=1, keepdims=True), (1, BLOCK)) for s in sums], axis=1
    )
    pack_ref[64:72, :] = jnp.zeros((8, width), jnp.float32)
    for r in range(cols * BLOCK // width):
        pack_ref[64 + r : 65 + r, :] = totals[:, r * width : (r + 1) * width]


def first_kernel(groups, cols, place_ref, *refs):
    adv_refs = refs[:groups]
    own_ref, other_ref, extra_ref, gain_ref, sums_ref, price_ref, rhs_ref, lhs_ref, step_ref = refs[groups:]
    order, half = place_ref[0], place_ref[1]
    width = own_ref.shape[1]
    count = cols * BLOCK
    for ref, at in ((own_ref, half * width), (other_ref, (1 - half) * width)):
        block = ref[0:64, :] * (SCORE_GAIN * LOG2E)
        high = block.astype(jnp.bfloat16)
        low = (block - high.astype(jnp.float32)).astype(jnp.bfloat16)
        at = pl.multiple_of(at, width)
        lhs_ref[0:64, pl.ds(at, width)] = high
        lhs_ref[64:128, pl.ds(at, width)] = low
        lhs_ref[128:192, pl.ds(at, width)] = high
    price_parts = own_ref[64:72, :] + other_ref[64:72, :]
    price = jnp.concatenate([price_parts[r : r + 1] for r in range(count // width)], axis=1)
    column = lax.broadcasted_iota(jnp.int32, (1, count), 1) // BLOCK
    rows = [(column == c).astype(jnp.float32) for c in range(cols)]
    rows += [jnp.ones((1, count), jnp.float32)] * 3
    rows += list(pieces(-jnp.log(price) * LOG2E))
    rows += [jnp.zeros((16 - len(rows), count), jnp.float32)]
    lhs_ref[192:208, :] = jnp.concatenate(rows, axis=0).astype(jnp.bfloat16)
    for c in range(cols):
        price_ref[c : c + 1, :] = price[:, c * BLOCK : (c + 1) * BLOCK]
    lhs = lhs_ref[...].T
    k = 0
    for ref in adv_refs:
        for p in range(ref.shape[0]):
            lanes = slice(k * BLOCK, (k + 1) * BLOCK)
            b = order ^ k
            block = ref[p]
            high = block.astype(jnp.bfloat16)
            low = (block - high.astype(jnp.float32)).astype(jnp.bfloat16)
            rhs_ref[0:64, lanes] = high
            rhs_ref[64:128, lanes] = high
            rhs_ref[128:192, lanes] = low
            rhs_ref[192:208, lanes] = extra_ref[:, pl.ds(pl.multiple_of(b * BLOCK, BLOCK), BLOCK)].astype(jnp.bfloat16)
            k += 1
            if k % 2 == 0:
                two = slice((k - 2) * BLOCK, k * BLOCK)
                gain = jnp.exp2(jnp.dot(lhs, rhs_ref[:, two], preferred_element_type=jnp.float32))
                gain_ref[:, two] = gain
                sums = jnp.sum(gain, axis=0, keepdims=True)
                sums_ref[pl.ds(order ^ (k - 2), 1), :] = sums[:, :BLOCK]
                sums_ref[pl.ds(order ^ (k - 1), 1), :] = sums[:, BLOCK:]


def prices_kernel(ratio, place_ref, gain_ref, class_ref, *refs):
    *sum_refs, part_ref, pacing_ref = refs
    order = place_ref[0]
    allowance = allowance_of(class_ref[...], ratio)
    pacing_ref[...] = allowance / jnp.maximum(tree([r[...] for r in sum_refs]), allowance)
    blocks = class_ref.shape[0]
    for c in range(gain_ref.shape[0] // BLOCK):
        total = jnp.zeros((BLOCK, BLOCK), jnp.float32)
        for k in range(blocks):
            gain = gain_ref[c * BLOCK : (c + 1) * BLOCK, k * BLOCK : (k + 1) * BLOCK]
            total = total + gain * pacing_ref[pl.ds(order ^ k, 1), :]
        part_ref[c : c + 1, :] = jnp.sum(total.T, axis=0, keepdims=True)


def second_kernel(ratio, imps, place_ref, gain_ref, class_ref, pacing_ref, price_ref, *refs):
    *part_refs, next_ref, sums_ref, prices_ref, factor_ref, step_ref = refs
    order = place_ref[0]
    prices = tree([r[...] for r in part_refs])
    prices_ref[...] = prices
    ratio_rows = price_ref[...] / prices
    factor_ref[...] = pacing_ref[...] * (imps / allowance_of(class_ref[...], ratio))
    blocks = class_ref.shape[0]
    count = gain_ref.shape[0]
    for c in range(count // BLOCK):
        step_ref[c * BLOCK : (c + 1) * BLOCK, :] = jnp.broadcast_to(ratio_rows[c : c + 1], (BLOCK, BLOCK)).T
    for k in range(blocks):
        lanes = slice(k * BLOCK, (k + 1) * BLOCK)
        factor = factor_ref[pl.ds(order ^ k, 1), :]
        total = jnp.zeros((8, BLOCK), jnp.float32)
        for c in range(count // BLOCK):
            rows = slice(c * BLOCK, (c + 1) * BLOCK)
            gain = gain_ref[rows, lanes]
            new = (gain * factor) * (gain * step_ref[rows, :])
            next_ref[rows, lanes] = new
            total = total + jnp.sum(new.reshape(BLOCK // 8, 8, BLOCK), axis=0)
        sums_ref[pl.ds(order ^ k, 1), :] = jnp.sum(total, axis=0, keepdims=True)


def final_kernel(ratio, advs, per_step, place_ref, gain_ref, class_ref, *refs):
    *sum_refs, out_ref, pacing_ref, factor_ref = refs
    order = place_ref[0]
    step = pl.program_id(0)

    @pl.when(step == 0)
    def _():
        allowance = allowance_of(class_ref[...], ratio)
        pacing = allowance / jnp.maximum(tree([r[...] for r in sum_refs]), allowance)
        pacing_ref[...] = pacing
        factor_ref[...] = pacing * advs

    for p in range(per_step):
        b = step * per_step + p
        factor = factor_ref[pl.ds(b, 1), :]
        lanes = pl.ds(pl.multiple_of((b ^ order) * BLOCK, BLOCK), BLOCK)
        for c in range(gain_ref.shape[0] // BLOCK):
            block = gain_ref[c * BLOCK : (c + 1) * BLOCK, lanes] * factor
            out_ref[p * BLOCK : (p + 1) * BLOCK, c * BLOCK : (c + 1) * BLOCK] = block.T


def tree(terms):
    while len(terms) > 1:
        terms = [a + b for a, b in zip(terms[::2], terms[1::2])]
    return terms[0]


def swap(x, axis, k):
    return lax.ppermute(x, axis, [(i, i ^ k) for i in range(lax.axis_size(axis))])


def with_partners(x, axis, keys):
    return [x] + [swap(x, axis, k) for k in keys]


def stages(n):
    found, bit = [], 1
    while bit < n:
        found.append((bit, 2 * bit, 3 * bit) if 4 * bit <= n else (bit,))
        bit *= 4
    return found


def terms_of_sum(x, axis):
    n = lax.axis_size(axis)
    if n & (n - 1):
        return [lax.psum(x, axis)]
    todo = stages(n)
    for keys in todo[:-1]:
        x = tree(with_partners(x, axis, keys))
    return with_partners(x, axis, todo[-1])


def per_device(adv_embed, imp_embed, value_scale, spend_class, eligible):
    n_adv, n_imp = lax.axis_size("adv"), lax.axis_size("imp")
    adv_count = spend_class.shape[0]
    rows, cols = eligible.shape
    imp_count = cols * BLOCK
    imps, advs = imp_count * n_imp, adv_count * n_adv
    ratio = imps / advs
    f32 = jnp.float32
    class_rows = spend_class.reshape(rows, BLOCK)
    scale_rows = value_scale.reshape(rows, BLOCK)

    def shape(*dims):
        return jax.ShapeDtypeStruct(dims, f32)

    staged = n_imp == 16 and adv_embed.shape[0] == BLOCK and n_adv == 2
    imp_t = imp_embed.T
    if not staged:
        imp_t = lax.all_gather(imp_embed, "adv", axis=0, tiled=True).T[:, : imp_count // 2]
    width = imp_t.shape[1]
    pack, extra = pl.pallas_call(
        lambda *refs: prepare_kernel(ratio, imps, *refs),
        out_shape=(shape(72, width), shape(16, adv_count)),
        in_specs=[SMEM, VMEM, VMEM, VMEM],
        out_specs=(VMEM, VMEM),
        compiler_params=PARAMS,
    )(eligible.T, class_rows, scale_rows, imp_t)
    if staged:
        me, half = lax.axis_index("imp"), lax.axis_index("adv")
        line = jnp.stack(with_partners(adv_embed.T, "imp", (4, 8, 12)))
        other = swap(pack, "adv", 1)
        line, other = lax.optimization_barrier((line, other))
        plane = jnp.stack([line, swap(line, "imp", 2)], axis=1)
        pair = swap(plane, "imp", 1)
        adv_blocks = [jnp.stack([plane, pair], axis=2).reshape(rows, 64, BLOCK)]
    else:
        me, half = jnp.int32(0), jnp.int32(0)
        gathered = lax.all_gather(adv_embed, "imp", axis=0, tiled=True)
        adv_blocks = [gathered.reshape(rows, BLOCK, 64).transpose(0, 2, 1)]
        whole = lax.all_gather(imp_embed, "adv", axis=0, tiled=True).T[:, imp_count // 2 :]
        price = lax.psum(pack[64:], "adv")
        other = jnp.concatenate([whole, jnp.zeros_like(price)])
        pack = jnp.concatenate([pack[:64], price])
    place = jnp.stack([me, half]).astype(jnp.int32)

    gain, sums, first_price = pl.pallas_call(
        lambda *refs: first_kernel(len(adv_blocks), cols, *refs),
        out_shape=(pltpu.VMEM((imp_count, adv_count), f32), shape(rows, BLOCK), shape(cols, BLOCK)),
        in_specs=[SMEM] + [VMEM] * (len(adv_blocks) + 3),
        out_specs=(VMEM, VMEM, VMEM),
        scratch_shapes=[
            pltpu.VMEM((DEPTH, adv_count), jnp.bfloat16),
            pltpu.VMEM((DEPTH, imp_count), jnp.bfloat16),
            pltpu.VMEM((8, BLOCK), f32),
        ],
        compiler_params=PARAMS,
    )(place, *adv_blocks, pack, other, extra)

    terms = terms_of_sum(sums, "imp")
    part, pacing = pl.pallas_call(
        lambda *refs: prices_kernel(ratio, *refs),
        out_shape=(shape(cols, BLOCK), shape(rows, BLOCK)),
        in_specs=[SMEM] + [VMEM] * (2 + len(terms)),
        out_specs=(VMEM, VMEM),
        compiler_params=PARAMS,
    )(place, gain, class_rows, *terms)

    terms = terms_of_sum(part, "adv")
    gain, sums, prices = pl.pallas_call(
        lambda *refs: second_kernel(ratio, imps, *refs),
        out_shape=(pltpu.VMEM((imp_count, adv_count), f32), shape(rows, BLOCK), shape(cols, BLOCK)),
        in_specs=[SMEM] + [VMEM] * (4 + len(terms)),
        out_specs=(VMEM, VMEM, VMEM),
        scratch_shapes=[pltpu.VMEM((rows, BLOCK), f32), pltpu.VMEM((imp_count, BLOCK), f32)],
        input_output_aliases={1: 0},
        compiler_params=PARAMS,
    )(place, gain, class_rows, pacing, first_price, *terms)

    terms = terms_of_sum(sums, "imp")
    per_step = 2
    density, pacing = pl.pallas_call(
        lambda *refs: final_kernel(ratio, advs, per_step, *refs),
        grid=(rows // per_step,),
        out_shape=(shape(adv_count, imp_count), shape(rows, BLOCK)),
        in_specs=[SMEM] + [VMEM] * (2 + len(terms)),
        out_specs=(pl.BlockSpec((per_step * BLOCK, imp_count), lambda i: (i, 0)), VMEM),
        scratch_shapes=[pltpu.VMEM((rows, BLOCK), f32)],
        compiler_params=PARAMS,
    )(place, gain, class_rows, *terms)
    return density, prices.reshape(imp_count), pacing.reshape(adv_count)


def solution(mesh):
    in_specs = (
        P(("adv", "imp"), None),
        P(("imp", "adv"), None),
        P("adv"),
        P("adv"),
        P("adv", "imp"),
    )
    out_specs = (P("adv", "imp"), P("imp"), P("adv"))
    return jax.shard_map(
        per_device, mesh=mesh, in_specs=in_specs, out_specs=out_specs, check_vma=False
    )
```

time: 132 us -> 58.8 us (0.45)
  blocking collectives: 100 us -> 0 us
  starting transfers between devices: 0 us -> 23.6 us
  waiting for transfers between devices: 0 us -> 19.2 us
  other arithmetic: 16.3 us -> 0.93 us
  Pallas kernels: 0 us -> 10.3 us
  matrix products: 8.14 us -> 0 us
  local copies, waits for them, and re-layouts: 5.69 us -> 3.65 us
    psum x4 -> x0, blocking collectives: 71.1 us -> none  [the longest x2 60.3 us: per_device(): spending = lax.psum(row_totals, 'imp')]
    all_gather x2 -> x0, blocking collectives: 29.1 us -> none  [the longest x1 23.9 us: per_device(): lax.all_gather(adv_embed, 'imp', axis=0, tiled=True)]
    ppermute x0 -> x19, starting transfers between devices: none -> 23.6 us  [swap(): lax.ppermute(x, axis, [(i, i ^ k) for i in range(lax.axis_size(axis))])]
    ppermute x0 -> x19, waiting for transfers between devices: none -> 19.2 us  [swap(): lax.ppermute(x, axis, [(i, i ^ k) for i in range(lax.axis_size(axis))])]
    pallas_call x0 -> x5, Pallas kernels: none -> 10.3 us  [the longest x1 4.87 us: per_device(): pl.pallas_call(lambda *refs: final_kernel(ratio, advs, per_step, *refs),...]
    dot_general x1 -> x0, matrix products: 8.14 us -> none  [score_block(): jnp.einsum('ae,ie->ai', embed_rows, imp_block, precision=lax.Precision.HI...]
    reduce_sum x3 -> x0, other arithmetic: 8.06 us -> none  [the longest x1 4.33 us: per_device(): row_totals = jnp.sum(gain, axis=1)]
    mul x2 -> x0, other arithmetic: 7.56 us -> none  [the longest x1 6.86 us: per_device(): return (bid_tile * total_advs, prices, pacing)]
  transfers between devices with their start and end apart: 0 -> 19, of which waited for: 0 -> 14; matrix products, arithmetic and copies ran while one was open for 0% -> 1% of each run, Pallas kernels for 0% -> 1%
where the time goes in v1:
time: 58.8 us; the launch traced here: 58.4 us
  starting transfers between devices  23.6 us (40%)
  waiting for transfers between devices  19.2 us (33%)
  Pallas kernels  10.3 us (18%)
  local copies, waits for them, and re-layouts  3.65 us (6%)
  other arithmetic  0.93 us (2%)
  between operations  0.72 us (1%)
    ppermute x19, starting transfers between devices, swap(): lax.ppermute(x, axis, [(i, i ^ k) for i in range(lax.axis_size(axis))])  23.6 us
    ppermute x19, waiting for transfers between devices, swap(): lax.ppermute(x, axis, [(i, i ^ k) for i in range(lax.axis_size(axis))])  19.2 us
    pallas_call x1, Pallas kernels, per_device(): pl.pallas_call(lambda *refs: final_kernel(ratio, advs, per_step, *refs),...  4.87 us
    unnamed x10, local copies, waits for them, and re-layouts  3.61 us
    pallas_call x1, Pallas kernels, per_device(): pl.pallas_call(lambda *refs: second_kernel(ratio, imps, *refs), out_shape...  2.39 us
    pallas_call x1, Pallas kernels, per_device(): pl.pallas_call(lambda *refs: first_kernel(len(adv_blocks), cols, *refs),...  1.4 us
  transfers between devices with their start and end apart: 19, of which 14 were waited for; matrix products, arithmetic and copies ran while one was open for 1% of the time, Pallas kernels for 1%

profile of v1, /device:TPU:0, one launch (start us, length us, event | category | flops | bytes accessed | tf_op | source)
XLA Modules:
  0.0 58.4 jit_solution(14237768655750457507)
XLA Ops:
  0.6 4.1 %collective-permute-start.1 = (f32[64,128]{1,0:T(8,128)}, f32[64,128]{1,0:T(8,128)S(1)}, u32[]{:S(2)}, u32[]{:S(2)}) collective-permute-start(f32[64,128]{1,0:T(8,128)} %bitcast.31), channel_id=1, source_target_pairs={{0,8},{1,9},{2,10},{3,11},{4,12},{5,13},{6,14},{7,15},{8,0},{9,1},... | collective-permute-start | bytes 98312 | tf_op jit(solution)/shard_map/ppermute | solution.py:174
  4.7 1.6 %collective-permute-start = (f32[64,128]{1,0:T(8,128)}, f32[64,128]{1,0:T(8,128)S(1)}, u32[]{:S(2)}, u32[]{:S(2)}) collective-permute-start(f32[64,128]{1,0:T(8,128)} %bitcast.32), channel_id=1, source_target_pairs={{0,4},{1,5},{2,6},{3,7},{4,0},{5,1},{6,2},{7,3},{8,12},{9,13},{10,... | collective-permute-start | bytes 98312 | tf_op jit(solution)/shard_map/ppermute | solution.py:174
  6.3 0.0 collective-permute-start.2
  6.3 0.0 copy-start
  6.3 0.7 %copy-done = s32[2048]{0:T(1024)S(1)} copy-done((s32[2048]{0:T(1024)S(1)}, s32[2048]{0:T(1024)}, u32[]{:S(2)}) %copy-start) | copy-done | bytes 8216
  7.0 0.0 copy-start.2
  7.0 0.8 %copy-done.2 = f32[256,64]{0,1:T(8,128)S(1)} copy-done((f32[256,64]{0,1:T(8,128)S(1)}, f32[256,64]{0,1:T(8,128)}, u32[]{:S(2)}) %copy-start.2) | copy-done | bytes 65560
  7.9 0.0 copy-start.3
  7.9 0.7 %copy-done.3 = f32[2048]{0:T(1024)S(1)} copy-done((f32[2048]{0:T(1024)S(1)}, f32[2048]{0:T(1024)}, u32[]{:S(2)}) %copy-start.3) | copy-done | bytes 8216
  8.5 0.0 copy-start.4
  8.6 0.7 %copy-done.4 = s32[16,4]{0,1:T(4,128)S(1)} copy-done((s32[16,4]{0,1:T(4,128)S(1)}, s32[16,4]{0,1:T(4,128)}, u32[]{:S(2)}) %copy-start.4) | copy-done | bytes 280
  9.2 0.7 %shard_map.76 = (f32[72,256]{1,0:T(8,128)S(1)}, f32[16,2048]{1,0:T(8,128)S(1)}) custom-call(s32[4,16]{1,0:T(4,128)S(1)} %bitcast.27, s32[16,128]{1,0:T(8,128)S(1)} %bitcast.21, f32[16,128]{1,0:T(8,128)S(1)} %bitcast.26, f32[64,256]{1,0:T(8,128)S(1)} %bitcast.25), custom_call_target="tpu_custom_call" | custom-call | tf_op jit(solution)/shard_map/pallas_call | solution.py:218
  9.9 1.8 %collective-permute-start.3 = (f32[72,256]{1,0:T(8,128)S(1)}, f32[72,256]{1,0:T(8,128)S(1)}, u32[]{:S(2)}, u32[]{:S(2)}) collective-permute-start(f32[72,256]{1,0:T(8,128)S(1)} %get-tuple-element.17.refs_2_), channel_id=1, source_target_pairs={{0,16},{16,0},{1,17},{17,1},{2,18},{18,2},{3,19},{19,3},{4,20},{20... | collective-permute-start | bytes 221192 | tf_op jit(solution)/shard_map/ppermute | solution.py:174
  11.7 0.0 collective-permute-done.1
  11.7 0.0 collective-permute-done
  11.7 0.5 collective-permute-done.2
  12.2 0.8 %pad_maximum_fusion.2 = f32[4,64,128]{2,1,0:T(8,128)S(1)} fusion(f32[1,64,128]{2,1,0:T(8,128)S(1)} %bitcast.37, f32[1,64,128]{2,1,0:T(8,128)S(1)} %bitcast.35, f32[1,64,128]{2,1,0:T(8,128)S(1)} %bitcast.36, f32[1,64,128]{2,1,0:T(8,128)} %bitcast.34), kind=kLoop, calls=%fused_computation.2 | loop fusion | flops 98304 | bytes 262144 | tf_op jit(solution)/shard_map/stack | solution.py:227
  13.0 1.3 %collective-permute-done.3.refs_3_ = f32[72,256]{1,0:T(8,128)S(1)} collective-permute-done((f32[72,256]{1,0:T(8,128)S(1)}, f32[72,256]{1,0:T(8,128)S(1)}, u32[]{:S(2)}, u32[]{:S(2)}) %collective-permute-start.3) | collective-permute-done | bytes 73760 | tf_op jit(solution)/shard_map/ppermute | solution.py:174
  14.3 1.7 %collective-permute-start.4 = (f32[4,64,128]{2,1,0:T(8,128)S(1)}, f32[4,64,128]{2,1,0:T(8,128)S(1)}, u32[]{:S(2)}, u32[]{:S(2)}) collective-permute-start(f32[4,64,128]{2,1,0:T(8,128)S(1)} %pad_maximum_fusion.2), channel_id=1, source_target_pairs={{0,2},{1,3},{2,0},{3,1},{4,6},{5,7},{6,4},{7,5},{8,10},{9,11},{10,... | collective-permute-start | bytes 393224 | tf_op jit(solution)/shard_map/ppermute | solution.py:174
  16.1 3.3 %collective-permute-done.4 = f32[4,64,128]{2,1,0:T(8,128)S(1)} collective-permute-done((f32[4,64,128]{2,1,0:T(8,128)S(1)}, f32[4,64,128]{2,1,0:T(8,128)S(1)}, u32[]{:S(2)}, u32[]{:S(2)}) %collective-permute-start.4) | collective-permute-done | bytes 131104 | tf_op jit(solution)/shard_map/ppermute | solution.py:174
  19.4 0.1 collective-permute-start.5
  19.4 0.1 pad_add_fusion.refs_0_
  19.5 1.4 %collective-permute-done.5 = f32[4,2,64,128]{3,2,0,1:T(8,128)S(1)} collective-permute-done((f32[4,2,64,128]{3,2,0,1:T(8,128)S(1)}, f32[4,2,64,128]{3,2,0,1:T(8,128)S(1)}, u32[]{:S(2)}, u32[]{:S(2)}) %collective-permute-start.5) | collective-permute-done | bytes 262176 | tf_op jit(solution)/shard_map/ppermute | solution.py:174
  21.1 1.4 %shard_map.77 = (f32[512,2048]{1,0:T(8,128)S(1)}, f32[16,128]{1,0:T(8,128)S(1)}, f32[4,128]{1,0:T(4,128)S(1)}) custom-call(s32[2]{0:T(128)S(1)} %pad_add_fusion.refs_0_, f32[16,64,128]{2,1,0:T(8,128)S(1)} %bitcast.20, f32[72,256]{1,0:T(8,128)S(1)} %get-tuple-element.17.refs_2_, f32[72,256]{1,0:T(8,128)S(1)} %collective-permute-done.3.refs_3_, ...), custom_call_target="tpu_custom_call" | custom-call | tf_op jit(solution)/shard_map/pallas_call | solution.py:243
  22.5 1.5 %collective-permute-start.8 = (f32[16,128]{1,0:T(8,128)S(1)}, f32[16,128]{1,0:T(8,128)S(1)}, u32[]{:S(2)}, u32[]{:S(2)}) collective-permute-start(f32[16,128]{1,0:T(8,128)S(1)} %get-tuple-element.22), channel_id=1, source_target_pairs={{0,3},{1,2},{2,1},{3,0},{4,7},{5,6},{6,5},{7,4},{8,11},{9,10},{10,... | collective-permute-start | bytes 24584 | tf_op jit(solution)/shard_map/ppermute | solution.py:174
  24.0 0.3 collective-permute-start.7
  24.3 0.1 collective-permute-start.6
  24.4 1.2 %collective-permute-done.8 = f32[16,128]{1,0:T(8,128)S(1)} collective-permute-done((f32[16,128]{1,0:T(8,128)S(1)}, f32[16,128]{1,0:T(8,128)S(1)}, u32[]{:S(2)}, u32[]{:S(2)}) %collective-permute-start.8) | collective-permute-done | bytes 8224 | tf_op jit(solution)/shard_map/ppermute | solution.py:174
  25.6 2.0 %collective-permute-done.7 = f32[16,128]{1,0:T(8,128)S(1)} collective-permute-done((f32[16,128]{1,0:T(8,128)S(1)}, f32[16,128]{1,0:T(8,128)S(1)}, u32[]{:S(2)}, u32[]{:S(2)}) %collective-permute-start.7) | collective-permute-done | bytes 8224 | tf_op jit(solution)/shard_map/ppermute | solution.py:174
  27.6 0.0 collective-permute-done.6
  27.6 3.7 %collective-permute-start.11 = (f32[16,128]{1,0:T(8,128)S(1)}, f32[16,128]{1,0:T(8,128)S(1)}, u32[]{:S(2)}, u32[]{:S(2)}) collective-permute-start(f32[16,128]{1,0:T(8,128)S(1)} %add_add_fusion.1.refs_3_), channel_id=1, source_target_pairs={{0,12},{1,13},{2,14},{3,15},{4,8},{5,9},{6,10},{7,11},{8,4},{9,5},... | collective-permute-start | bytes 24584 | tf_op jit(solution)/shard_map/ppermute | solution.py:174
  31.3 0.0 collective-permute-start.10
  31.3 0.8 %collective-permute-start.9 = (f32[16,128]{1,0:T(8,128)S(1)}, f32[16,128]{1,0:T(8,128)S(1)}, u32[]{:S(2)}, u32[]{:S(2)}) collective-permute-start(f32[16,128]{1,0:T(8,128)S(1)} %add_add_fusion.1.refs_3_), channel_id=1, source_target_pairs={{0,4},{1,5},{2,6},{3,7},{4,0},{5,1},{6,2},{7,3},{8,12},{9,13},{10,... | collective-permute-start | bytes 24584 | tf_op jit(solution)/shard_map/ppermute | solution.py:174
  32.1 1.1 %collective-permute-done.11.refs_6_ = f32[16,128]{1,0:T(8,128)S(1)} collective-permute-done((f32[16,128]{1,0:T(8,128)S(1)}, f32[16,128]{1,0:T(8,128)S(1)}, u32[]{:S(2)}, u32[]{:S(2)}) %collective-permute-start.11) | collective-permute-done | bytes 8224 | tf_op jit(solution)/shard_map/ppermute | solution.py:174
  33.2 2.7 %collective-permute-done.10.refs_5_ = f32[16,128]{1,0:T(8,128)S(1)} collective-permute-done((f32[16,128]{1,0:T(8,128)S(1)}, f32[16,128]{1,0:T(8,128)S(1)}, u32[]{:S(2)}, u32[]{:S(2)}) %collective-permute-start.10) | collective-permute-done | bytes 8224 | tf_op jit(solution)/shard_map/ppermute | solution.py:174
  35.9 0.0 collective-permute-done.9.refs_4_
  35.9 0.0 copy-start.1
  35.9 0.7 %copy-done.1 = s32[2048]{0:T(1024)S(1)} copy-done((s32[2048]{0:T(1024)S(1)}, s32[2048]{0:T(1024)}, u32[]{:S(2)}) %copy-start.1) | copy-done | bytes 8216
  36.6 0.9 %shard_map.78 = (f32[4,128]{1,0:T(4,128)S(1)}, f32[16,128]{1,0:T(8,128)S(1)}) custom-call(s32[2]{0:T(128)S(1)} %pad_add_fusion.refs_0_, f32[512,2048]{1,0:T(8,128)S(1)} %get-tuple-element.21.refs_1_, s32[16,128]{1,0:T(8,128)S(1)} %bitcast.22, f32[16,128]{1,0:T(8,128)S(1)} %add_add_fusion.1.refs_3_, f32[16,128]{1,0:T(8,128)S(1)} %collective-permute-done.9.refs_4_, ...), custom_call_target="tpu_custom_call" | custom-call | tf_op jit(solution)/shard_map/pallas_call | solution.py:257
  37.5 1.6 %collective-permute-start.12 = (f32[4,128]{1,0:T(4,128)S(1)}, f32[4,128]{1,0:T(4,128)S(1)}, u32[]{:S(2)}, u32[]{:S(2)}) collective-permute-start(f32[4,128]{1,0:T(4,128)S(1)} %get-tuple-element.25.refs_5_), channel_id=1, source_target_pairs={{0,16},{16,0},{1,17},{17,1},{2,18},{18,2},{3,19},{19,3},{4,20},{20... | collective-permute-start | bytes 6152 | tf_op jit(solution)/shard_map/ppermute | solution.py:174
  39.1 2.1 %collective-permute-done.12.refs_6_ = f32[4,128]{1,0:T(4,128)S(1)} collective-permute-done((f32[4,128]{1,0:T(4,128)S(1)}, f32[4,128]{1,0:T(4,128)S(1)}, u32[]{:S(2)}, u32[]{:S(2)}) %collective-permute-start.12) | collective-permute-done | bytes 2080 | tf_op jit(solution)/shard_map/ppermute | solution.py:174
  41.1 2.4 %shard_map.79 = (f32[512,2048]{1,0:T(8,128)S(1)}, f32[16,128]{1,0:T(8,128)S(1)}, f32[4,128]{1,0:T(4,128)}) custom-call(s32[2]{0:T(128)S(1)} %pad_add_fusion.refs_0_, f32[512,2048]{1,0:T(8,128)S(1)} %get-tuple-element.21.refs_1_, s32[16,128]{1,0:T(8,128)S(1)} %bitcast.23, f32[16,128]{1,0:T(8,128)S(1)} %get-tuple-element.23.refs_3_, ...), custom_call_target="tpu_custom_call", output_to_operand_aliasing={{0}: (1, {})} | custom-call | tf_op jit(solution)/shard_map/pallas_call | solution.py:266
  43.5 0.1 collective-permute-start.15
  43.6 0.6 %collective-permute-start.14 = (f32[16,128]{1,0:T(8,128)S(1)}, f32[16,128]{1,0:T(8,128)S(1)}, u32[]{:S(2)}, u32[]{:S(2)}) collective-permute-start(f32[16,128]{1,0:T(8,128)S(1)} %get-tuple-element.27), channel_id=1, source_target_pairs={{0,2},{1,3},{2,0},{3,1},{4,6},{5,7},{6,4},{7,5},{8,10},{9,11},{10,... | collective-permute-start | bytes 24584 | tf_op jit(solution)/shard_map/ppermute | solution.py:174
  44.2 1.2 %collective-permute-start.13 = (f32[16,128]{1,0:T(8,128)S(1)}, f32[16,128]{1,0:T(8,128)S(1)}, u32[]{:S(2)}, u32[]{:S(2)}) collective-permute-start(f32[16,128]{1,0:T(8,128)S(1)} %get-tuple-element.27), channel_id=1, source_target_pairs={{0,1},{1,0},{2,3},{3,2},{4,5},{5,4},{6,7},{7,6},{8,9},{9,8},{10,11... | collective-permute-start | bytes 24584 | tf_op jit(solution)/shard_map/ppermute | solution.py:174
  45.5 1.2 %collective-permute-done.15 = f32[16,128]{1,0:T(8,128)S(1)} collective-permute-done((f32[16,128]{1,0:T(8,128)S(1)}, f32[16,128]{1,0:T(8,128)S(1)}, u32[]{:S(2)}, u32[]{:S(2)}) %collective-permute-start.15) | collective-permute-done | bytes 8224 | tf_op jit(solution)/shard_map/ppermute | solution.py:174
  46.7 0.7 %collective-permute-done.14 = f32[16,128]{1,0:T(8,128)S(1)} collective-permute-done((f32[16,128]{1,0:T(8,128)S(1)}, f32[16,128]{1,0:T(8,128)S(1)}, u32[]{:S(2)}, u32[]{:S(2)}) %collective-permute-start.14) | collective-permute-done | bytes 8224 | tf_op jit(solution)/shard_map/ppermute | solution.py:174
  47.3 0.0 collective-permute-done.13
  47.3 1.5 %collective-permute-start.18 = (f32[16,128]{1,0:T(8,128)S(1)}, f32[16,128]{1,0:T(8,128)S(1)}, u32[]{:S(2)}, u32[]{:S(2)}) collective-permute-start(f32[16,128]{1,0:T(8,128)S(1)} %add_add_fusion.refs_3_), channel_id=1, source_target_pairs={{0,12},{1,13},{2,14},{3,15},{4,8},{5,9},{6,10},{7,11},{8,4},{9,5},... | collective-permute-start | bytes 24584 | tf_op jit(solution)/shard_map/ppermute | solution.py:174
  48.9 0.6 %collective-permute-start.17 = (f32[16,128]{1,0:T(8,128)S(1)}, f32[16,128]{1,0:T(8,128)S(1)}, u32[]{:S(2)}, u32[]{:S(2)}) collective-permute-start(f32[16,128]{1,0:T(8,128)S(1)} %add_add_fusion.refs_3_), channel_id=1, source_target_pairs={{0,8},{1,9},{2,10},{3,11},{4,12},{5,13},{6,14},{7,15},{8,0},{9,1},... | collective-permute-start | bytes 24584 | tf_op jit(solution)/shard_map/ppermute | solution.py:174
  49.5 2.3 %collective-permute-start.16 = (f32[16,128]{1,0:T(8,128)S(1)}, f32[16,128]{1,0:T(8,128)S(1)}, u32[]{:S(2)}, u32[]{:S(2)}) collective-permute-start(f32[16,128]{1,0:T(8,128)S(1)} %add_add_fusion.refs_3_), channel_id=1, source_target_pairs={{0,4},{1,5},{2,6},{3,7},{4,0},{5,1},{6,2},{7,3},{8,12},{9,13},{10,... | collective-permute-start | bytes 24584 | tf_op jit(solution)/shard_map/ppermute | solution.py:174
  51.8 1.1 %collective-permute-done.18.refs_6_ = f32[16,128]{1,0:T(8,128)S(1)} collective-permute-done((f32[16,128]{1,0:T(8,128)S(1)}, f32[16,128]{1,0:T(8,128)S(1)}, u32[]{:S(2)}, u32[]{:S(2)}) %collective-permute-start.18) | collective-permute-done | bytes 8224 | tf_op jit(solution)/shard_map/ppermute | solution.py:174
  52.9 0.5 collective-permute-done.17.refs_5_
  53.4 0.1 collective-permute-done.16.refs_4_
  53.5 4.9 %shard_map.80 = (f32[2048,512]{1,0:T(8,128)}, f32[16,128]{1,0:T(8,128)}) custom-call(s32[2]{0:T(128)S(1)} %pad_add_fusion.refs_0_, f32[512,2048]{1,0:T(8,128)S(1)} %get-tuple-element.26.refs_1_, s32[16,128]{1,0:T(8,128)S(1)} %bitcast.24, f32[16,128]{1,0:T(8,128)S(1)} %add_add_fusion.refs_3_, f32[16,128]{1,0:T(8,128)S(1)} %collective-permute-done.16.refs_4_, ...), custom_call_target="tpu_custom_call" | custom-call | tf_op jit(solution)/shard_map/pallas_call | solution.py:278
  (5 shorter events, 0.1 us)
Async XLA Ops:
  0.6 11.1 %collective-permute-start.1 = (f32[64,128]{1,0:T(8,128)}, f32[64,128]{1,0:T(8,128)S(1)}, u32[]{:S(2)}, u32[]{:S(2)}) collective-permute-start(f32[64,128]{1,0:T(8,128)} %bitcast.31), channel_id=1, source_target_pairs={{0,8},{1,9},{2,10},{3,11},{4,12},{5,13},{6,14},{7,15},{8,0},{9,1},... | collective-permute-start | bytes 98312 | tf_op jit(solution)/shard_map/ppermute | solution.py:174
  4.7 7.0 %collective-permute-start = (f32[64,128]{1,0:T(8,128)}, f32[64,128]{1,0:T(8,128)S(1)}, u32[]{:S(2)}, u32[]{:S(2)}) collective-permute-start(f32[64,128]{1,0:T(8,128)} %bitcast.32), channel_id=1, source_target_pairs={{0,4},{1,5},{2,6},{3,7},{4,0},{5,1},{6,2},{7,3},{8,12},{9,13},{10,... | collective-permute-start | bytes 98312 | tf_op jit(solution)/shard_map/ppermute | solution.py:174
  6.3 5.9 %collective-permute-start.2 = (f32[64,128]{1,0:T(8,128)}, f32[64,128]{1,0:T(8,128)S(1)}, u32[]{:S(2)}, u32[]{:S(2)}) collective-permute-start(f32[64,128]{1,0:T(8,128)} %bitcast.33), channel_id=1, source_target_pairs={{0,12},{1,13},{2,14},{3,15},{4,8},{5,9},{6,10},{7,11},{8,4},{9,5},... | collective-permute-start | bytes 98312 | tf_op jit(solution)/shard_map/ppermute | solution.py:174
  6.3 0.7 %copy-start = (s32[2048]{0:T(1024)S(1)}, s32[2048]{0:T(1024)}, u32[]{:S(2)}) copy-start(s32[2048]{0:T(1024)} %param.8) | copy-start | bytes 24580
  7.0 0.8 %copy-start.2 = (f32[256,64]{0,1:T(8,128)S(1)}, f32[256,64]{0,1:T(8,128)}, u32[]{:S(2)}) copy-start(f32[256,64]{0,1:T(8,128)} %param.6) | copy-start | bytes 196612
  7.9 0.7 %copy-start.3 = (f32[2048]{0:T(1024)S(1)}, f32[2048]{0:T(1024)}, u32[]{:S(2)}) copy-start(f32[2048]{0:T(1024)} %param.7) | copy-start | bytes 24580
  8.5 0.7 %copy-start.4 = (s32[16,4]{0,1:T(4,128)S(1)}, s32[16,4]{0,1:T(4,128)}, u32[]{:S(2)}) copy-start(s32[16,4]{0,1:T(4,128)} %param.9) | copy-start | bytes 772
  9.9 4.4 %collective-permute-start.3 = (f32[72,256]{1,0:T(8,128)S(1)}, f32[72,256]{1,0:T(8,128)S(1)}, u32[]{:S(2)}, u32[]{:S(2)}) collective-permute-start(f32[72,256]{1,0:T(8,128)S(1)} %get-tuple-element.17.refs_2_), channel_id=1, source_target_pairs={{0,16},{16,0},{1,17},{17,1},{2,18},{18,2},{3,19},{19,3},{4,20},{20... | collective-permute-start | bytes 221192 | tf_op jit(solution)/shard_map/ppermute | solution.py:174
  14.3 5.0 %collective-permute-start.4 = (f32[4,64,128]{2,1,0:T(8,128)S(1)}, f32[4,64,128]{2,1,0:T(8,128)S(1)}, u32[]{:S(2)}, u32[]{:S(2)}) collective-permute-start(f32[4,64,128]{2,1,0:T(8,128)S(1)} %pad_maximum_fusion.2), channel_id=1, source_target_pairs={{0,2},{1,3},{2,0},{3,1},{4,6},{5,7},{6,4},{7,5},{8,10},{9,11},{10,... | collective-permute-start | bytes 393224 | tf_op jit(solution)/shard_map/ppermute | solution.py:174
  19.4 1.6 %collective-permute-start.5 = (f32[4,2,64,128]{3,2,0,1:T(8,128)S(1)}, f32[4,2,64,128]{3,2,0,1:T(8,128)S(1)}, u32[]{:S(2)}, u32[]{:S(2)}) collective-permute-start(f32[4,2,64,128]{3,2,0,1:T(8,128)S(1)} %get-tuple-element.32), channel_id=1, source_target_pairs={{0,1},{1,0},{2,3},{3,2},{4,5},{5,4},{6,7},{7,6},{8,9},{9,8},{10,11... | collective-permute-start | bytes 786440 | tf_op jit(solution)/shard_map/ppermute | solution.py:174
  22.5 3.1 %collective-permute-start.8 = (f32[16,128]{1,0:T(8,128)S(1)}, f32[16,128]{1,0:T(8,128)S(1)}, u32[]{:S(2)}, u32[]{:S(2)}) collective-permute-start(f32[16,128]{1,0:T(8,128)S(1)} %get-tuple-element.22), channel_id=1, source_target_pairs={{0,3},{1,2},{2,1},{3,0},{4,7},{5,6},{6,5},{7,4},{8,11},{9,10},{10,... | collective-permute-start | bytes 24584 | tf_op jit(solution)/shard_map/ppermute | solution.py:174
  24.0 3.7 %collective-permute-start.7 = (f32[16,128]{1,0:T(8,128)S(1)}, f32[16,128]{1,0:T(8,128)S(1)}, u32[]{:S(2)}, u32[]{:S(2)}) collective-permute-start(f32[16,128]{1,0:T(8,128)S(1)} %get-tuple-element.22), channel_id=1, source_target_pairs={{0,2},{1,3},{2,0},{3,1},{4,6},{5,7},{6,4},{7,5},{8,10},{9,11},{10,... | collective-permute-start | bytes 24584 | tf_op jit(solution)/shard_map/ppermute | solution.py:174
  24.3 3.3 %collective-permute-start.6 = (f32[16,128]{1,0:T(8,128)S(1)}, f32[16,128]{1,0:T(8,128)S(1)}, u32[]{:S(2)}, u32[]{:S(2)}) collective-permute-start(f32[16,128]{1,0:T(8,128)S(1)} %get-tuple-element.22), channel_id=1, source_target_pairs={{0,1},{1,0},{2,3},{3,2},{4,5},{5,4},{6,7},{7,6},{8,9},{9,8},{10,11... | collective-permute-start | bytes 24584 | tf_op jit(solution)/shard_map/ppermute | solution.py:174
  27.6 5.5 %collective-permute-start.11 = (f32[16,128]{1,0:T(8,128)S(1)}, f32[16,128]{1,0:T(8,128)S(1)}, u32[]{:S(2)}, u32[]{:S(2)}) collective-permute-start(f32[16,128]{1,0:T(8,128)S(1)} %add_add_fusion.1.refs_3_), channel_id=1, source_target_pairs={{0,12},{1,13},{2,14},{3,15},{4,8},{5,9},{6,10},{7,11},{8,4},{9,5},... | collective-permute-start | bytes 24584 | tf_op jit(solution)/shard_map/ppermute | solution.py:174
  31.3 4.5 %collective-permute-start.10 = (f32[16,128]{1,0:T(8,128)S(1)}, f32[16,128]{1,0:T(8,128)S(1)}, u32[]{:S(2)}, u32[]{:S(2)}) collective-permute-start(f32[16,128]{1,0:T(8,128)S(1)} %add_add_fusion.1.refs_3_), channel_id=1, source_target_pairs={{0,8},{1,9},{2,10},{3,11},{4,12},{5,13},{6,14},{7,15},{8,0},{9,1},... | collective-permute-start | bytes 24584 | tf_op jit(solution)/shard_map/ppermute | solution.py:174
  31.3 4.5 %collective-permute-start.9 = (f32[16,128]{1,0:T(8,128)S(1)}, f32[16,128]{1,0:T(8,128)S(1)}, u32[]{:S(2)}, u32[]{:S(2)}) collective-permute-start(f32[16,128]{1,0:T(8,128)S(1)} %add_add_fusion.1.refs_3_), channel_id=1, source_target_pairs={{0,4},{1,5},{2,6},{3,7},{4,0},{5,1},{6,2},{7,3},{8,12},{9,13},{10,... | collective-permute-start | bytes 24584 | tf_op jit(solution)/shard_map/ppermute | solution.py:174
  35.9 0.7 %copy-start.1 = (s32[2048]{0:T(1024)S(1)}, s32[2048]{0:T(1024)}, u32[]{:S(2)}) copy-start(s32[2048]{0:T(1024)} %param.8) | copy-start | bytes 24580
  37.5 3.7 %collective-permute-start.12 = (f32[4,128]{1,0:T(4,128)S(1)}, f32[4,128]{1,0:T(4,128)S(1)}, u32[]{:S(2)}, u32[]{:S(2)}) collective-permute-start(f32[4,128]{1,0:T(4,128)S(1)} %get-tuple-element.25.refs_5_), channel_id=1, source_target_pairs={{0,16},{16,0},{1,17},{17,1},{2,18},{18,2},{3,19},{19,3},{4,20},{20... | collective-permute-start | bytes 6152 | tf_op jit(solution)/shard_map/ppermute | solution.py:174
  43.5 3.1 %collective-permute-start.15 = (f32[16,128]{1,0:T(8,128)S(1)}, f32[16,128]{1,0:T(8,128)S(1)}, u32[]{:S(2)}, u32[]{:S(2)}) collective-permute-start(f32[16,128]{1,0:T(8,128)S(1)} %get-tuple-element.27), channel_id=1, source_target_pairs={{0,3},{1,2},{2,1},{3,0},{4,7},{5,6},{6,5},{7,4},{8,11},{9,10},{10,... | collective-permute-start | bytes 24584 | tf_op jit(solution)/shard_map/ppermute | solution.py:174
  43.6 3.7 %collective-permute-start.14 = (f32[16,128]{1,0:T(8,128)S(1)}, f32[16,128]{1,0:T(8,128)S(1)}, u32[]{:S(2)}, u32[]{:S(2)}) collective-permute-start(f32[16,128]{1,0:T(8,128)S(1)} %get-tuple-element.27), channel_id=1, source_target_pairs={{0,2},{1,3},{2,0},{3,1},{4,6},{5,7},{6,4},{7,5},{8,10},{9,11},{10,... | collective-permute-start | bytes 24584 | tf_op jit(solution)/shard_map/ppermute | solution.py:174
  44.2 3.1 %collective-permute-start.13 = (f32[16,128]{1,0:T(8,128)S(1)}, f32[16,128]{1,0:T(8,128)S(1)}, u32[]{:S(2)}, u32[]{:S(2)}) collective-permute-start(f32[16,128]{1,0:T(8,128)S(1)} %get-tuple-element.27), channel_id=1, source_target_pairs={{0,1},{1,0},{2,3},{3,2},{4,5},{5,4},{6,7},{7,6},{8,9},{9,8},{10,11... | collective-permute-start | bytes 24584 | tf_op jit(solution)/shard_map/ppermute | solution.py:174
  47.3 5.6 %collective-permute-start.18 = (f32[16,128]{1,0:T(8,128)S(1)}, f32[16,128]{1,0:T(8,128)S(1)}, u32[]{:S(2)}, u32[]{:S(2)}) collective-permute-start(f32[16,128]{1,0:T(8,128)S(1)} %add_add_fusion.refs_3_), channel_id=1, source_target_pairs={{0,12},{1,13},{2,14},{3,15},{4,8},{5,9},{6,10},{7,11},{8,4},{9,5},... | collective-permute-start | bytes 24584 | tf_op jit(solution)/shard_map/ppermute | solution.py:174
  48.9 4.6 %collective-permute-start.17 = (f32[16,128]{1,0:T(8,128)S(1)}, f32[16,128]{1,0:T(8,128)S(1)}, u32[]{:S(2)}, u32[]{:S(2)}) collective-permute-start(f32[16,128]{1,0:T(8,128)S(1)} %add_add_fusion.refs_3_), channel_id=1, source_target_pairs={{0,8},{1,9},{2,10},{3,11},{4,12},{5,13},{6,14},{7,15},{8,0},{9,1},... | collective-permute-start | bytes 24584 | tf_op jit(solution)/shard_map/ppermute | solution.py:174
  49.5 4.0 %collective-permute-start.16 = (f32[16,128]{1,0:T(8,128)S(1)}, f32[16,128]{1,0:T(8,128)S(1)}, u32[]{:S(2)}, u32[]{:S(2)}) collective-permute-start(f32[16,128]{1,0:T(8,128)S(1)} %add_add_fusion.refs_3_), channel_id=1, source_target_pairs={{0,4},{1,5},{2,6},{3,7},{4,0},{5,1},{6,2},{7,3},{8,12},{9,13},{10,... | collective-permute-start | bytes 24584 | tf_op jit(solution)/shard_map/ppermute | solution.py:174

commit v2 on v1

v2 whole, which is shorter than its diff:
```python
import math

import jax
import jax.numpy as jnp
from jax import lax
from jax.experimental import pallas as pl
from jax.experimental.pallas import tpu as pltpu
from jax.sharding import PartitionSpec as P

BLOCK = 128
ITERS = 2
SCORE_GAIN = 0.0875
LOG2E = 1.4426950408889634
OFF = 1e30
DEPTH = 208

VMEM = pl.BlockSpec(memory_space=pltpu.VMEM)
HBM = pl.BlockSpec(memory_space=pltpu.HBM)
PARAMS = pltpu.CompilerParams(vmem_limit_bytes=48 * 1024 * 1024)


def pieces(x):
    first = x.astype(jnp.bfloat16).astype(jnp.float32)
    rest = x - first
    second = rest.astype(jnp.bfloat16).astype(jnp.float32)
    third = (rest - second).astype(jnp.bfloat16).astype(jnp.float32)
    return first, second, third


def place(axis, staged):
    return lax.axis_index(axis) if staged else jnp.int32(0)


def prepare_kernel(ratio, imps, elig_hbm, class_hbm, scale_hbm, imp_hbm, adv_hbm, pack_ref, extra_ref, limit_ref, own_ref, elig_ref, class_ref, scale_ref, sems):
    moves = ((elig_hbm, elig_ref), (class_hbm, class_ref), (scale_hbm, scale_ref), (imp_hbm, pack_ref.at[0:64]), (adv_hbm, own_ref))
    copies = [pltpu.make_async_copy(src, dst, sems.at[n]) for n, (src, dst) in enumerate(moves)]
    for copy in copies:
        copy.start()
    for copy in copies:
        copy.wait()
    spend_class = class_ref[...].astype(jnp.float32)
    limit_ref[...] = ratio * jnp.exp(0.3 * spend_class - 1.2)
    allowance = limit_ref[...] / imps
    log_scale = jnp.log(scale_ref[...]) * LOG2E + ((0.3 * spend_class - 1.2) * LOG2E + math.log2(ratio / imps))
    parts = pieces(log_scale)
    rows, cols = class_ref.shape[0], elig_ref.shape[0]
    width = pack_ref.shape[1]
    ones = jnp.ones((1, BLOCK), jnp.float32)
    sums = [jnp.zeros((1, BLOCK), jnp.float32) for _ in range(cols)]
    for b in range(rows):
        masks = []
        for c in range(cols):
            flag = elig_ref[c : c + 1, b : b + 1].astype(jnp.float32)
            sums[c] = sums[c] + flag * allowance[b : b + 1]
            masks.append(ones * ((flag - 1.0) * OFF))
        block = masks + [p[b : b + 1] for p in parts] + [ones] * 3
        block += [jnp.zeros((16 - len(block), BLOCK), jnp.float32)]
        extra_ref[:, b * BLOCK : (b + 1) * BLOCK] = jnp.concatenate(block, axis=0).astype(jnp.bfloat16)
    totals = jnp.concatenate(
        [jnp.broadcast_to(jnp.sum(s, axis=1, keepdims=True), (1, BLOCK)) for s in sums], axis=1
    )
    pack_ref[64:72, :] = jnp.zeros((8, width), jnp.float32)
    for r in range(cols * BLOCK // width):
        pack_ref[64 + r : 65 + r, :] = totals[:, r * width : (r + 1) * width]


def impressions_kernel(staged, cols, own_ref, other_ref, lhs_ref, lhs_t_ref, price_ref):
    half = place("adv", staged)
    width = own_ref.shape[1]
    count = cols * BLOCK
    for ref, at in ((own_ref, half * width), (other_ref, (1 - half) * width)):
        block = ref[0:64, :] * (SCORE_GAIN * LOG2E)
        high = block.astype(jnp.bfloat16)
        low = (block - high.astype(jnp.float32)).astype(jnp.bfloat16)
        at = pl.multiple_of(at, width)
        lhs_ref[0:64, pl.ds(at, width)] = high
        lhs_ref[64:128, pl.ds(at, width)] = low
        lhs_ref[128:192, pl.ds(at, width)] = high
    price_parts = own_ref[64:72, :] + other_ref[64:72, :]
    price = jnp.concatenate([price_parts[r : r + 1] for r in range(count // width)], axis=1)
    column = lax.broadcasted_iota(jnp.int32, (1, count), 1) // BLOCK
    rows = [(column == c).astype(jnp.float32) for c in range(cols)]
    rows += [jnp.ones((1, count), jnp.float32)] * 3
    rows += list(pieces(-jnp.log(price) * LOG2E))
    rows += [jnp.zeros((16 - len(rows), count), jnp.float32)]
    lhs_ref[192:208, :] = jnp.concatenate(rows, axis=0).astype(jnp.bfloat16)
    for c in range(cols):
        price_ref[c : c + 1, :] = price[:, c * BLOCK : (c + 1) * BLOCK]
    lhs_t_ref[...] = lhs_ref[...].T


def first_kernel(staged, keys, adv_ref, extra_ref, lhs_t_ref, *refs):
    gain_ref, sums_ref, rhs_ref = refs[-3:]
    order = place("imp", staged)
    lhs = lhs_t_ref[...]
    for n in range(0, len(keys), 2):
        two = keys[n : n + 2]
        for p, k in enumerate(two):
            lanes = slice(k * BLOCK, (k + 1) * BLOCK)
            block = adv_ref[n + p]
            high = block.astype(jnp.bfloat16)
            low = (block - high.astype(jnp.float32)).astype(jnp.bfloat16)
            rhs_ref[0:64, lanes] = high
            rhs_ref[64:128, lanes] = high
            rhs_ref[128:192, lanes] = low
            at = pl.multiple_of((order ^ k) * BLOCK, BLOCK)
            rhs_ref[192:208, lanes] = extra_ref[:, pl.ds(at, BLOCK)]
        rhs = jnp.concatenate([rhs_ref[:, k * BLOCK : (k + 1) * BLOCK] for k in two], axis=1)
        gain = jnp.exp2(jnp.dot(lhs, rhs, preferred_element_type=jnp.float32))
        sums = jnp.sum(gain, axis=0, keepdims=True)
        for p, k in enumerate(two):
            gain_ref[:, k * BLOCK : (k + 1) * BLOCK] = gain[:, p * BLOCK : (p + 1) * BLOCK]
            sums_ref[pl.ds(order ^ k, 1), :] = sums[:, p * BLOCK : (p + 1) * BLOCK]


def rows_kernel(lhs_ref, rhs_ref, gain_ref):
    lhs = lhs_ref[...]
    for k in range(rhs_ref.shape[1] // BLOCK):
        rows = slice(k * BLOCK, (k + 1) * BLOCK)
        gain_ref[rows, :] = jnp.exp2(jnp.dot(rhs_ref[:, rows].T, lhs, preferred_element_type=jnp.float32))


def prices_kernel(staged, gain_ref, limit_ref, *refs):
    *sum_refs, part_ref, pacing_ref = refs
    order = place("imp", staged)
    limit = limit_ref[...]
    pacing_ref[...] = limit / jnp.maximum(tree([r[...] for r in sum_refs]), limit)
    factors = [pacing_ref[pl.ds(order ^ k, 1), :] for k in range(limit.shape[0])]
    for c in range(gain_ref.shape[0] // BLOCK):
        total = jnp.zeros((BLOCK, BLOCK), jnp.float32)
        for k, factor in enumerate(factors):
            total = total + gain_ref[c * BLOCK : (c + 1) * BLOCK, k * BLOCK : (k + 1) * BLOCK] * factor
        part_ref[c : c + 1, :] = jnp.sum(total.T, axis=0, keepdims=True)


def second_kernel(staged, imps, gain_ref, limit_ref, pacing_ref, price_ref, *refs):
    *part_refs, sums_ref, prices_ref, factor_ref, change_ref = refs
    order = place("imp", staged)
    prices = tree([r[...] for r in part_refs])
    prices_ref[...] = prices
    changes = price_ref[...] / prices
    factor_ref[...] = pacing_ref[...] * (imps / limit_ref[...])
    blocks = limit_ref.shape[0]
    factors = [factor_ref[pl.ds(order ^ k, 1), :] for k in range(blocks)]
    totals = [jnp.zeros((8, BLOCK), jnp.float32) for _ in range(blocks)]
    for c in range(gain_ref.shape[0] // BLOCK):
        change_ref[:, c * BLOCK : (c + 1) * BLOCK] = changes[c : c + 1]
        change = jnp.broadcast_to(changes[c : c + 1], (BLOCK, BLOCK)).T
        for k in range(blocks):
            gain = gain_ref[c * BLOCK : (c + 1) * BLOCK, k * BLOCK : (k + 1) * BLOCK]
            new = (gain * factors[k]) * (gain * change)
            totals[k] = totals[k] + jnp.sum(new.reshape(BLOCK // 8, 8, BLOCK), axis=0)
    for k in range(blocks):
        sums_ref[pl.ds(order ^ k, 1), :] = jnp.sum(totals[k], axis=0, keepdims=True)


def final_kernel(staged, advs, gain_ref, limit_ref, factor_ref, change_ref, *refs):
    *sum_refs, out_ref, pacing_ref, scale_ref, block_ref, sems = refs
    order = place("imp", staged)
    limit = limit_ref[...]
    pacing = limit / jnp.maximum(tree([r[...] for r in sum_refs]), limit)
    pacing_ref[...] = pacing
    scale_ref[...] = pacing * factor_ref[...] * advs
    change = change_ref[...]
    shape = (BLOCK, BLOCK)
    diagonal = lax.broadcasted_iota(jnp.int32, shape, 0) == lax.broadcasted_iota(jnp.int32, shape, 1)
    copies = []
    for k in range(limit.shape[0]):
        b = order ^ k
        rows = slice(k * BLOCK, (k + 1) * BLOCK)
        scale = jnp.sum(jnp.where(diagonal, scale_ref[pl.ds(b, 1), :], 0.0), axis=1, keepdims=True)
        gain = gain_ref[rows, :]
        block_ref[rows, :] = (gain * scale) * (gain * change)
        to = pl.ds(pl.multiple_of(b * BLOCK, BLOCK), BLOCK)
        copy = pltpu.make_async_copy(block_ref.at[rows], out_ref.at[to], sems.at[k])
        copy.start()
        copies.append(copy)
    for copy in copies:
        copy.wait()


def tree(terms):
    while len(terms) > 1:
        terms = [a + b for a, b in zip(terms[::2], terms[1::2])]
    return terms[0]


def swap(x, axis, k):
    return lax.ppermute(x, axis, [(i, i ^ k) for i in range(lax.axis_size(axis))])


def with_partners(x, axis, keys):
    return [x] + [swap(x, axis, k) for k in keys]


def stages(n):
    found, bit = [], 1
    while bit < n:
        found.append((bit, 2 * bit, 3 * bit) if 4 * bit <= n else (bit,))
        bit *= 4
    return found


def terms_of_sum(x, axis):
    n = lax.axis_size(axis)
    if n & (n - 1):
        return [lax.psum(x, axis)]
    todo = stages(n)
    for keys in todo[:-1]:
        x = tree(with_partners(x, axis, keys))
    return with_partners(x, axis, todo[-1])


def per_device(adv_embed, imp_embed, value_scale, spend_class, eligible):
    n_adv, n_imp = lax.axis_size("adv"), lax.axis_size("imp")
    adv_count = spend_class.shape[0]
    rows, cols = eligible.shape
    imp_count = cols * BLOCK
    imps, advs = imp_count * n_imp, adv_count * n_adv
    ratio = imps / advs
    f32 = jnp.float32
    class_rows = spend_class.reshape(rows, BLOCK)
    scale_rows = value_scale.reshape(rows, BLOCK)

    def shape(*dims, dtype=f32):
        return jax.ShapeDtypeStruct(dims, dtype)

    def call(kernel, out, operands, cost=0, **kw):
        return pl.pallas_call(
            kernel,
            out_shape=out,
            in_specs=[VMEM] * len(operands),
            out_specs=tuple(VMEM for _ in out),
            compiler_params=PARAMS,
            cost_estimate=pl.CostEstimate(flops=cost, bytes_accessed=cost // 256, transcendentals=0),
            **kw,
        )(*operands)

    staged = n_imp == 16 and adv_embed.shape[0] == BLOCK and n_adv == 2
    imp_t, adv_t = imp_embed.T, adv_embed.T
    if not staged:
        imp_t = lax.all_gather(imp_embed, "adv", axis=0, tiled=True).T[:, : imp_count // 2]
    width = imp_t.shape[1]
    ins = [pltpu.with_memory_space_constraint(x, pltpu.HBM) for x in (eligible.T, class_rows, scale_rows, imp_t, adv_t)]
    pack, extra, limit, own = pl.pallas_call(
        lambda *refs: prepare_kernel(ratio, imps, *refs),
        out_shape=(shape(72, width), shape(16, adv_count, dtype=jnp.bfloat16), shape(rows, BLOCK), shape(*adv_t.shape)),
        in_specs=[HBM] * len(ins),
        out_specs=(VMEM,) * 4,
        scratch_shapes=[
            pltpu.VMEM((cols, rows), jnp.int32),
            pltpu.VMEM((rows, BLOCK), jnp.int32),
            pltpu.VMEM((rows, BLOCK), f32),
            pltpu.SemaphoreType.DMA((len(ins),)),
        ],
        compiler_params=PARAMS,
    )(*ins)
    if staged:
        line = jnp.stack([own] + [swap(adv_t, "imp", k) for k in (4, 8, 12)])
        other = swap(pack, "adv", 1)
        plane = swap(line, "imp", 2)
        plane, _ = lax.optimization_barrier((plane, other))
        pair = swap(jnp.concatenate([line, plane]), "imp", 1)
        groups = [((0, 4, 8, 12), line), ((2, 6, 10, 14), plane), ((1, 5, 9, 13, 3, 7, 11, 15), pair)]
    else:
        gathered = lax.all_gather(adv_embed, "imp", axis=0, tiled=True)
        groups = [(tuple(range(rows)), gathered.reshape(rows, BLOCK, 64).transpose(0, 2, 1))]
        whole = lax.all_gather(imp_embed, "adv", axis=0, tiled=True).T[:, imp_count // 2 :]
        price = lax.psum(pack[64:], "adv")
        other = jnp.concatenate([whole, jnp.zeros_like(price)])
        pack = jnp.concatenate([pack[:64], price])

    bf16 = jnp.bfloat16
    lhs, lhs_t, first_price = call(
        lambda *refs: impressions_kernel(staged, cols, *refs),
        (shape(DEPTH, imp_count, dtype=bf16), shape(imp_count, DEPTH, dtype=bf16), shape(cols, BLOCK)),
        (pack, other),
        cost=10**8,
    )
    held = ()
    for keys, blocks in groups:
        held = call(
            lambda *refs, keys=keys: first_kernel(staged, keys, *refs),
            (
                pltpu.VMEM((imp_count, adv_count), f32),
                shape(rows, BLOCK),
                pltpu.VMEM((DEPTH, adv_count), bf16),
            ),
            (blocks, extra, lhs_t, *held),
            cost=10**8 * len(keys),
            input_output_aliases={3 + i: i for i in range(len(held))},
        )
    gain, sums, rhs = held
    (gain_rows,) = call(rows_kernel, (pltpu.VMEM((adv_count, imp_count), f32),), (lhs, rhs), cost=10**9)

    part, pacing = call(
        lambda *refs: prices_kernel(staged, *refs), (shape(cols, BLOCK), shape(rows, BLOCK)), (gain, limit, *terms_of_sum(sums, "imp"))
    )
    sums, prices, factor, change = call(
        lambda *refs: second_kernel(staged, imps, *refs),
        (shape(rows, BLOCK), shape(cols, BLOCK), shape(rows, BLOCK), shape(1, imp_count)),
        (gain, limit, pacing, first_price, *terms_of_sum(part, "adv")),
    )

    terms = terms_of_sum(sums, "imp")
    density, pacing = pl.pallas_call(
        lambda *refs: final_kernel(staged, advs, *refs),
        out_shape=(shape(adv_count, imp_count), shape(rows, BLOCK)),
        in_specs=[VMEM] * (4 + len(terms)),
        out_specs=(HBM, VMEM),
        scratch_shapes=[
            pltpu.VMEM((rows, BLOCK), f32),
            pltpu.VMEM((adv_count, imp_count), f32),
            pltpu.SemaphoreType.DMA((rows,)),
        ],
        compiler_params=PARAMS,
    )(gain_rows, limit, factor, change, *terms)
    return density, prices.reshape(imp_count), pacing.reshape(adv_count)


def solution(mesh):
    in_specs = (
        P(("adv", "imp"), None),
        P(("imp", "adv"), None),
        P("adv"),
        P("adv"),
        P("adv", "imp"),
    )
    out_specs = (P("adv", "imp"), P("imp"), P("adv"))
    return jax.shard_map(
        per_device, mesh=mesh, in_specs=in_specs, out_specs=out_specs, check_vma=False
    )
```

time: 58.8 us -> 49.5 us (0.84)
  local copies, waits for them, and re-layouts: 3.65 us -> 0.03 us
  Pallas kernels: 10.3 us -> 7.31 us
  starting transfers between devices: 23.6 us -> 22.4 us
  other arithmetic: 0.93 us -> 0.02 us
    unnamed x10 -> x4, local copies, waits for them, and re-layouts: 3.61 us -> 0.02 us
    pallas_call x4 -> x8, Pallas kernels: 9.57 us -> 6.1 us  [the longest x7 3.23 us: call(): pl.pallas_call(kernel, out_shape=out, in_specs=[VMEM] * len(operands), ou...]
    ppermute x19, starting transfers between devices: 23.6 us -> 22.4 us  [swap(): lax.ppermute(x, axis, [(i, i ^ k) for i in range(lax.axis_size(axis))])]
    another operation x4 -> x1, other arithmetic: 0.92 us -> 0.01 us  [per_device(): line = jnp.stack([own] + [swap(adv_t, 'imp', k) for k in (4, 8, 12)])]
  transfers between devices with their start and end apart: 19 -> 19, of which waited for: 14 -> 12; matrix products, arithmetic and copies ran while one was open for 1% -> 0% of each run, Pallas kernels for 1% -> 6%
where the time goes in v2:
time: 49.5 us; the launch traced here: 49.3 us
  starting transfers between devices  22.4 us (45%)
  waiting for transfers between devices  18.8 us (38%)
  Pallas kernels  7.31 us (15%)
  between operations  0.76 us (2%)
    ppermute x19, starting transfers between devices, swap(): lax.ppermute(x, axis, [(i, i ^ k) for i in range(lax.axis_size(axis))])  22.4 us
    ppermute x19, waiting for transfers between devices, swap(): lax.ppermute(x, axis, [(i, i ^ k) for i in range(lax.axis_size(axis))])  18.8 us
    pallas_call x7, Pallas kernels, call(): pl.pallas_call(kernel, out_shape=out, in_specs=[VMEM] * len(operands), ou...  3.23 us
    pallas_call x1, Pallas kernels, per_device(): pl.pallas_call(lambda *refs: final_kernel(staged, advs, *refs), out_shape...  2.87 us
    pallas_call x1, Pallas kernels, per_device(): pl.pallas_call(lambda *refs: prepare_kernel(ratio, imps, *refs), out_shap...  1.21 us
  transfers between devices with their start and end apart: 19, of which 12 were waited for; matrix products, arithmetic and copies ran while one was open for 0% of the time, Pallas kernels for 6%

profile of v2, /device:TPU:0, one launch (start us, length us, event | category | flops | bytes accessed | tf_op | source)
XLA Modules:
  0.0 49.3 jit_solution(1310889430449145381)
XLA Ops:
  0.6 3.1 %collective-permute-start.1 = (f32[64,128]{1,0:T(8,128)}, f32[64,128]{1,0:T(8,128)S(1)}, u32[]{:S(2)}, u32[]{:S(2)}) collective-permute-start(f32[64,128]{1,0:T(8,128)} %bitcast.20), channel_id=1, source_target_pairs={{0,4},{1,5},{2,6},{3,7},{4,0},{5,1},{6,2},{7,3},{8,12},{9,13},{10,... | collective-permute-start | bytes 98312 | tf_op jit(solution)/shard_map/ppermute | solution.py:189
  3.7 2.6 %collective-permute-start.2 = (f32[64,128]{1,0:T(8,128)}, f32[64,128]{1,0:T(8,128)S(1)}, u32[]{:S(2)}, u32[]{:S(2)}) collective-permute-start(f32[64,128]{1,0:T(8,128)} %bitcast.21), channel_id=1, source_target_pairs={{0,8},{1,9},{2,10},{3,11},{4,12},{5,13},{6,14},{7,15},{8,0},{9,1},... | collective-permute-start | bytes 98312 | tf_op jit(solution)/shard_map/ppermute | solution.py:189
  6.3 0.0 collective-permute-start.3
  6.3 1.2 %shard_map.76 = (f32[72,256]{1,0:T(8,128)S(1)}, bf16[16,2048]{1,0:T(8,128)(2,1)S(1)}, f32[16,128]{1,0:T(8,128)S(1)}, f32[64,128]{1,0:T(8,128)S(1)}) custom-call(s32[4,16]{1,0:T(4,128)} %bitcast.26, s32[16,128]{1,0:T(8,128)} %bitcast.24, f32[16,128]{1,0:T(8,128)} %bitcast.25, f32[64,256]{1,0:T(8,128)} %bitcast.19, f32[64,128]{1,0:T(8,128)} %bitcast.23), custom_call_target="tpu_custom_call" | custom-call | tf_op jit(solution)/shard_map/pallas_call | solution.py:245
  7.5 1.8 %collective-permute-start = (f32[72,256]{1,0:T(8,128)S(1)}, f32[72,256]{1,0:T(8,128)S(1)}, u32[]{:S(2)}, u32[]{:S(2)}) collective-permute-start(f32[72,256]{1,0:T(8,128)S(1)} %get-tuple-element.28.refs_0_), channel_id=1, source_target_pairs={{0,16},{16,0},{1,17},{17,1},{2,18},{18,2},{3,19},{19,3},{4,20},{20... | collective-permute-start | bytes 221192 | tf_op jit(solution)/shard_map/ppermute | solution.py:189
  9.3 0.0 collective-permute-done.1
  9.3 0.0 collective-permute-done.2
  9.3 2.9 %collective-permute-done.3 = f32[64,128]{1,0:T(8,128)S(1)} collective-permute-done((f32[64,128]{1,0:T(8,128)}, f32[64,128]{1,0:T(8,128)S(1)}, u32[]{:S(2)}, u32[]{:S(2)}) %collective-permute-start.3) | collective-permute-done | bytes 32800 | tf_op jit(solution)/shard_map/ppermute | solution.py:189
  12.2 1.6 %collective-permute-start.4 = (f32[4,64,128]{2,1,0:T(8,128)S(1)}, f32[4,64,128]{2,1,0:T(8,128)S(1)}, u32[]{:S(2)}, u32[]{:S(2)}) collective-permute-start(f32[4,64,128]{2,1,0:T(8,128)S(1)} %pad_maximum_fusion.refs_0_), channel_id=1, source_target_pairs={{0,2},{1,3},{2,0},{3,1},{4,6},{5,7},{6,4},{7,5},{8,10},{9,11},{10,... | collective-permute-start | bytes 393224 | tf_op jit(solution)/shard_map/ppermute | solution.py:189
  13.8 0.0 collective-permute-done.refs_1_
  13.8 3.4 %collective-permute-done.4.refs_0_ = f32[4,64,128]{2,1,0:T(8,128)S(1)} collective-permute-done((f32[4,64,128]{2,1,0:T(8,128)S(1)}, f32[4,64,128]{2,1,0:T(8,128)S(1)}, u32[]{:S(2)}, u32[]{:S(2)}) %collective-permute-start.4) | collective-permute-done | bytes 131104 | tf_op jit(solution)/shard_map/ppermute | solution.py:189
  17.3 0.1 collective-permute-start.5
  17.4 0.2 shard_map.77
  17.5 0.3 shard_map.78
  17.9 0.3 shard_map.79
  18.2 0.7 %collective-permute-done.5.refs_0_ = f32[8,64,128]{2,1,0:T(8,128)S(1)} collective-permute-done((f32[8,64,128]{2,1,0:T(8,128)S(1)}, f32[8,64,128]{2,1,0:T(8,128)S(1)}, u32[]{:S(2)}, u32[]{:S(2)}) %collective-permute-start.5) | collective-permute-done | bytes 262176 | tf_op jit(solution)/shard_map/ppermute | solution.py:189
  18.9 0.5 %shard_map.80 = (f32[512,2048]{1,0:T(8,128)S(1)}, f32[16,128]{1,0:T(8,128)S(1)}, bf16[208,2048]{1,0:T(8,128)(2,1)S(1)}) custom-call(f32[8,64,128]{2,1,0:T(8,128)S(1)} %collective-permute-done.5.refs_0_, bf16[16,2048]{1,0:T(8,128)(2,1)S(1)} %get-tuple-element.32.refs_1_, ...), custom_call_target="tpu_custom_call", output_to_operand_aliasing={{0}: (3, {}), {1}: (4, {}), {2}: (5, {})} | custom-call | flops 800000000 | bytes 3125000 | tf_op jit(solution)/shard_map/pallas_call | solution.py:229
  19.4 0.2 collective-permute-start.6
  19.6 1.5 %collective-permute-start.7 = (f32[16,128]{1,0:T(8,128)S(1)}, f32[16,128]{1,0:T(8,128)S(1)}, u32[]{:S(2)}, u32[]{:S(2)}) collective-permute-start(f32[16,128]{1,0:T(8,128)S(1)} %get-tuple-element.43), channel_id=1, source_target_pairs={{0,2},{1,3},{2,0},{3,1},{4,6},{5,7},{6,4},{7,5},{8,10},{9,11},{10,... | collective-permute-start | bytes 24584 | tf_op jit(solution)/shard_map/ppermute | solution.py:189
  21.1 0.2 collective-permute-start.8
  21.3 0.0 collective-permute-done.6
  21.3 1.9 %collective-permute-done.7 = f32[16,128]{1,0:T(8,128)S(1)} collective-permute-done((f32[16,128]{1,0:T(8,128)S(1)}, f32[16,128]{1,0:T(8,128)S(1)}, u32[]{:S(2)}, u32[]{:S(2)}) %collective-permute-start.7) | collective-permute-done | bytes 8224 | tf_op jit(solution)/shard_map/ppermute | solution.py:189
  23.3 0.9 %collective-permute-done.8 = f32[16,128]{1,0:T(8,128)S(1)} collective-permute-done((f32[16,128]{1,0:T(8,128)S(1)}, f32[16,128]{1,0:T(8,128)S(1)}, u32[]{:S(2)}, u32[]{:S(2)}) %collective-permute-start.8) | collective-permute-done | bytes 8224 | tf_op jit(solution)/shard_map/ppermute | solution.py:189
  24.2 0.0 collective-permute-start.10
  24.2 1.4 %collective-permute-start.11 = (f32[16,128]{1,0:T(8,128)S(1)}, f32[16,128]{1,0:T(8,128)S(1)}, u32[]{:S(2)}, u32[]{:S(2)}) collective-permute-start(f32[16,128]{1,0:T(8,128)S(1)} %add_add_fusion.1.refs_2_), channel_id=1, source_target_pairs={{0,12},{1,13},{2,14},{3,15},{4,8},{5,9},{6,10},{7,11},{8,4},{9,5},... | collective-permute-start | bytes 24584 | tf_op jit(solution)/shard_map/ppermute | solution.py:189
  25.6 2.1 %collective-permute-start.9 = (f32[16,128]{1,0:T(8,128)S(1)}, f32[16,128]{1,0:T(8,128)S(1)}, u32[]{:S(2)}, u32[]{:S(2)}) collective-permute-start(f32[16,128]{1,0:T(8,128)S(1)} %add_add_fusion.1.refs_2_), channel_id=1, source_target_pairs={{0,4},{1,5},{2,6},{3,7},{4,0},{5,1},{6,2},{7,3},{8,12},{9,13},{10,... | collective-permute-start | bytes 24584 | tf_op jit(solution)/shard_map/ppermute | solution.py:189
  27.7 1.1 %collective-permute-done.10.refs_4_ = f32[16,128]{1,0:T(8,128)S(1)} collective-permute-done((f32[16,128]{1,0:T(8,128)S(1)}, f32[16,128]{1,0:T(8,128)S(1)}, u32[]{:S(2)}, u32[]{:S(2)}) %collective-permute-start.10) | collective-permute-done | bytes 8224 | tf_op jit(solution)/shard_map/ppermute | solution.py:189
  28.8 1.0 %collective-permute-done.11.refs_5_ = f32[16,128]{1,0:T(8,128)S(1)} collective-permute-done((f32[16,128]{1,0:T(8,128)S(1)}, f32[16,128]{1,0:T(8,128)S(1)}, u32[]{:S(2)}, u32[]{:S(2)}) %collective-permute-start.11) | collective-permute-done | bytes 8224 | tf_op jit(solution)/shard_map/ppermute | solution.py:189
  29.7 0.0 collective-permute-done.9.refs_3_
  29.7 0.4 shard_map.82
  30.1 1.6 %collective-permute-start.12 = (f32[4,128]{1,0:T(4,128)S(1)}, f32[4,128]{1,0:T(4,128)S(1)}, u32[]{:S(2)}, u32[]{:S(2)}) collective-permute-start(f32[4,128]{1,0:T(4,128)S(1)} %get-tuple-element.46.refs_4_), channel_id=1, source_target_pairs={{0,16},{16,0},{1,17},{17,1},{2,18},{18,2},{3,19},{19,3},{4,20},{20... | collective-permute-start | bytes 6152 | tf_op jit(solution)/shard_map/ppermute | solution.py:189
  31.7 2.1 %collective-permute-done.12.refs_5_ = f32[4,128]{1,0:T(4,128)S(1)} collective-permute-done((f32[4,128]{1,0:T(4,128)S(1)}, f32[4,128]{1,0:T(4,128)S(1)}, u32[]{:S(2)}, u32[]{:S(2)}) %collective-permute-start.12) | collective-permute-done | bytes 2080 | tf_op jit(solution)/shard_map/ppermute | solution.py:189
  33.8 0.7 %shard_map.83 = (f32[16,128]{1,0:T(8,128)S(1)}, f32[4,128]{1,0:T(4,128)}, f32[16,128]{1,0:T(8,128)S(1)}, f32[1,512]{1,0:T(1,128)S(1)}) custom-call(f32[512,2048]{1,0:T(8,128)S(1)} %get-tuple-element.42.refs_0_, f32[16,128]{1,0:T(8,128)S(1)} %get-tuple-element.41.refs_1_, f32[16,128]{1,0:T(8,128)S(1)} %get-tuple-element.44.refs_2_, ...), custom_call_target="tpu_custom_call" | custom-call | tf_op jit(solution)/shard_map/pallas_call | solution.py:229
  34.5 0.1 collective-permute-start.13
  34.5 0.8 %collective-permute-start.14 = (f32[16,128]{1,0:T(8,128)S(1)}, f32[16,128]{1,0:T(8,128)S(1)}, u32[]{:S(2)}, u32[]{:S(2)}) collective-permute-start(f32[16,128]{1,0:T(8,128)S(1)} %get-tuple-element.49), channel_id=1, source_target_pairs={{0,2},{1,3},{2,0},{3,1},{4,6},{5,7},{6,4},{7,5},{8,10},{9,11},{10,... | collective-permute-start | bytes 24584 | tf_op jit(solution)/shard_map/ppermute | solution.py:189
  35.3 1.1 %collective-permute-start.15 = (f32[16,128]{1,0:T(8,128)S(1)}, f32[16,128]{1,0:T(8,128)S(1)}, u32[]{:S(2)}, u32[]{:S(2)}) collective-permute-start(f32[16,128]{1,0:T(8,128)S(1)} %get-tuple-element.49), channel_id=1, source_target_pairs={{0,3},{1,2},{2,1},{3,0},{4,7},{5,6},{6,5},{7,4},{8,11},{9,10},{10,... | collective-permute-start | bytes 24584 | tf_op jit(solution)/shard_map/ppermute | solution.py:189
  36.4 0.0 collective-permute-done.13
  36.4 1.9 %collective-permute-done.14 = f32[16,128]{1,0:T(8,128)S(1)} collective-permute-done((f32[16,128]{1,0:T(8,128)S(1)}, f32[16,128]{1,0:T(8,128)S(1)}, u32[]{:S(2)}, u32[]{:S(2)}) %collective-permute-start.14) | collective-permute-done | bytes 8224 | tf_op jit(solution)/shard_map/ppermute | solution.py:189
  38.3 0.1 collective-permute-done.15
  38.4 1.6 %collective-permute-start.16 = (f32[16,128]{1,0:T(8,128)S(1)}, f32[16,128]{1,0:T(8,128)S(1)}, u32[]{:S(2)}, u32[]{:S(2)}) collective-permute-start(f32[16,128]{1,0:T(8,128)S(1)} %add_add_fusion.refs_4_), channel_id=1, source_target_pairs={{0,4},{1,5},{2,6},{3,7},{4,0},{5,1},{6,2},{7,3},{8,12},{9,13},{10,... | collective-permute-start | bytes 24584 | tf_op jit(solution)/shard_map/ppermute | solution.py:189
  40.0 1.0 %collective-permute-start.17 = (f32[16,128]{1,0:T(8,128)S(1)}, f32[16,128]{1,0:T(8,128)S(1)}, u32[]{:S(2)}, u32[]{:S(2)}) collective-permute-start(f32[16,128]{1,0:T(8,128)S(1)} %add_add_fusion.refs_4_), channel_id=1, source_target_pairs={{0,8},{1,9},{2,10},{3,11},{4,12},{5,13},{6,14},{7,15},{8,0},{9,1},... | collective-permute-start | bytes 24584 | tf_op jit(solution)/shard_map/ppermute | solution.py:189
  41.0 1.8 %collective-permute-start.18 = (f32[16,128]{1,0:T(8,128)S(1)}, f32[16,128]{1,0:T(8,128)S(1)}, u32[]{:S(2)}, u32[]{:S(2)}) collective-permute-start(f32[16,128]{1,0:T(8,128)S(1)} %add_add_fusion.refs_4_), channel_id=1, source_target_pairs={{0,12},{1,13},{2,14},{3,15},{4,8},{5,9},{6,10},{7,11},{8,4},{9,5},... | collective-permute-start | bytes 24584 | tf_op jit(solution)/shard_map/ppermute | solution.py:189
  42.8 0.8 %shard_map.81.refs_0_ = f32[2048,512]{1,0:T(8,128)S(1)} custom-call(bf16[208,512]{1,0:T(8,128)(2,1)S(1)} %get-tuple-element.29.lhs_ref, bf16[208,2048]{1,0:T(8,128)(2,1)S(1)} %get-tuple-element.40.rhs_ref), custom_call_target="tpu_custom_call" | custom-call | flops 1000000000 | bytes 3906250 | tf_op jit(solution)/shard_map/pallas_call | solution.py:229
  43.6 0.0 collective-permute-done.16.refs_5_
  43.6 1.0 %collective-permute-done.17.refs_6_ = f32[16,128]{1,0:T(8,128)S(1)} collective-permute-done((f32[16,128]{1,0:T(8,128)S(1)}, f32[16,128]{1,0:T(8,128)S(1)}, u32[]{:S(2)}, u32[]{:S(2)}) %collective-permute-start.17) | collective-permute-done | bytes 8224 | tf_op jit(solution)/shard_map/ppermute | solution.py:189
  44.6 1.9 %collective-permute-done.18.refs_7_ = f32[16,128]{1,0:T(8,128)S(1)} collective-permute-done((f32[16,128]{1,0:T(8,128)S(1)}, f32[16,128]{1,0:T(8,128)S(1)}, u32[]{:S(2)}, u32[]{:S(2)}) %collective-permute-start.18) | collective-permute-done | bytes 8224 | tf_op jit(solution)/shard_map/ppermute | solution.py:189
  46.4 2.9 %shard_map.84 = (f32[2048,512]{1,0:T(8,128)}, f32[16,128]{1,0:T(8,128)}) custom-call(f32[2048,512]{1,0:T(8,128)S(1)} %shard_map.81.refs_0_, f32[16,128]{1,0:T(8,128)S(1)} %get-tuple-element.41.refs_1_, f32[16,128]{1,0:T(8,128)S(1)} %get-tuple-element.47.refs_2_, f32[1,512]{1,0:T(1,128)S(1)} %get-tuple-element.48.refs_3_, f32[16,128]{1,0:T(8,128)S(1)} %add_add_fusion.refs_4_, ...), custom_call_target="tpu_custom_call" | custom-call | tf_op jit(solution)/shard_map/pallas_call | solution.py:306
  (8 shorter events, 0.0 us)
Async XLA Ops:
  0.6 8.7 %collective-permute-start.1 = (f32[64,128]{1,0:T(8,128)}, f32[64,128]{1,0:T(8,128)S(1)}, u32[]{:S(2)}, u32[]{:S(2)}) collective-permute-start(f32[64,128]{1,0:T(8,128)} %bitcast.20), channel_id=1, source_target_pairs={{0,4},{1,5},{2,6},{3,7},{4,0},{5,1},{6,2},{7,3},{8,12},{9,13},{10,... | collective-permute-start | bytes 98312 | tf_op jit(solution)/shard_map/ppermute | solution.py:189
  3.7 5.6 %collective-permute-start.2 = (f32[64,128]{1,0:T(8,128)}, f32[64,128]{1,0:T(8,128)S(1)}, u32[]{:S(2)}, u32[]{:S(2)}) collective-permute-start(f32[64,128]{1,0:T(8,128)} %bitcast.21), channel_id=1, source_target_pairs={{0,8},{1,9},{2,10},{3,11},{4,12},{5,13},{6,14},{7,15},{8,0},{9,1},... | collective-permute-start | bytes 98312 | tf_op jit(solution)/shard_map/ppermute | solution.py:189
  6.3 5.9 %collective-permute-start.3 = (f32[64,128]{1,0:T(8,128)}, f32[64,128]{1,0:T(8,128)S(1)}, u32[]{:S(2)}, u32[]{:S(2)}) collective-permute-start(f32[64,128]{1,0:T(8,128)} %bitcast.22), channel_id=1, source_target_pairs={{0,12},{1,13},{2,14},{3,15},{4,8},{5,9},{6,10},{7,11},{8,4},{9,5},... | collective-permute-start | bytes 98312 | tf_op jit(solution)/shard_map/ppermute | solution.py:189
  7.5 6.3 %collective-permute-start = (f32[72,256]{1,0:T(8,128)S(1)}, f32[72,256]{1,0:T(8,128)S(1)}, u32[]{:S(2)}, u32[]{:S(2)}) collective-permute-start(f32[72,256]{1,0:T(8,128)S(1)} %get-tuple-element.28.refs_0_), channel_id=1, source_target_pairs={{0,16},{16,0},{1,17},{17,1},{2,18},{18,2},{3,19},{19,3},{4,20},{20... | collective-permute-start | bytes 221192 | tf_op jit(solution)/shard_map/ppermute | solution.py:189
  12.2 5.0 %collective-permute-start.4 = (f32[4,64,128]{2,1,0:T(8,128)S(1)}, f32[4,64,128]{2,1,0:T(8,128)S(1)}, u32[]{:S(2)}, u32[]{:S(2)}) collective-permute-start(f32[4,64,128]{2,1,0:T(8,128)S(1)} %pad_maximum_fusion.refs_0_), channel_id=1, source_target_pairs={{0,2},{1,3},{2,0},{3,1},{4,6},{5,7},{6,4},{7,5},{8,10},{9,11},{10,... | collective-permute-start | bytes 393224 | tf_op jit(solution)/shard_map/ppermute | solution.py:189
  17.3 1.6 %collective-permute-start.5 = (f32[8,64,128]{2,1,0:T(8,128)S(1)}, f32[8,64,128]{2,1,0:T(8,128)S(1)}, u32[]{:S(2)}, u32[]{:S(2)}) collective-permute-start(f32[8,64,128]{2,1,0:T(8,128)S(1)} %constant_dynamic-update-slice_fusion), channel_id=1, source_target_pairs={{0,1},{1,0},{2,3},{3,2},{4,5},{5,4},{6,7},{7,6},{8,9},{9,8},{10,11... | collective-permute-start | bytes 786440 | tf_op jit(solution)/shard_map/ppermute | solution.py:189
  19.4 1.9 %collective-permute-start.6 = (f32[16,128]{1,0:T(8,128)S(1)}, f32[16,128]{1,0:T(8,128)S(1)}, u32[]{:S(2)}, u32[]{:S(2)}) collective-permute-start(f32[16,128]{1,0:T(8,128)S(1)} %get-tuple-element.43), channel_id=1, source_target_pairs={{0,1},{1,0},{2,3},{3,2},{4,5},{5,4},{6,7},{7,6},{8,9},{9,8},{10,11... | collective-permute-start | bytes 24584 | tf_op jit(solution)/shard_map/ppermute | solution.py:189
  19.6 3.7 %collective-permute-start.7 = (f32[16,128]{1,0:T(8,128)S(1)}, f32[16,128]{1,0:T(8,128)S(1)}, u32[]{:S(2)}, u32[]{:S(2)}) collective-permute-start(f32[16,128]{1,0:T(8,128)S(1)} %get-tuple-element.43), channel_id=1, source_target_pairs={{0,2},{1,3},{2,0},{3,1},{4,6},{5,7},{6,4},{7,5},{8,10},{9,11},{10,... | collective-permute-start | bytes 24584 | tf_op jit(solution)/shard_map/ppermute | solution.py:189
  21.1 3.1 %collective-permute-start.8 = (f32[16,128]{1,0:T(8,128)S(1)}, f32[16,128]{1,0:T(8,128)S(1)}, u32[]{:S(2)}, u32[]{:S(2)}) collective-permute-start(f32[16,128]{1,0:T(8,128)S(1)} %get-tuple-element.43), channel_id=1, source_target_pairs={{0,3},{1,2},{2,1},{3,0},{4,7},{5,6},{6,5},{7,4},{8,11},{9,10},{10,... | collective-permute-start | bytes 24584 | tf_op jit(solution)/shard_map/ppermute | solution.py:189
  24.2 4.5 %collective-permute-start.10 = (f32[16,128]{1,0:T(8,128)S(1)}, f32[16,128]{1,0:T(8,128)S(1)}, u32[]{:S(2)}, u32[]{:S(2)}) collective-permute-start(f32[16,128]{1,0:T(8,128)S(1)} %add_add_fusion.1.refs_2_), channel_id=1, source_target_pairs={{0,8},{1,9},{2,10},{3,11},{4,12},{5,13},{6,14},{7,15},{8,0},{9,1},... | collective-permute-start | bytes 24584 | tf_op jit(solution)/shard_map/ppermute | solution.py:189
  24.2 5.5 %collective-permute-start.11 = (f32[16,128]{1,0:T(8,128)S(1)}, f32[16,128]{1,0:T(8,128)S(1)}, u32[]{:S(2)}, u32[]{:S(2)}) collective-permute-start(f32[16,128]{1,0:T(8,128)S(1)} %add_add_fusion.1.refs_2_), channel_id=1, source_target_pairs={{0,12},{1,13},{2,14},{3,15},{4,8},{5,9},{6,10},{7,11},{8,4},{9,5},... | collective-permute-start | bytes 24584 | tf_op jit(solution)/shard_map/ppermute | solution.py:189
  25.6 4.2 %collective-permute-start.9 = (f32[16,128]{1,0:T(8,128)S(1)}, f32[16,128]{1,0:T(8,128)S(1)}, u32[]{:S(2)}, u32[]{:S(2)}) collective-permute-start(f32[16,128]{1,0:T(8,128)S(1)} %add_add_fusion.1.refs_2_), channel_id=1, source_target_pairs={{0,4},{1,5},{2,6},{3,7},{4,0},{5,1},{6,2},{7,3},{8,12},{9,13},{10,... | collective-permute-start | bytes 24584 | tf_op jit(solution)/shard_map/ppermute | solution.py:189
  30.1 3.7 %collective-permute-start.12 = (f32[4,128]{1,0:T(4,128)S(1)}, f32[4,128]{1,0:T(4,128)S(1)}, u32[]{:S(2)}, u32[]{:S(2)}) collective-permute-start(f32[4,128]{1,0:T(4,128)S(1)} %get-tuple-element.46.refs_4_), channel_id=1, source_target_pairs={{0,16},{16,0},{1,17},{17,1},{2,18},{18,2},{3,19},{19,3},{4,20},{20... | collective-permute-start | bytes 6152 | tf_op jit(solution)/shard_map/ppermute | solution.py:189
  34.5 1.9 %collective-permute-start.13 = (f32[16,128]{1,0:T(8,128)S(1)}, f32[16,128]{1,0:T(8,128)S(1)}, u32[]{:S(2)}, u32[]{:S(2)}) collective-permute-start(f32[16,128]{1,0:T(8,128)S(1)} %get-tuple-element.49), channel_id=1, source_target_pairs={{0,1},{1,0},{2,3},{3,2},{4,5},{5,4},{6,7},{7,6},{8,9},{9,8},{10,11... | collective-permute-start | bytes 24584 | tf_op jit(solution)/shard_map/ppermute | solution.py:189
  34.5 3.7 %collective-permute-start.14 = (f32[16,128]{1,0:T(8,128)S(1)}, f32[16,128]{1,0:T(8,128)S(1)}, u32[]{:S(2)}, u32[]{:S(2)}) collective-permute-start(f32[16,128]{1,0:T(8,128)S(1)} %get-tuple-element.49), channel_id=1, source_target_pairs={{0,2},{1,3},{2,0},{3,1},{4,6},{5,7},{6,4},{7,5},{8,10},{9,11},{10,... | collective-permute-start | bytes 24584 | tf_op jit(solution)/shard_map/ppermute | solution.py:189
  35.3 3.1 %collective-permute-start.15 = (f32[16,128]{1,0:T(8,128)S(1)}, f32[16,128]{1,0:T(8,128)S(1)}, u32[]{:S(2)}, u32[]{:S(2)}) collective-permute-start(f32[16,128]{1,0:T(8,128)S(1)} %get-tuple-element.49), channel_id=1, source_target_pairs={{0,3},{1,2},{2,1},{3,0},{4,7},{5,6},{6,5},{7,4},{8,11},{9,10},{10,... | collective-permute-start | bytes 24584 | tf_op jit(solution)/shard_map/ppermute | solution.py:189
  38.4 5.2 %collective-permute-start.16 = (f32[16,128]{1,0:T(8,128)S(1)}, f32[16,128]{1,0:T(8,128)S(1)}, u32[]{:S(2)}, u32[]{:S(2)}) collective-permute-start(f32[16,128]{1,0:T(8,128)S(1)} %add_add_fusion.refs_4_), channel_id=1, source_target_pairs={{0,4},{1,5},{2,6},{3,7},{4,0},{5,1},{6,2},{7,3},{8,12},{9,13},{10,... | collective-permute-start | bytes 24584 | tf_op jit(solution)/shard_map/ppermute | solution.py:189
  40.0 4.5 %collective-permute-start.17 = (f32[16,128]{1,0:T(8,128)S(1)}, f32[16,128]{1,0:T(8,128)S(1)}, u32[]{:S(2)}, u32[]{:S(2)}) collective-permute-start(f32[16,128]{1,0:T(8,128)S(1)} %add_add_fusion.refs_4_), channel_id=1, source_target_pairs={{0,8},{1,9},{2,10},{3,11},{4,12},{5,13},{6,14},{7,15},{8,0},{9,1},... | collective-permute-start | bytes 24584 | tf_op jit(solution)/shard_map/ppermute | solution.py:189
  41.0 5.4 %collective-permute-start.18 = (f32[16,128]{1,0:T(8,128)S(1)}, f32[16,128]{1,0:T(8,128)S(1)}, u32[]{:S(2)}, u32[]{:S(2)}) collective-permute-start(f32[16,128]{1,0:T(8,128)S(1)} %add_add_fusion.refs_4_), channel_id=1, source_target_pairs={{0,12},{1,13},{2,14},{3,15},{4,8},{5,9},{6,10},{7,11},{8,4},{9,5},... | collective-permute-start | bytes 24584 | tf_op jit(solution)/shard_map/ppermute | solution.py:189

commit v3 on v0

v3 whole, which is shorter than its diff:
```python
import math

import jax
import jax.numpy as jnp
from jax import lax
from jax.experimental import pallas as pl
from jax.experimental.pallas import tpu as pltpu
from jax.sharding import PartitionSpec as P

BLOCK = 128
ITERS = 2
SCORE_GAIN = 0.0875
LOG2E = 1.4426950408889634
OFF = 1e30
EMB = 64
DEPTH = 3 * EMB + 16
F32, BF16 = jnp.float32, jnp.bfloat16

VMEM = pl.BlockSpec(memory_space=pltpu.VMEM)
HBM = pl.BlockSpec(memory_space=pltpu.HBM)
PARAMS = pltpu.CompilerParams(vmem_limit_bytes=16 * 1024 * 1024)


def home():
    m = lax.axis_index("imp")
    return m, (m >> 2) & 1


def pieces(x):
    first = x.astype(BF16).astype(F32)
    rest = x - first
    second = rest.astype(BF16).astype(F32)
    third = (rest - second).astype(BF16).astype(F32)
    return first, second, third


def halves(block):
    high = block.astype(BF16)
    return high, (block - high.astype(F32)).astype(BF16)


def tree(terms):
    while len(terms) > 1:
        terms = [a + b for a, b in zip(terms[::2], terms[1::2])]
    return terms[0]


def in_order(w, own, other):
    return jnp.concatenate([jnp.where(w == 0, own, other), jnp.where(w == 0, other, own)], axis=0)


def prepare_kernel(
    ratio, imps, elig_hbm, class_hbm, scale_hbm, imp_hbm, adv_hbm,
    pack_ref, logs_ref, limit_ref, own_ref, elig_ref, class_ref, scale_ref, sems,
):
    moves = (
        (elig_hbm, elig_ref),
        (class_hbm, class_ref),
        (scale_hbm, scale_ref),
        (imp_hbm, pack_ref.at[0:EMB]),
        (adv_hbm, own_ref),
    )
    copies = [pltpu.make_async_copy(src, dst, sems.at[n]) for n, (src, dst) in enumerate(moves)]
    for copy in copies:
        copy.start()
    for copy in copies:
        copy.wait()
    exponent = 0.3 * class_ref[...].astype(F32) - 1.2
    limit = ratio * jnp.exp(exponent)
    limit_ref[...] = limit
    logs_ref[...] = jnp.log(scale_ref[...]) * LOG2E + (exponent * LOG2E + math.log2(ratio / imps))
    rows, cols = class_ref.shape[0], elig_ref.shape[0]
    flags = elig_ref[...].astype(F32)
    allowance = limit / imps
    totals = []
    for c in range(cols):
        total = jnp.zeros((1, BLOCK), F32)
        for b in range(rows):
            total = total + flags[c : c + 1, b : b + 1] * allowance[b : b + 1]
        totals.append(jnp.broadcast_to(jnp.sum(total, axis=1, keepdims=True), (1, BLOCK)))
    pack_ref[EMB : EMB + 8, :] = jnp.zeros((8, pack_ref.shape[1]), F32)
    for c in range(cols):
        pack_ref[EMB + c // 2 : EMB + c // 2 + 1, c % 2 * BLOCK : (c % 2 + 1) * BLOCK] = totals[c]
    pack_ref[EMB + 4 : EMB + 4 + cols, 0:rows] = flags


def own_flags(pack_ref, cols, rows):
    return pack_ref[EMB + 4 : EMB + 4 + cols, 0:rows]


def extra_rows(flags, logs):
    cols, rows = flags.shape
    count = logs.shape[0] * BLOCK
    at = lax.broadcasted_iota(jnp.int32, (rows, count), 0)
    spread = (at == lax.broadcasted_iota(jnp.int32, (rows, count), 1) // BLOCK).astype(BF16)
    masks = (jnp.dot(flags.astype(BF16), spread, preferred_element_type=F32) - 1.0) * OFF
    line = jnp.concatenate([logs[r : r + 1] for r in range(logs.shape[0])], axis=1)
    ones = jnp.ones((1, count), F32)
    parts = [masks, *pieces(line), ones, ones, ones, jnp.zeros((10 - cols, count), F32)]
    return jnp.concatenate(parts, axis=0).astype(BF16)


def impressions_kernel(cols, rows, own_ref, down_ref, side_ref, cross_ref, logs_ref, lhs_ref, lhs_t_ref, extra_ref, price_ref):
    _, w = home()
    half = lax.axis_index("adv")
    width = own_ref.shape[1]
    count = 2 * cols * BLOCK
    places = ((own_ref, w, half), (down_ref, w, 1 - half), (side_ref, 1 - w, half), (cross_ref, 1 - w, 1 - half))
    for ref, side, part in places:
        high, low = halves(ref[0:EMB, :] * (SCORE_GAIN * LOG2E))
        at = pl.ds(pl.multiple_of(side * (2 * width) + part * width, width), width)
        lhs_ref[0:EMB, at] = high
        lhs_ref[EMB : 2 * EMB, at] = low
        lhs_ref[2 * EMB : 3 * EMB, at] = high
    rows_of = [a[EMB : EMB + 2, :] + b[EMB : EMB + 2, :] for a, b in ((own_ref, down_ref), (side_ref, cross_ref))]
    price = in_order(w, *rows_of)
    price = jnp.concatenate([price[r : r + 1] for r in range(4)], axis=1)
    column = lax.broadcasted_iota(jnp.int32, (2 * cols, count), 1) // BLOCK
    own = (column == lax.broadcasted_iota(jnp.int32, (2 * cols, count), 0)).astype(F32)
    ones = jnp.ones((1, count), F32)
    parts = [own, ones, ones, ones, *pieces(-jnp.log(price) * LOG2E), jnp.zeros((10 - 2 * cols, count), F32)]
    lhs_ref[3 * EMB :, :] = jnp.concatenate(parts, axis=0).astype(BF16)
    for c in range(2 * cols):
        price_ref[c : c + 1, :] = price[:, c * BLOCK : (c + 1) * BLOCK]
    lhs_t_ref[...] = lhs_ref[...].T
    flags = in_order(w, own_flags(own_ref, cols, rows), own_flags(side_ref, cols, rows))
    extra_ref[...] = extra_rows(flags, logs_ref[...])


def first_kernel(keys, adv_ref, extra_ref, lhs_t_ref, *refs):
    *earlier, gain_ref, sums_ref, rhs_ref = refs
    m, _ = home()
    count = gain_ref.shape[0]
    if earlier:
        sums_ref[...] = earlier[0][...]
    else:
        sums_ref[...] = jnp.zeros(sums_ref.shape, F32)
    for n in range(0, len(keys), 2):
        two = slice(n * BLOCK, (n + 2) * BLOCK)
        for p in range(2):
            lanes = slice((n + p) * BLOCK, (n + p + 1) * BLOCK)
            high, low = halves(adv_ref[n + p])
            rhs_ref[0:EMB, lanes] = high
            rhs_ref[EMB : 2 * EMB, lanes] = high
            rhs_ref[2 * EMB : 3 * EMB, lanes] = low
            at = pl.multiple_of((m ^ keys[n + p]) * BLOCK, BLOCK)
            rhs_ref[3 * EMB :, lanes] = extra_ref[:, pl.ds(at, BLOCK)]
        sums = jnp.zeros((1, 2 * BLOCK), F32)
        for h in range(2):
            part = slice(h * count // 2, (h + 1) * count // 2)
            gain = jnp.exp2(jnp.dot(lhs_t_ref[part, :], rhs_ref[:, two], preferred_element_type=F32))
            sums = sums + jnp.sum(gain, axis=0, keepdims=True)
            gain_ref[part, two] = gain
        for p in range(2):
            sums_ref[pl.ds(m ^ keys[n + p], 1), :] = sums[:, p * BLOCK : (p + 1) * BLOCK]


def rows_kernel(lhs_ref, *refs):
    *rhs_refs, gain_ref = refs
    _, w = home()
    width = gain_ref.shape[1]
    lhs = lhs_ref[:, pl.ds(pl.multiple_of(w * width, width), width)]
    at = 0
    for ref in rhs_refs:
        for lane in range(0, ref.shape[1], BLOCK):
            rhs = ref[:, lane : lane + BLOCK].T
            gain_ref[at : at + BLOCK, :] = jnp.exp2(jnp.dot(rhs, lhs, preferred_element_type=F32))
            at += BLOCK


def tiles(refs, c):
    rows = slice(c * BLOCK, (c + 1) * BLOCK)
    return [(ref, (rows, slice(lane, lane + BLOCK))) for ref in refs for lane in range(0, ref.shape[1], BLOCK)]


def prices_kernel(keys, parts, limit_ref, *refs):
    gains, sum_refs, (part_ref, pacing_ref), bids = refs[:parts], refs[parts : -2 - parts], refs[-2 - parts : -parts], refs[-parts:]
    m, _ = home()
    limit = limit_ref[...]
    pacing_ref[...] = limit / jnp.maximum(tree([ref[...] for ref in sum_refs]), limit)
    factors = [pacing_ref[pl.ds(m ^ k, 1), :] for k in keys]
    for c in range(part_ref.shape[0]):
        total = jnp.zeros((BLOCK, BLOCK), F32)
        for (gain_ref, at), (bid_ref, _), factor in zip(tiles(gains, c), tiles(bids, c), factors):
            bid = gain_ref[at] * factor
            bid_ref[at] = bid
            total = total + bid
        part_ref[c : c + 1, :] = jnp.sum(total.T, axis=0, keepdims=True)


def second_kernel(keys, parts, imps, limit_ref, pacing_ref, price_ref, *refs):
    bids, part_refs, (sums_ref, prices_ref, factor_ref, change_ref) = refs[:parts], refs[parts:-4], refs[-4:]
    m, w = home()
    prices = tree([ref[...] for ref in part_refs])
    changes = price_ref[...] / prices
    half = prices.shape[0] // 2
    prices_ref[...] = jnp.where(w == 0, prices[0:half], prices[half:])
    change = jnp.where(w == 0, changes[0:half], changes[half:])
    for c in range(half):
        change_ref[:, c * BLOCK : (c + 1) * BLOCK] = change[c : c + 1]
    factor_ref[...] = pacing_ref[...] * (imps / limit_ref[...])
    totals = [jnp.zeros((8, BLOCK), F32) for _ in keys]
    for c in range(2 * half):
        column = jnp.broadcast_to(changes[c : c + 1], (BLOCK, BLOCK)).T
        for n, (ref, at) in enumerate(tiles(bids, c)):
            bid = ref[at]
            totals[n] = totals[n] + jnp.sum((bid * (bid * column)).reshape(BLOCK // 8, 8, BLOCK), axis=0)
    for k, total in zip(keys, totals):
        sums_ref[pl.ds(m ^ k, 1), :] = jnp.sum(total, axis=0, keepdims=True)
    sums_ref[...] = sums_ref[...] * (imps / (limit_ref[...] * pacing_ref[...]))


def final_kernel(keys, advs, gain_ref, limit_ref, factor_ref, change_ref, *refs):
    *sum_refs, out_ref, pacing_out, pacing_ref, scale_ref, block_ref, sems = refs
    m, _ = home()
    limit = limit_ref[...]
    pacing = limit / jnp.maximum(tree([ref[...] for ref in sum_refs]), limit)
    scale_ref[...] = pacing * factor_ref[...] * advs
    pacing_ref[...] = pacing
    copies = [pltpu.make_async_copy(pacing_ref, pacing_out, sems.at[len(keys)])]
    copies[0].start()
    change = change_ref[...]
    shape = (BLOCK, BLOCK)
    diagonal = lax.broadcasted_iota(jnp.int32, shape, 0) == lax.broadcasted_iota(jnp.int32, shape, 1)
    for n, k in enumerate(keys):
        rows = slice(n * BLOCK, (n + 1) * BLOCK)
        scale = jnp.sum(jnp.where(diagonal, scale_ref[pl.ds(m ^ k, 1), :], 0.0), axis=1, keepdims=True)
        gain = gain_ref[rows, :]
        block_ref[rows, :] = (gain * scale) * (gain * change)
        to = pl.ds(pl.multiple_of((m ^ k) * BLOCK, BLOCK), BLOCK)
        copy = pltpu.make_async_copy(block_ref.at[rows], out_ref.at[to], sems.at[n])
        copy.start()
        copies.append(copy)
    for copy in copies:
        copy.wait()


def swap(x, axis, k):
    return lax.ppermute(x, axis, [(i, i ^ k) for i in range(lax.axis_size(axis))])


def with_partners(x, keys):
    return [x] + [swap(x, "imp", k) for k in keys]


def over_impressions(sums):
    return with_partners(tree(with_partners(sums, (1, 2, 3))), (8,))


def staged(adv_embed, imp_embed, value_scale, spend_class, eligible):
    adv_count = spend_class.shape[0]
    rows, cols = eligible.shape
    imp_count = cols * BLOCK
    imps, advs = imp_count * lax.axis_size("imp"), adv_count * lax.axis_size("adv")
    ratio = imps / advs

    def shape(*dims, dtype=F32):
        return jax.ShapeDtypeStruct(dims, dtype)

    def call(kernel, out, operands, cost=0, **kw):
        return pl.pallas_call(
            kernel,
            out_shape=out,
            in_specs=[VMEM] * len(operands),
            out_specs=tuple(VMEM for _ in out),
            compiler_params=PARAMS,
            cost_estimate=pl.CostEstimate(flops=cost, bytes_accessed=cost // 256, transcendentals=0),
            **kw,
        )(*operands)

    adv_t = adv_embed.T
    ins = (eligible.T, spend_class.reshape(rows, BLOCK), value_scale.reshape(rows, BLOCK), imp_embed.T, adv_t)
    ins = [pltpu.with_memory_space_constraint(x, pltpu.HBM) for x in ins]
    pack, logs, limit, own = pl.pallas_call(
        lambda *refs: prepare_kernel(ratio, imps, *refs),
        out_shape=(shape(EMB + 8, imp_embed.shape[0]), shape(rows, BLOCK), shape(rows, BLOCK), shape(*adv_t.shape)),
        in_specs=[HBM] * len(ins),
        out_specs=(VMEM,) * 4,
        scratch_shapes=[
            pltpu.VMEM((cols, rows), jnp.int32),
            pltpu.VMEM((rows, BLOCK), jnp.int32),
            pltpu.VMEM((rows, BLOCK), F32),
            pltpu.SemaphoreType.DMA((len(ins),)),
        ],
        compiler_params=PARAMS,
    )(*ins)
    line = jnp.stack([own, *with_partners(adv_t, (8, 12, 4))[1:]])
    down, side, cross = [swap(pack, ("adv", "imp"), k) for k in (16, 4, 20)]
    plane = swap(line, "imp", 2)
    plane, _ = lax.optimization_barrier((plane, (down, side, cross)))
    pair = swap(jnp.concatenate([line, plane]), "imp", 1)
    at_line = (0, 8, 12, 4)
    at_plane = tuple(k + 2 for k in at_line)
    at_pair = tuple(k + 1 for k in at_line + at_plane)
    keys = at_line + at_plane + at_pair

    count = 2 * imp_count
    lhs, lhs_t, extra, first_price = call(
        lambda *refs: impressions_kernel(cols, rows, *refs),
        (
            shape(DEPTH, count, dtype=BF16),
            shape(count, DEPTH, dtype=BF16),
            shape(16, adv_count, dtype=BF16),
            shape(2 * cols, BLOCK),
        ),
        (pack, down, side, cross, logs),
        cost=10**8,
    )
    gains, rhs, sums = [], [], ()
    for at, blocks in ((at_line, line), (at_plane, plane), (at_pair, pair)):
        width = len(at) * BLOCK
        gain, total, side = call(
            lambda *refs, at=at: first_kernel(at, *refs),
            (pltpu.VMEM((count, width), F32), shape(rows, BLOCK), pltpu.VMEM((DEPTH, width), BF16)),
            (blocks, extra, lhs_t, *sums),
            cost=10**8 * len(at),
        )
        gains.append(gain)
        rhs.append(side)
        sums = (total,)

    terms = over_impressions(sums[0])
    (gain_rows,) = call(rows_kernel, (pltpu.VMEM((adv_count, imp_count), F32),), (lhs, *rhs), cost=10**9)

    part, pacing, *bids = call(
        lambda *refs: prices_kernel(keys, len(gains), *refs),
        (shape(2 * cols, BLOCK), shape(rows, BLOCK), *(pltpu.VMEM(g.shape, F32) for g in gains)),
        (limit, *gains, *terms),
    )
    sums, prices, factor, change = call(
        lambda *refs: second_kernel(keys, len(gains), imps, *refs),
        (shape(rows, BLOCK), pltpu.VMEM((cols, BLOCK), F32), shape(rows, BLOCK), shape(1, imp_count)),
        (limit, pacing, first_price, *bids, part, swap(part, "adv", 1)),
    )

    terms = over_impressions(sums)
    density, pacing = pl.pallas_call(
        lambda *refs: final_kernel(keys, advs, *refs),
        out_shape=(shape(adv_count, imp_count), shape(rows, BLOCK)),
        in_specs=[VMEM] * (4 + len(terms)),
        out_specs=(HBM, HBM),
        scratch_shapes=[
            pltpu.VMEM((rows, BLOCK), F32),
            pltpu.VMEM((rows, BLOCK), F32),
            pltpu.VMEM((adv_count, imp_count), F32),
            pltpu.SemaphoreType.DMA((rows + 1,)),
        ],
        compiler_params=PARAMS,
    )(gain_rows, limit, factor, change, *terms)
    return density, prices.reshape(imp_count), pacing.reshape(adv_count)


def plain(adv_embed, imp_embed, value_scale, spend_class, eligible):
    imp_block = lax.all_gather(imp_embed, "adv", axis=0, tiled=True)
    rows = lax.all_gather(adv_embed, "imp", axis=0, tiled=True)
    scores = SCORE_GAIN * jnp.einsum(
        "ae,ie->ai", rows, imp_block, precision=lax.Precision.HIGHEST, preferred_element_type=F32
    )
    total_advs = scores.shape[0] * lax.axis_size("adv")
    total_imps = scores.shape[1] * lax.axis_size("imp")
    mask = jnp.repeat(jnp.repeat(eligible.astype(F32), BLOCK, axis=0), BLOCK, axis=1)
    values = value_scale[:, None] * jnp.exp(scores) * mask
    allowance = total_imps / total_advs * jnp.exp(0.3 * spend_class.astype(F32) - 1.2)
    bid_tile = mask * allowance[:, None] / total_imps
    for _ in range(ITERS):
        prices = lax.psum(jnp.sum(bid_tile, axis=0), "adv")
        gain = values * bid_tile / prices[None, :]
        spending = lax.psum(jnp.sum(gain, axis=1), "imp")
        pacing = allowance / jnp.maximum(spending, allowance)
        bid_tile = pacing[:, None] * gain
    return bid_tile * total_advs, prices, pacing


def per_device(adv_embed, imp_embed, value_scale, spend_class, eligible):
    sizes = (lax.axis_size("adv"), lax.axis_size("imp"), adv_embed.shape, imp_embed.shape, eligible.shape)
    fits = sizes == (2, 16, (BLOCK, EMB), (2 * BLOCK, EMB), (16, 4))
    return (staged if fits else plain)(adv_embed, imp_embed, value_scale, spend_class, eligible)


def solution(mesh):
    in_specs = (
        P(("adv", "imp"), None),
        P(("imp", "adv"), None),
        P("adv"),
        P("adv"),
        P("adv", "imp"),
    )
    out_specs = (P("adv", "imp"), P("imp"), P("adv"))
    return jax.shard_map(
        per_device, mesh=mesh, in_specs=in_specs, out_specs=out_specs, check_vma=False
    )
```

time: 132 us -> 45 us (0.34)
  blocking collectives: 100 us -> 0 us
  starting transfers between devices: 0 us -> 20.9 us
  other arithmetic: 16.3 us -> 0.02 us
  waiting for transfers between devices: 0 us -> 14.6 us
  matrix products: 8.14 us -> 0 us
  Pallas kernels: 0 us -> 7.96 us
  local copies, waits for them, and re-layouts: 5.69 us -> 0.61 us
    psum x4 -> x0, blocking collectives: 71.1 us -> none  [the longest x2 60.3 us: per_device(): spending = lax.psum(row_totals, 'imp')]
    all_gather x2 -> x0, blocking collectives: 29.1 us -> none  [the longest x1 23.9 us: per_device(): lax.all_gather(adv_embed, 'imp', axis=0, tiled=True)]
    ppermute x0 -> x17, starting transfers between devices: none -> 20.9 us  [swap(): lax.ppermute(x, axis, [(i, i ^ k) for i in range(lax.axis_size(axis))])]
    ppermute x0 -> x17, waiting for transfers between devices: none -> 14.6 us  [swap(): lax.ppermute(x, axis, [(i, i ^ k) for i in range(lax.axis_size(axis))])]
    dot_general x1 -> x0, matrix products: 8.14 us -> none  [score_block(): jnp.einsum('ae,ie->ai', embed_rows, imp_block, precision=lax.Precision.HI...]
    reduce_sum x3 -> x0, other arithmetic: 8.06 us -> none  [the longest x1 4.33 us: per_device(): row_totals = jnp.sum(gain, axis=1)]
    pallas_call x0 -> x9, Pallas kernels: none -> 7.96 us  [the longest x7 4.57 us: call(): pl.pallas_call(kernel, out_shape=out, in_specs=[VMEM] * len(operands), ou...]
    mul x2 -> x0, other arithmetic: 7.56 us -> none  [the longest x1 6.86 us: per_device(): return (bid_tile * total_advs, prices, pacing)]
  transfers between devices with their start and end apart: 0 -> 17, of which waited for: 0 -> 13; matrix products, arithmetic and copies ran while one was open for 0% -> 1% of each run, Pallas kernels for 0% -> 7%
where the time goes in v3:
time: 45 us; the launch traced here: 44.9 us
  starting transfers between devices  20.9 us (46%)
  waiting for transfers between devices  14.6 us (32%)
  Pallas kernels  7.96 us (18%)
  between operations  0.74 us (2%)
  local copies, waits for them, and re-layouts  0.61 us (1%)
    ppermute x17, starting transfers between devices, swap(): lax.ppermute(x, axis, [(i, i ^ k) for i in range(lax.axis_size(axis))])  20.9 us
    ppermute x17, waiting for transfers between devices, swap(): lax.ppermute(x, axis, [(i, i ^ k) for i in range(lax.axis_size(axis))])  14.6 us
    pallas_call x7, Pallas kernels, call(): pl.pallas_call(kernel, out_shape=out, in_specs=[VMEM] * len(operands), ou...  4.57 us
    pallas_call x1, Pallas kernels, staged(): pl.pallas_call(lambda *refs: final_kernel(keys, advs, *refs), out_shape=(...  2.29 us
    pallas_call x1, Pallas kernels, staged(): pl.pallas_call(lambda *refs: prepare_kernel(ratio, imps, *refs), out_shap...  1.11 us
  transfers between devices with their start and end apart: 17, of which 13 were waited for; matrix products, arithmetic and copies ran while one was open for 1% of the time, Pallas kernels for 7%

profile of v3, /device:TPU:0, one launch (start us, length us, event | category | flops | bytes accessed | tf_op | source)
XLA Modules:
  0.0 44.9 jit_solution(8223303053918228603)
XLA Ops:
  0.6 3.1 %collective-permute-start.5 = (f32[64,128]{1,0:T(8,128)}, f32[64,128]{1,0:T(8,128)S(1)}, u32[]{:S(2)}, u32[]{:S(2)}) collective-permute-start(f32[64,128]{1,0:T(8,128)} %bitcast.21), channel_id=1, source_target_pairs={{0,4},{1,5},{2,6},{3,7},{4,0},{5,1},{6,2},{7,3},{8,12},{9,13},{10,... | collective-permute-start | bytes 98312 | tf_op jit(solution)/shard_map/ppermute | solution.py:239
  3.7 2.5 %collective-permute-start.4 = (f32[64,128]{1,0:T(8,128)}, f32[64,128]{1,0:T(8,128)S(1)}, u32[]{:S(2)}, u32[]{:S(2)}) collective-permute-start(f32[64,128]{1,0:T(8,128)} %bitcast.22), channel_id=1, source_target_pairs={{0,12},{1,13},{2,14},{3,15},{4,8},{5,9},{6,10},{7,11},{8,4},{9,5},... | collective-permute-start | bytes 98312 | tf_op jit(solution)/shard_map/ppermute | solution.py:239
  6.2 0.1 collective-permute-start.3
  6.3 1.1 %shard_map.76 = (f32[72,256]{1,0:T(8,128)S(1)}, f32[16,128]{1,0:T(8,128)S(1)}, f32[16,128]{1,0:T(8,128)S(1)}, f32[64,128]{1,0:T(8,128)S(1)}) custom-call(s32[4,16]{1,0:T(4,128)} %bitcast.27, s32[16,128]{1,0:T(8,128)} %bitcast.25, f32[16,128]{1,0:T(8,128)} %bitcast.26, f32[64,256]{1,0:T(8,128)} %bitcast.20, f32[64,128]{1,0:T(8,128)} %bitcast.24), custom_call_target="tpu_custom_call" | custom-call | tf_op jit(solution)/shard_map/pallas_call | solution.py:274
  7.4 2.8 %collective-permute-start.2 = (f32[72,256]{1,0:T(8,128)S(1)}, f32[72,256]{1,0:T(8,128)S(1)}, u32[]{:S(2)}, u32[]{:S(2)}) collective-permute-start(f32[72,256]{1,0:T(8,128)S(1)} %get-tuple-element.32.refs_0_), channel_id=1, source_target_pairs={{0,20},{1,21},{2,22},{3,23},{4,16},{5,17},{6,18},{7,19},{8,28},{9,... | collective-permute-start | bytes 221192 | tf_op jit(solution)/shard_map/ppermute | solution.py:239
  10.2 0.2 collective-permute-start.1
  10.5 0.0 collective-permute-done.5
  10.5 0.5 %collective-permute-start = (f32[72,256]{1,0:T(8,128)S(1)}, f32[72,256]{1,0:T(8,128)S(1)}, u32[]{:S(2)}, u32[]{:S(2)}) collective-permute-start(f32[72,256]{1,0:T(8,128)S(1)} %get-tuple-element.32.refs_0_), channel_id=1, source_target_pairs={{0,16},{1,17},{2,18},{3,19},{4,20},{5,21},{6,22},{7,23},{8,24},{9,... | collective-permute-start | bytes 221192 | tf_op jit(solution)/shard_map/ppermute | solution.py:239
  11.0 0.0 collective-permute-done.4
  11.0 0.6 %collective-permute-done.3 = f32[64,128]{1,0:T(8,128)S(1)} collective-permute-done((f32[64,128]{1,0:T(8,128)}, f32[64,128]{1,0:T(8,128)S(1)}, u32[]{:S(2)}, u32[]{:S(2)}) %collective-permute-start.3) | collective-permute-done | bytes 32800 | tf_op jit(solution)/shard_map/ppermute | solution.py:239
  11.6 1.6 %collective-permute-start.6 = (f32[4,64,128]{2,1,0:T(8,128)S(1)}, f32[4,64,128]{2,1,0:T(8,128)S(1)}, u32[]{:S(2)}, u32[]{:S(2)}) collective-permute-start(f32[4,64,128]{2,1,0:T(8,128)S(1)} %pad_maximum_fusion.refs_0_), channel_id=1, source_target_pairs={{0,2},{1,3},{2,0},{3,1},{4,6},{5,7},{6,4},{7,5},{8,10},{9,11},{10,... | collective-permute-start | bytes 393224 | tf_op jit(solution)/shard_map/ppermute | solution.py:239
  13.2 0.4 collective-permute-done.2.refs_3_
  13.6 1.0 %collective-permute-done.1.refs_2_ = f32[72,256]{1,0:T(8,128)S(1)} collective-permute-done((f32[72,256]{1,0:T(8,128)S(1)}, f32[72,256]{1,0:T(8,128)S(1)}, u32[]{:S(2)}, u32[]{:S(2)}) %collective-permute-start.1) | collective-permute-done | bytes 73760 | tf_op jit(solution)/shard_map/ppermute | solution.py:239
  14.6 0.2 collective-permute-done.refs_1_
  14.8 1.8 %collective-permute-done.6.refs_0_ = f32[4,64,128]{2,1,0:T(8,128)S(1)} collective-permute-done((f32[4,64,128]{2,1,0:T(8,128)S(1)}, f32[4,64,128]{2,1,0:T(8,128)S(1)}, u32[]{:S(2)}, u32[]{:S(2)}) %collective-permute-start.6) | collective-permute-done | bytes 131104 | tf_op jit(solution)/shard_map/ppermute | solution.py:239
  16.6 0.1 collective-permute-start.7
  16.7 0.3 shard_map.77
  17.0 0.5 %shard_map.78 = (f32[1024,512]{1,0:T(8,128)S(1)}, f32[16,128]{1,0:T(8,128)S(1)}, bf16[208,512]{1,0:T(8,128)(2,1)S(1)}) custom-call(f32[4,64,128]{2,1,0:T(8,128)S(1)} %pad_maximum_fusion.refs_0_, bf16[16,2048]{1,0:T(8,128)(2,1)S(1)} %get-tuple-element.36.refs_1_, bf16[1024,208]{1,0:T(8,128)(2,1)S(1)} %get-tuple-element.37.refs_2_), custom_call_target="tpu_custom_call" | custom-call | flops 400000000 | bytes 1562500 | tf_op jit(solution)/shard_map/pallas_call | solution.py:261
  17.5 0.5 %shard_map.79 = (f32[1024,512]{1,0:T(8,128)S(1)}, f32[16,128]{1,0:T(8,128)S(1)}, bf16[208,512]{1,0:T(8,128)(2,1)S(1)}) custom-call(f32[4,64,128]{2,1,0:T(8,128)S(1)} %collective-permute-done.6.refs_0_, bf16[16,2048]{1,0:T(8,128)(2,1)S(1)} %get-tuple-element.36.refs_1_, bf16[1024,208]{1,0:T(8,128)(2,1)S(1)} %get-tuple-element.37.refs_2_, ...), custom_call_target="tpu_custom_call" | custom-call | flops 400000000 | bytes 1562500 | tf_op jit(solution)/shard_map/pallas_call | solution.py:261
  17.9 0.3 collective-permute-done.7.refs_0_
  18.2 0.8 %shard_map.80 = (f32[1024,1024]{1,0:T(8,128)S(1)}, f32[16,128]{1,0:T(8,128)S(1)}, bf16[208,1024]{1,0:T(8,128)(2,1)S(1)}) custom-call(f32[8,64,128]{2,1,0:T(8,128)S(1)} %collective-permute-done.7.refs_0_, bf16[16,2048]{1,0:T(8,128)(2,1)S(1)} %get-tuple-element.36.refs_1_, bf16[1024,208]{1,0:T(8,128)(2,1)S(1)} %get-tuple-element.37.refs_2_, ...), custom_call_target="tpu_custom_call" | custom-call | flops 800000000 | bytes 3125000 | tf_op jit(solution)/shard_map/pallas_call | solution.py:261
  19.0 1.4 %collective-permute-start.10 = (f32[16,128]{1,0:T(8,128)S(1)}, f32[16,128]{1,0:T(8,128)S(1)}, u32[]{:S(2)}, u32[]{:S(2)}) collective-permute-start(f32[16,128]{1,0:T(8,128)S(1)} %get-tuple-element.48), channel_id=1, source_target_pairs={{0,3},{1,2},{2,1},{3,0},{4,7},{5,6},{6,5},{7,4},{8,11},{9,10},{10,... | collective-permute-start | bytes 24584 | tf_op jit(solution)/shard_map/ppermute | solution.py:239
  20.4 0.5 %collective-permute-start.9 = (f32[16,128]{1,0:T(8,128)S(1)}, f32[16,128]{1,0:T(8,128)S(1)}, u32[]{:S(2)}, u32[]{:S(2)}) collective-permute-start(f32[16,128]{1,0:T(8,128)S(1)} %get-tuple-element.48), channel_id=1, source_target_pairs={{0,2},{1,3},{2,0},{3,1},{4,6},{5,7},{6,4},{7,5},{8,10},{9,11},{10,... | collective-permute-start | bytes 24584 | tf_op jit(solution)/shard_map/ppermute | solution.py:239
  20.9 0.0 collective-permute-start.8
  20.9 1.2 %collective-permute-done.10 = f32[16,128]{1,0:T(8,128)S(1)} collective-permute-done((f32[16,128]{1,0:T(8,128)S(1)}, f32[16,128]{1,0:T(8,128)S(1)}, u32[]{:S(2)}, u32[]{:S(2)}) %collective-permute-start.10) | collective-permute-done | bytes 8224 | tf_op jit(solution)/shard_map/ppermute | solution.py:239
  22.1 1.9 %collective-permute-done.9 = f32[16,128]{1,0:T(8,128)S(1)} collective-permute-done((f32[16,128]{1,0:T(8,128)S(1)}, f32[16,128]{1,0:T(8,128)S(1)}, u32[]{:S(2)}, u32[]{:S(2)}) %collective-permute-start.9) | collective-permute-done | bytes 8224 | tf_op jit(solution)/shard_map/ppermute | solution.py:239
  24.0 0.0 collective-permute-done.8
  24.0 2.3 %collective-permute-start.11 = (f32[16,128]{1,0:T(8,128)S(1)}, f32[16,128]{1,0:T(8,128)S(1)}, u32[]{:S(2)}, u32[]{:S(2)}) collective-permute-start(f32[16,128]{1,0:T(8,128)S(1)} %add_add_fusion.1.refs_4_), channel_id=1, source_target_pairs={{0,8},{1,9},{2,10},{3,11},{4,12},{5,13},{6,14},{7,15},{8,0},{9,1},... | collective-permute-start | bytes 24584 | tf_op jit(solution)/shard_map/ppermute | solution.py:239
  26.3 2.3 %collective-permute-done.11.refs_5_ = f32[16,128]{1,0:T(8,128)S(1)} collective-permute-done((f32[16,128]{1,0:T(8,128)S(1)}, f32[16,128]{1,0:T(8,128)S(1)}, u32[]{:S(2)}, u32[]{:S(2)}) %collective-permute-start.11) | collective-permute-done | bytes 8224 | tf_op jit(solution)/shard_map/ppermute | solution.py:239
  28.6 0.8 %shard_map.82 = (f32[8,128]{1,0:T(8,128)S(1)}, f32[16,128]{1,0:T(8,128)S(1)}, f32[1024,512]{1,0:T(8,128)S(1)}, f32[1024,512]{1,0:T(8,128)S(1)}, f32[1024,1024]{1,0:T(8,128)S(1)}) custom-call(f32[16,128]{1,0:T(8,128)S(1)} %get-tuple-element.44.refs_0_.refs_1_, f32[1024,512]{1,0:T(8,128)S(1)} %get-tuple-element.45.refs_1_, ...), custom_call_target="tpu_custom_call" | custom-call | tf_op jit(solution)/shard_map/pallas_call | solution.py:261
  29.5 1.6 %collective-permute-start.12 = (f32[8,128]{1,0:T(8,128)S(1)}, f32[8,128]{1,0:T(8,128)S(1)}, u32[]{:S(2)}, u32[]{:S(2)}) collective-permute-start(f32[8,128]{1,0:T(8,128)S(1)} %get-tuple-element.54.refs_6_), channel_id=1, source_target_pairs={{0,16},{16,0},{1,17},{17,1},{2,18},{18,2},{3,19},{19,3},{4,20},{20... | collective-permute-start | bytes 12296 | tf_op jit(solution)/shard_map/ppermute | solution.py:239
  31.1 2.1 %collective-permute-done.12.refs_7_ = f32[8,128]{1,0:T(8,128)S(1)} collective-permute-done((f32[8,128]{1,0:T(8,128)S(1)}, f32[8,128]{1,0:T(8,128)S(1)}, u32[]{:S(2)}, u32[]{:S(2)}) %collective-permute-start.12) | collective-permute-done | bytes 4128 | tf_op jit(solution)/shard_map/ppermute | solution.py:239
  33.2 1.0 %shard_map.83 = (f32[16,128]{1,0:T(8,128)S(1)}, f32[4,128]{1,0:T(4,128)S(1)}, f32[16,128]{1,0:T(8,128)S(1)}, f32[1,512]{1,0:T(1,128)S(1)}) custom-call(f32[16,128]{1,0:T(8,128)S(1)} %get-tuple-element.44.refs_0_.refs_1_, f32[16,128]{1,0:T(8,128)S(1)} %get-tuple-element.49.refs_1_, f32[8,128]{1,0:T(8,128)S(1)} %get-tuple-element.50.refs_2_, ...), custom_call_target="tpu_custom_call" | custom-call | tf_op jit(solution)/shard_map/pallas_call | solution.py:261
  34.1 0.1 collective-permute-start.15
  34.2 0.6 %collective-permute-start.14 = (f32[16,128]{1,0:T(8,128)S(1)}, f32[16,128]{1,0:T(8,128)S(1)}, u32[]{:S(2)}, u32[]{:S(2)}) collective-permute-start(f32[16,128]{1,0:T(8,128)S(1)} %get-tuple-element.57), channel_id=1, source_target_pairs={{0,2},{1,3},{2,0},{3,1},{4,6},{5,7},{6,4},{7,5},{8,10},{9,11},{10,... | collective-permute-start | bytes 24584 | tf_op jit(solution)/shard_map/ppermute | solution.py:239
  34.8 1.3 %collective-permute-start.13 = (f32[16,128]{1,0:T(8,128)S(1)}, f32[16,128]{1,0:T(8,128)S(1)}, u32[]{:S(2)}, u32[]{:S(2)}) collective-permute-start(f32[16,128]{1,0:T(8,128)S(1)} %get-tuple-element.57), channel_id=1, source_target_pairs={{0,1},{1,0},{2,3},{3,2},{4,5},{5,4},{6,7},{7,6},{8,9},{9,8},{10,11... | collective-permute-start | bytes 24584 | tf_op jit(solution)/shard_map/ppermute | solution.py:239
  36.1 1.2 %collective-permute-done.15 = f32[16,128]{1,0:T(8,128)S(1)} collective-permute-done((f32[16,128]{1,0:T(8,128)S(1)}, f32[16,128]{1,0:T(8,128)S(1)}, u32[]{:S(2)}, u32[]{:S(2)}) %collective-permute-start.15) | collective-permute-done | bytes 8224 | tf_op jit(solution)/shard_map/ppermute | solution.py:239
  37.3 0.7 %collective-permute-done.14 = f32[16,128]{1,0:T(8,128)S(1)} collective-permute-done((f32[16,128]{1,0:T(8,128)S(1)}, f32[16,128]{1,0:T(8,128)S(1)}, u32[]{:S(2)}, u32[]{:S(2)}) %collective-permute-start.14) | collective-permute-done | bytes 8224 | tf_op jit(solution)/shard_map/ppermute | solution.py:239
  37.9 0.0 collective-permute-done.13
  37.9 2.3 %collective-permute-start.16 = (f32[16,128]{1,0:T(8,128)S(1)}, f32[16,128]{1,0:T(8,128)S(1)}, u32[]{:S(2)}, u32[]{:S(2)}) collective-permute-start(f32[16,128]{1,0:T(8,128)S(1)} %add_add_fusion.refs_4_), channel_id=1, source_target_pairs={{0,8},{1,9},{2,10},{3,11},{4,12},{5,13},{6,14},{7,15},{8,0},{9,1},... | collective-permute-start | bytes 24584 | tf_op jit(solution)/shard_map/ppermute | solution.py:239
  40.2 0.8 %shard_map.81.refs_0_ = f32[2048,512]{1,0:T(8,128)S(1)} custom-call(bf16[208,1024]{1,0:T(8,128)(2,1)S(1)} %get-tuple-element.34.lhs_ref, bf16[208,512]{1,0:T(8,128)(2,1)S(1)} %get-tuple-element.38.refs_0_, bf16[208,512]{1,0:T(8,128)(2,1)S(1)} %get-tuple-element.41.refs_1_, bf16[208,1024]{1,0:T(8,128)(2,1)S(1)} %get-tuple-element.43.refs_2_), custom_call_target="tpu_custom_call" | custom-call | flops 1000000000 | bytes 3906250 | tf_op jit(solution)/shard_map/pallas_call | solution.py:261
  41.1 0.6 %copy.12 = f32[512]{0:T(512)} copy(f32[512]{0:T(512)S(1)} %bitcast.15) | data formatting | bytes 4096
  41.6 0.9 %collective-permute-done.16.refs_5_ = f32[16,128]{1,0:T(8,128)S(1)} collective-permute-done((f32[16,128]{1,0:T(8,128)S(1)}, f32[16,128]{1,0:T(8,128)S(1)}, u32[]{:S(2)}, u32[]{:S(2)}) %collective-permute-start.16) | collective-permute-done | bytes 8224 | tf_op jit(solution)/shard_map/ppermute | solution.py:239
  42.6 2.3 %shard_map.84 = (f32[2048,512]{1,0:T(8,128)}, f32[16,128]{1,0:T(8,128)}) custom-call(f32[2048,512]{1,0:T(8,128)S(1)} %shard_map.81.refs_0_, f32[16,128]{1,0:T(8,128)S(1)} %get-tuple-element.44.refs_0_.refs_1_, f32[16,128]{1,0:T(8,128)S(1)} %get-tuple-element.55.refs_2_, f32[1,512]{1,0:T(1,128)S(1)} %get-tuple-element.56.refs_3_, ...), custom_call_target="tpu_custom_call" | custom-call | tf_op jit(solution)/shard_map/pallas_call | solution.py:337
  (8 shorter events, 0.0 us)
Async XLA Ops:
  0.6 9.9 %collective-permute-start.5 = (f32[64,128]{1,0:T(8,128)}, f32[64,128]{1,0:T(8,128)S(1)}, u32[]{:S(2)}, u32[]{:S(2)}) collective-permute-start(f32[64,128]{1,0:T(8,128)} %bitcast.21), channel_id=1, source_target_pairs={{0,4},{1,5},{2,6},{3,7},{4,0},{5,1},{6,2},{7,3},{8,12},{9,13},{10,... | collective-permute-start | bytes 98312 | tf_op jit(solution)/shard_map/ppermute | solution.py:239
  3.7 7.3 %collective-permute-start.4 = (f32[64,128]{1,0:T(8,128)}, f32[64,128]{1,0:T(8,128)S(1)}, u32[]{:S(2)}, u32[]{:S(2)}) collective-permute-start(f32[64,128]{1,0:T(8,128)} %bitcast.22), channel_id=1, source_target_pairs={{0,12},{1,13},{2,14},{3,15},{4,8},{5,9},{6,10},{7,11},{8,4},{9,5},... | collective-permute-start | bytes 98312 | tf_op jit(solution)/shard_map/ppermute | solution.py:239
  6.2 5.4 %collective-permute-start.3 = (f32[64,128]{1,0:T(8,128)}, f32[64,128]{1,0:T(8,128)S(1)}, u32[]{:S(2)}, u32[]{:S(2)}) collective-permute-start(f32[64,128]{1,0:T(8,128)} %bitcast.23), channel_id=1, source_target_pairs={{0,8},{1,9},{2,10},{3,11},{4,12},{5,13},{6,14},{7,15},{8,0},{9,1},... | collective-permute-start | bytes 98312 | tf_op jit(solution)/shard_map/ppermute | solution.py:239
  7.4 6.1 %collective-permute-start.2 = (f32[72,256]{1,0:T(8,128)S(1)}, f32[72,256]{1,0:T(8,128)S(1)}, u32[]{:S(2)}, u32[]{:S(2)}) collective-permute-start(f32[72,256]{1,0:T(8,128)S(1)} %get-tuple-element.32.refs_0_), channel_id=1, source_target_pairs={{0,20},{1,21},{2,22},{3,23},{4,16},{5,17},{6,18},{7,19},{8,28},{9,... | collective-permute-start | bytes 221192 | tf_op jit(solution)/shard_map/ppermute | solution.py:239
  10.2 4.4 %collective-permute-start.1 = (f32[72,256]{1,0:T(8,128)S(1)}, f32[72,256]{1,0:T(8,128)S(1)}, u32[]{:S(2)}, u32[]{:S(2)}) collective-permute-start(f32[72,256]{1,0:T(8,128)S(1)} %get-tuple-element.32.refs_0_), channel_id=1, source_target_pairs={{0,4},{1,5},{2,6},{3,7},{4,0},{5,1},{6,2},{7,3},{8,12},{9,13},{10,... | collective-permute-start | bytes 221192 | tf_op jit(solution)/shard_map/ppermute | solution.py:239
  10.5 4.4 %collective-permute-start = (f32[72,256]{1,0:T(8,128)S(1)}, f32[72,256]{1,0:T(8,128)S(1)}, u32[]{:S(2)}, u32[]{:S(2)}) collective-permute-start(f32[72,256]{1,0:T(8,128)S(1)} %get-tuple-element.32.refs_0_), channel_id=1, source_target_pairs={{0,16},{1,17},{2,18},{3,19},{4,20},{5,21},{6,22},{7,23},{8,24},{9,... | collective-permute-start | bytes 221192 | tf_op jit(solution)/shard_map/ppermute | solution.py:239
  11.6 5.0 %collective-permute-start.6 = (f32[4,64,128]{2,1,0:T(8,128)S(1)}, f32[4,64,128]{2,1,0:T(8,128)S(1)}, u32[]{:S(2)}, u32[]{:S(2)}) collective-permute-start(f32[4,64,128]{2,1,0:T(8,128)S(1)} %pad_maximum_fusion.refs_0_), channel_id=1, source_target_pairs={{0,2},{1,3},{2,0},{3,1},{4,6},{5,7},{6,4},{7,5},{8,10},{9,11},{10,... | collective-permute-start | bytes 393224 | tf_op jit(solution)/shard_map/ppermute | solution.py:239
  16.6 1.6 %collective-permute-start.7 = (f32[8,64,128]{2,1,0:T(8,128)S(1)}, f32[8,64,128]{2,1,0:T(8,128)S(1)}, u32[]{:S(2)}, u32[]{:S(2)}) collective-permute-start(f32[8,64,128]{2,1,0:T(8,128)S(1)} %constant_dynamic-update-slice_fusion), channel_id=1, source_target_pairs={{0,1},{1,0},{2,3},{3,2},{4,5},{5,4},{6,7},{7,6},{8,9},{9,8},{10,11... | collective-permute-start | bytes 786440 | tf_op jit(solution)/shard_map/ppermute | solution.py:239
  19.0 3.1 %collective-permute-start.10 = (f32[16,128]{1,0:T(8,128)S(1)}, f32[16,128]{1,0:T(8,128)S(1)}, u32[]{:S(2)}, u32[]{:S(2)}) collective-permute-start(f32[16,128]{1,0:T(8,128)S(1)} %get-tuple-element.48), channel_id=1, source_target_pairs={{0,3},{1,2},{2,1},{3,0},{4,7},{5,6},{6,5},{7,4},{8,11},{9,10},{10,... | collective-permute-start | bytes 24584 | tf_op jit(solution)/shard_map/ppermute | solution.py:239
  20.4 3.7 %collective-permute-start.9 = (f32[16,128]{1,0:T(8,128)S(1)}, f32[16,128]{1,0:T(8,128)S(1)}, u32[]{:S(2)}, u32[]{:S(2)}) collective-permute-start(f32[16,128]{1,0:T(8,128)S(1)} %get-tuple-element.48), channel_id=1, source_target_pairs={{0,2},{1,3},{2,0},{3,1},{4,6},{5,7},{6,4},{7,5},{8,10},{9,11},{10,... | collective-permute-start | bytes 24584 | tf_op jit(solution)/shard_map/ppermute | solution.py:239
  20.9 3.1 %collective-permute-start.8 = (f32[16,128]{1,0:T(8,128)S(1)}, f32[16,128]{1,0:T(8,128)S(1)}, u32[]{:S(2)}, u32[]{:S(2)}) collective-permute-start(f32[16,128]{1,0:T(8,128)S(1)} %get-tuple-element.48), channel_id=1, source_target_pairs={{0,1},{1,0},{2,3},{3,2},{4,5},{5,4},{6,7},{7,6},{8,9},{9,8},{10,11... | collective-permute-start | bytes 24584 | tf_op jit(solution)/shard_map/ppermute | solution.py:239
  24.0 4.6 %collective-permute-start.11 = (f32[16,128]{1,0:T(8,128)S(1)}, f32[16,128]{1,0:T(8,128)S(1)}, u32[]{:S(2)}, u32[]{:S(2)}) collective-permute-start(f32[16,128]{1,0:T(8,128)S(1)} %add_add_fusion.1.refs_4_), channel_id=1, source_target_pairs={{0,8},{1,9},{2,10},{3,11},{4,12},{5,13},{6,14},{7,15},{8,0},{9,1},... | collective-permute-start | bytes 24584 | tf_op jit(solution)/shard_map/ppermute | solution.py:239
  29.5 3.7 %collective-permute-start.12 = (f32[8,128]{1,0:T(8,128)S(1)}, f32[8,128]{1,0:T(8,128)S(1)}, u32[]{:S(2)}, u32[]{:S(2)}) collective-permute-start(f32[8,128]{1,0:T(8,128)S(1)} %get-tuple-element.54.refs_6_), channel_id=1, source_target_pairs={{0,16},{16,0},{1,17},{17,1},{2,18},{18,2},{3,19},{19,3},{4,20},{20... | collective-permute-start | bytes 12296 | tf_op jit(solution)/shard_map/ppermute | solution.py:239
  34.1 3.1 %collective-permute-start.15 = (f32[16,128]{1,0:T(8,128)S(1)}, f32[16,128]{1,0:T(8,128)S(1)}, u32[]{:S(2)}, u32[]{:S(2)}) collective-permute-start(f32[16,128]{1,0:T(8,128)S(1)} %get-tuple-element.57), channel_id=1, source_target_pairs={{0,3},{1,2},{2,1},{3,0},{4,7},{5,6},{6,5},{7,4},{8,11},{9,10},{10,... | collective-permute-start | bytes 24584 | tf_op jit(solution)/shard_map/ppermute | solution.py:239
  34.2 3.7 %collective-permute-start.14 = (f32[16,128]{1,0:T(8,128)S(1)}, f32[16,128]{1,0:T(8,128)S(1)}, u32[]{:S(2)}, u32[]{:S(2)}) collective-permute-start(f32[16,128]{1,0:T(8,128)S(1)} %get-tuple-element.57), channel_id=1, source_target_pairs={{0,2},{1,3},{2,0},{3,1},{4,6},{5,7},{6,4},{7,5},{8,10},{9,11},{10,... | collective-permute-start | bytes 24584 | tf_op jit(solution)/shard_map/ppermute | solution.py:239
  34.8 3.1 %collective-permute-start.13 = (f32[16,128]{1,0:T(8,128)S(1)}, f32[16,128]{1,0:T(8,128)S(1)}, u32[]{:S(2)}, u32[]{:S(2)}) collective-permute-start(f32[16,128]{1,0:T(8,128)S(1)} %get-tuple-element.57), channel_id=1, source_target_pairs={{0,1},{1,0},{2,3},{3,2},{4,5},{5,4},{6,7},{7,6},{8,9},{9,8},{10,11... | collective-permute-start | bytes 24584 | tf_op jit(solution)/shard_map/ppermute | solution.py:239
  37.9 4.6 %collective-permute-start.16 = (f32[16,128]{1,0:T(8,128)S(1)}, f32[16,128]{1,0:T(8,128)S(1)}, u32[]{:S(2)}, u32[]{:S(2)}) collective-permute-start(f32[16,128]{1,0:T(8,128)S(1)} %add_add_fusion.refs_4_), channel_id=1, source_target_pairs={{0,8},{1,9},{2,10},{3,11},{4,12},{5,13},{6,14},{7,15},{8,0},{9,1},... | collective-permute-start | bytes 24584 | tf_op jit(solution)/shard_map/ppermute | solution.py:239

commit v4 on v3

--- a/solution.py
+++ b/solution.py
@@ -243,8 +243,9 @@
     return [x] + [swap(x, "imp", k) for k in keys]
 
 
-def over_impressions(sums):
-    return with_partners(tree(with_partners(sums, (1, 2, 3))), (8,))
+def over_impressions(sums, stages):
+    first, last = stages
+    return with_partners(tree(with_partners(sums, first)), last)
 
 
 def staged(adv_embed, imp_embed, value_scale, spend_class, eligible):
@@ -288,11 +289,13 @@
     down, side, cross = [swap(pack, ("adv", "imp"), k) for k in (16, 4, 20)]
     plane = swap(line, "imp", 2)
     plane, _ = lax.optimization_barrier((plane, (down, side, cross)))
-    pair = swap(jnp.concatenate([line, plane]), "imp", 1)
+    ready, _ = lax.optimization_barrier((line, (down, side, cross)))
+    line_pair = swap(ready, "imp", 1)
     at_line = (0, 8, 12, 4)
+    at_line_pair = tuple(k + 1 for k in at_line)
     at_plane = tuple(k + 2 for k in at_line)
-    at_pair = tuple(k + 1 for k in at_line + at_plane)
-    keys = at_line + at_plane + at_pair
+    at_plane_pair = tuple(k + 3 for k in at_line)
+    keys = at_line + at_line_pair + at_plane + at_plane_pair
 
     count = 2 * imp_count
     lhs, lhs_t, extra, first_price = call(
@@ -307,10 +310,12 @@
         cost=10**8,
     )
     gains, rhs, sums = [], [], ()
-    for at, blocks in ((at_line, line), (at_plane, plane), (at_pair, pair)):
+
+    def work(at, blocks):
+        nonlocal sums
         width = len(at) * BLOCK
         gain, total, side = call(
-            lambda *refs, at=at: first_kernel(at, *refs),
+            lambda *refs: first_kernel(at, *refs),
             (pltpu.VMEM((count, width), F32), shape(rows, BLOCK), pltpu.VMEM((DEPTH, width), BF16)),
             (blocks, extra, lhs_t, *sums),
             cost=10**8 * len(at),
@@ -319,7 +324,13 @@
         rhs.append(side)
         sums = (total,)
 
-    terms = over_impressions(sums[0])
+    work(at_line, line)
+    plane, sums = lax.optimization_barrier((plane, sums))
+    work(at_line_pair, line_pair)
+    work(at_plane, plane)
+    work(at_plane_pair, swap(plane, "imp", 1))
+
+    terms = over_impressions(sums[0], ((8,),(1,2,3)))
     (gain_rows,) = call(rows_kernel, (pltpu.VMEM((adv_count, imp_count), F32),), (lhs, *rhs), cost=10**9)
 
     part, pacing, *bids = call(
@@ -333,7 +344,7 @@
         (limit, pacing, first_price, *bids, part, swap(part, "adv", 1)),
     )
 
-    terms = over_impressions(sums)
+    terms = over_impressions(sums, ((8,),(1,2,3)))
     density, pacing = pl.pallas_call(
         lambda *refs: final_kernel(keys, advs, *refs),
         out_shape=(shape(adv_count, imp_count), shape(rows, BLOCK)),

time: 45 us -> 43.1 us (0.958)
  waiting for transfers between devices: 14.6 us -> 12.8 us
    ppermute x17 -> x18, waiting for transfers between devices: 14.6 us -> 12.8 us  [swap(): lax.ppermute(x, axis, [(i, i ^ k) for i in range(lax.axis_size(axis))])]
    pallas_call x7 -> x8, Pallas kernels: 4.57 us -> 4.74 us  [call(): pl.pallas_call(kernel, out_shape=out, in_specs=[VMEM] * len(operands), ou...]
    ppermute x17 -> x18, starting transfers between devices: 20.9 us -> 20.7 us  [swap(): lax.ppermute(x, axis, [(i, i ^ k) for i in range(lax.axis_size(axis))])]
  transfers between devices with their start and end apart: 17 -> 18, of which waited for: 13 -> 12; matrix products, arithmetic and copies ran while one was open for 1% -> 1% of each run, Pallas kernels for 7% -> 8%
where the time goes in v4:
time: 43.1 us; the launch traced here: 42.9 us
  starting transfers between devices  20.7 us (48%)
  waiting for transfers between devices  12.8 us (30%)
  Pallas kernels  8.14 us (19%)
  between operations  0.72 us (2%)
  local copies, waits for them, and re-layouts  0.58 us (1%)
    ppermute x18, starting transfers between devices, swap(): lax.ppermute(x, axis, [(i, i ^ k) for i in range(lax.axis_size(axis))])  20.7 us
    ppermute x18, waiting for transfers between devices, swap(): lax.ppermute(x, axis, [(i, i ^ k) for i in range(lax.axis_size(axis))])  12.8 us
    pallas_call x8, Pallas kernels, call(): pl.pallas_call(kernel, out_shape=out, in_specs=[VMEM] * len(operands), ou...  4.74 us
    pallas_call x1, Pallas kernels, staged(): pl.pallas_call(lambda *refs: final_kernel(keys, advs, *refs), out_shape=(...  2.29 us
    pallas_call x1, Pallas kernels, staged(): pl.pallas_call(lambda *refs: prepare_kernel(ratio, imps, *refs), out_shap...  1.11 us
  transfers between devices with their start and end apart: 18, of which 12 were waited for; matrix products, arithmetic and copies ran while one was open for 1% of the time, Pallas kernels for 8%

profile of v4, /device:TPU:0, one launch (start us, length us, event | category | flops | bytes accessed | tf_op | source)
XLA Modules:
  0.0 42.9 jit_solution(5207883395229471719)
XLA Ops:
  0.6 3.1 %collective-permute-start.5 = (f32[64,128]{1,0:T(8,128)}, f32[64,128]{1,0:T(8,128)S(1)}, u32[]{:S(2)}, u32[]{:S(2)}) collective-permute-start(f32[64,128]{1,0:T(8,128)} %bitcast.14), channel_id=1, source_target_pairs={{0,4},{1,5},{2,6},{3,7},{4,0},{5,1},{6,2},{7,3},{8,12},{9,13},{10,... | collective-permute-start | bytes 98312 | tf_op jit(solution)/shard_map/ppermute | solution.py:239
  3.7 2.5 %collective-permute-start.4 = (f32[64,128]{1,0:T(8,128)}, f32[64,128]{1,0:T(8,128)S(1)}, u32[]{:S(2)}, u32[]{:S(2)}) collective-permute-start(f32[64,128]{1,0:T(8,128)} %bitcast.15), channel_id=1, source_target_pairs={{0,12},{1,13},{2,14},{3,15},{4,8},{5,9},{6,10},{7,11},{8,4},{9,5},... | collective-permute-start | bytes 98312 | tf_op jit(solution)/shard_map/ppermute | solution.py:239
  6.2 0.1 collective-permute-start.3
  6.3 1.1 %shard_map.76 = (f32[72,256]{1,0:T(8,128)S(1)}, f32[16,128]{1,0:T(8,128)S(1)}, f32[16,128]{1,0:T(8,128)S(1)}, f32[64,128]{1,0:T(8,128)S(1)}) custom-call(s32[4,16]{1,0:T(4,128)} %bitcast.23, s32[16,128]{1,0:T(8,128)} %bitcast.21, f32[16,128]{1,0:T(8,128)} %bitcast.22, f32[64,256]{1,0:T(8,128)} %bitcast.13, f32[64,128]{1,0:T(8,128)} %bitcast.17), custom_call_target="tpu_custom_call" | custom-call | tf_op jit(solution)/shard_map/pallas_call | solution.py:275
  7.4 2.8 %collective-permute-start.2 = (f32[72,256]{1,0:T(8,128)S(1)}, f32[72,256]{1,0:T(8,128)S(1)}, u32[]{:S(2)}, u32[]{:S(2)}) collective-permute-start(f32[72,256]{1,0:T(8,128)S(1)} %get-tuple-element.39.refs_0_), channel_id=1, source_target_pairs={{0,20},{1,21},{2,22},{3,23},{4,16},{5,17},{6,18},{7,19},{8,28},{9,... | collective-permute-start | bytes 221192 | tf_op jit(solution)/shard_map/ppermute | solution.py:239
  10.2 0.2 collective-permute-start.1
  10.5 0.0 collective-permute-done.5
  10.5 0.5 %collective-permute-start = (f32[72,256]{1,0:T(8,128)S(1)}, f32[72,256]{1,0:T(8,128)S(1)}, u32[]{:S(2)}, u32[]{:S(2)}) collective-permute-start(f32[72,256]{1,0:T(8,128)S(1)} %get-tuple-element.39.refs_0_), channel_id=1, source_target_pairs={{0,16},{1,17},{2,18},{3,19},{4,20},{5,21},{6,22},{7,23},{8,24},{9,... | collective-permute-start | bytes 221192 | tf_op jit(solution)/shard_map/ppermute | solution.py:239
  11.0 0.0 collective-permute-done.4
  11.0 0.6 %collective-permute-done.3 = f32[64,128]{1,0:T(8,128)S(1)} collective-permute-done((f32[64,128]{1,0:T(8,128)}, f32[64,128]{1,0:T(8,128)S(1)}, u32[]{:S(2)}, u32[]{:S(2)}) %collective-permute-start.3) | collective-permute-done | bytes 32800 | tf_op jit(solution)/shard_map/ppermute | solution.py:239
  11.6 1.6 %collective-permute-start.7 = (f32[4,64,128]{2,1,0:T(8,128)S(1)}, f32[4,64,128]{2,1,0:T(8,128)S(1)}, u32[]{:S(2)}, u32[]{:S(2)}) collective-permute-start(f32[4,64,128]{2,1,0:T(8,128)S(1)} %pad_maximum_fusion.refs_0_), channel_id=1, source_target_pairs={{0,2},{1,3},{2,0},{3,1},{4,6},{5,7},{6,4},{7,5},{8,10},{9,11},{10,... | collective-permute-start | bytes 393224 | tf_op jit(solution)/shard_map/ppermute | solution.py:239
  13.1 0.4 collective-permute-done.2.refs_3_
  13.6 1.0 %collective-permute-done.1.refs_2_ = f32[72,256]{1,0:T(8,128)S(1)} collective-permute-done((f32[72,256]{1,0:T(8,128)S(1)}, f32[72,256]{1,0:T(8,128)S(1)}, u32[]{:S(2)}, u32[]{:S(2)}) %collective-permute-start.1) | collective-permute-done | bytes 73760 | tf_op jit(solution)/shard_map/ppermute | solution.py:239
  14.6 0.2 collective-permute-done.refs_1_
  14.8 0.0 collective-permute-start.6
  14.8 0.3 shard_map.77
  15.1 0.5 %shard_map.78 = (f32[1024,512]{1,0:T(8,128)S(1)}, f32[16,128]{1,0:T(8,128)S(1)}, bf16[208,512]{1,0:T(8,128)(2,1)S(1)}) custom-call(f32[4,64,128]{2,1,0:T(8,128)S(1)} %pad_maximum_fusion.refs_0_, bf16[16,2048]{1,0:T(8,128)(2,1)S(1)} %get-tuple-element.43.refs_1_, bf16[1024,208]{1,0:T(8,128)(2,1)S(1)} %get-tuple-element.44.refs_2_), custom_call_target="tpu_custom_call" | custom-call | flops 400000000 | bytes 1562500 | tf_op jit(solution)/shard_map/pallas_call | solution.py:262
  15.6 1.0 %collective-permute-done.7.refs_0_ = f32[4,64,128]{2,1,0:T(8,128)S(1)} collective-permute-done((f32[4,64,128]{2,1,0:T(8,128)S(1)}, f32[4,64,128]{2,1,0:T(8,128)S(1)}, u32[]{:S(2)}, u32[]{:S(2)}) %collective-permute-start.7) | collective-permute-done | bytes 131104 | tf_op jit(solution)/shard_map/ppermute | solution.py:239
  16.6 0.0 collective-permute-start.8
  16.6 0.0 collective-permute-done.6.refs_0_
  16.6 0.5 %shard_map.79 = (f32[1024,512]{1,0:T(8,128)S(1)}, f32[16,128]{1,0:T(8,128)S(1)}, bf16[208,512]{1,0:T(8,128)(2,1)S(1)}) custom-call(f32[4,64,128]{2,1,0:T(8,128)S(1)} %collective-permute-done.6.refs_0_, bf16[16,2048]{1,0:T(8,128)(2,1)S(1)} %get-tuple-element.43.refs_1_, bf16[1024,208]{1,0:T(8,128)(2,1)S(1)} %get-tuple-element.44.refs_2_, ...), custom_call_target="tpu_custom_call" | custom-call | flops 400000000 | bytes 1562500 | tf_op jit(solution)/shard_map/pallas_call | solution.py:262
  17.1 0.5 %shard_map.80 = (f32[1024,512]{1,0:T(8,128)S(1)}, f32[16,128]{1,0:T(8,128)S(1)}, bf16[208,512]{1,0:T(8,128)(2,1)S(1)}) custom-call(f32[4,64,128]{2,1,0:T(8,128)S(1)} %collective-permute-done.7.refs_0_, bf16[16,2048]{1,0:T(8,128)(2,1)S(1)} %get-tuple-element.43.refs_1_, bf16[1024,208]{1,0:T(8,128)(2,1)S(1)} %get-tuple-element.44.refs_2_, ...), custom_call_target="tpu_custom_call" | custom-call | flops 400000000 | bytes 1562500 | tf_op jit(solution)/shard_map/pallas_call | solution.py:262
  17.6 0.4 collective-permute-done.8.refs_0_
  18.0 0.5 %shard_map.81 = (f32[1024,512]{1,0:T(8,128)S(1)}, f32[16,128]{1,0:T(8,128)S(1)}, bf16[208,512]{1,0:T(8,128)(2,1)S(1)}) custom-call(f32[4,64,128]{2,1,0:T(8,128)S(1)} %collective-permute-done.8.refs_0_, bf16[16,2048]{1,0:T(8,128)(2,1)S(1)} %get-tuple-element.43.refs_1_, bf16[1024,208]{1,0:T(8,128)(2,1)S(1)} %get-tuple-element.44.refs_2_, ...), custom_call_target="tpu_custom_call" | custom-call | flops 400000000 | bytes 1562500 | tf_op jit(solution)/shard_map/pallas_call | solution.py:262
  18.4 2.3 %collective-permute-start.9 = (f32[16,128]{1,0:T(8,128)S(1)}, f32[16,128]{1,0:T(8,128)S(1)}, u32[]{:S(2)}, u32[]{:S(2)}) collective-permute-start(f32[16,128]{1,0:T(8,128)S(1)} %get-tuple-element.61), channel_id=1, source_target_pairs={{0,8},{1,9},{2,10},{3,11},{4,12},{5,13},{6,14},{7,15},{8,0},{9,1},... | collective-permute-start | bytes 24584 | tf_op jit(solution)/shard_map/ppermute | solution.py:239
  20.7 2.3 %collective-permute-done.9 = f32[16,128]{1,0:T(8,128)S(1)} collective-permute-done((f32[16,128]{1,0:T(8,128)S(1)}, f32[16,128]{1,0:T(8,128)S(1)}, u32[]{:S(2)}, u32[]{:S(2)}) %collective-permute-start.9) | collective-permute-done | bytes 8224 | tf_op jit(solution)/shard_map/ppermute | solution.py:239
  23.1 0.1 collective-permute-start.12
  23.1 1.4 %collective-permute-start.11 = (f32[16,128]{1,0:T(8,128)S(1)}, f32[16,128]{1,0:T(8,128)S(1)}, u32[]{:S(2)}, u32[]{:S(2)}) collective-permute-start(f32[16,128]{1,0:T(8,128)S(1)} %add.6.refs_5_), channel_id=1, source_target_pairs={{0,2},{1,3},{2,0},{3,1},{4,6},{5,7},{6,4},{7,5},{8,10},{9,11},{10,... | collective-permute-start | bytes 24584 | tf_op jit(solution)/shard_map/ppermute | solution.py:239
  24.6 0.3 collective-permute-start.10
  24.9 1.3 %collective-permute-done.12.refs_8_ = f32[16,128]{1,0:T(8,128)S(1)} collective-permute-done((f32[16,128]{1,0:T(8,128)S(1)}, f32[16,128]{1,0:T(8,128)S(1)}, u32[]{:S(2)}, u32[]{:S(2)}) %collective-permute-start.12) | collective-permute-done | bytes 8224 | tf_op jit(solution)/shard_map/ppermute | solution.py:239
  26.2 0.6 %collective-permute-done.11.refs_7_ = f32[16,128]{1,0:T(8,128)S(1)} collective-permute-done((f32[16,128]{1,0:T(8,128)S(1)}, f32[16,128]{1,0:T(8,128)S(1)}, u32[]{:S(2)}, u32[]{:S(2)}) %collective-permute-start.11) | collective-permute-done | bytes 8224 | tf_op jit(solution)/shard_map/ppermute | solution.py:239
  26.8 0.0 collective-permute-done.10.refs_6_
  26.8 0.9 %shard_map.83 = (f32[8,128]{1,0:T(8,128)S(1)}, f32[16,128]{1,0:T(8,128)S(1)}, f32[1024,512]{1,0:T(8,128)S(1)}, f32[1024,512]{1,0:T(8,128)S(1)}, f32[1024,512]{1,0:T(8,128)S(1)}, /*index=5*/f32[1024,512]{1,0:T(8,128)S(1)}) custom-call(f32[16,128]{1,0:T(8,128)S(1)} %get-tuple-element.56.refs_0_.refs_1_, f32[1024,512]{1,0:T(8,128)S(1)} %get-tuple-element.57.refs_1_, ...), custom_call_target="tpu_custom_call" | custom-call | tf_op jit(solution)/shard_map/pallas_call | solution.py:262
  27.7 1.6 %collective-permute-start.13 = (f32[8,128]{1,0:T(8,128)S(1)}, f32[8,128]{1,0:T(8,128)S(1)}, u32[]{:S(2)}, u32[]{:S(2)}) collective-permute-start(f32[8,128]{1,0:T(8,128)S(1)} %get-tuple-element.68.refs_7_), channel_id=1, source_target_pairs={{0,16},{16,0},{1,17},{17,1},{2,18},{18,2},{3,19},{19,3},{4,20},{20... | collective-permute-start | bytes 12296 | tf_op jit(solution)/shard_map/ppermute | solution.py:239
  29.3 2.1 %collective-permute-done.13.refs_8_ = f32[8,128]{1,0:T(8,128)S(1)} collective-permute-done((f32[8,128]{1,0:T(8,128)S(1)}, f32[8,128]{1,0:T(8,128)S(1)}, u32[]{:S(2)}, u32[]{:S(2)}) %collective-permute-start.13) | collective-permute-done | bytes 4128 | tf_op jit(solution)/shard_map/ppermute | solution.py:239
  31.4 1.0 %shard_map.84 = (f32[16,128]{1,0:T(8,128)S(1)}, f32[4,128]{1,0:T(4,128)S(1)}, f32[16,128]{1,0:T(8,128)S(1)}, f32[1,512]{1,0:T(1,128)S(1)}) custom-call(f32[16,128]{1,0:T(8,128)S(1)} %get-tuple-element.56.refs_0_.refs_1_, f32[16,128]{1,0:T(8,128)S(1)} %get-tuple-element.62.refs_1_, f32[8,128]{1,0:T(8,128)S(1)} %get-tuple-element.63.refs_2_, ...), custom_call_target="tpu_custom_call" | custom-call | tf_op jit(solution)/shard_map/pallas_call | solution.py:262
  32.3 2.3 %collective-permute-start.14 = (f32[16,128]{1,0:T(8,128)S(1)}, f32[16,128]{1,0:T(8,128)S(1)}, u32[]{:S(2)}, u32[]{:S(2)}) collective-permute-start(f32[16,128]{1,0:T(8,128)S(1)} %get-tuple-element.71), channel_id=1, source_target_pairs={{0,8},{1,9},{2,10},{3,11},{4,12},{5,13},{6,14},{7,15},{8,0},{9,1},... | collective-permute-start | bytes 24584 | tf_op jit(solution)/shard_map/ppermute | solution.py:239
  34.6 2.3 %collective-permute-done.14 = f32[16,128]{1,0:T(8,128)S(1)} collective-permute-done((f32[16,128]{1,0:T(8,128)S(1)}, f32[16,128]{1,0:T(8,128)S(1)}, u32[]{:S(2)}, u32[]{:S(2)}) %collective-permute-start.14) | collective-permute-done | bytes 8224 | tf_op jit(solution)/shard_map/ppermute | solution.py:239
  37.0 0.0 collective-permute-start.17
  37.0 1.4 %collective-permute-start.16 = (f32[16,128]{1,0:T(8,128)S(1)}, f32[16,128]{1,0:T(8,128)S(1)}, u32[]{:S(2)}, u32[]{:S(2)}) collective-permute-start(f32[16,128]{1,0:T(8,128)S(1)} %add.7.refs_4_), channel_id=1, source_target_pairs={{0,2},{1,3},{2,0},{3,1},{4,6},{5,7},{6,4},{7,5},{8,10},{9,11},{10,... | collective-permute-start | bytes 24584 | tf_op jit(solution)/shard_map/ppermute | solution.py:239
  38.4 0.4 collective-permute-start.15
  38.8 0.8 %shard_map.82.refs_0_ = f32[2048,512]{1,0:T(8,128)S(1)} custom-call(bf16[208,1024]{1,0:T(8,128)(2,1)S(1)} %get-tuple-element.41.lhs_ref, bf16[208,512]{1,0:T(8,128)(2,1)S(1)} %get-tuple-element.45.refs_0_, bf16[208,512]{1,0:T(8,128)(2,1)S(1)} %get-tuple-element.50.refs_1_, bf16[208,512]{1,0:T(8,128)(2,1)S(1)} %get-tuple-element.53.refs_2_, ...), custom_call_target="tpu_custom_call" | custom-call | flops 1000000000 | bytes 3906250 | tf_op jit(solution)/shard_map/pallas_call | solution.py:262
  39.6 0.6 %copy.8 = f32[512]{0:T(512)} copy(f32[512]{0:T(512)S(1)} %bitcast.11) | data formatting | bytes 4096
  40.2 0.0 collective-permute-done.17.refs_7_
  40.2 0.4 %collective-permute-done.16.refs_6_ = f32[16,128]{1,0:T(8,128)S(1)} collective-permute-done((f32[16,128]{1,0:T(8,128)S(1)}, f32[16,128]{1,0:T(8,128)S(1)}, u32[]{:S(2)}, u32[]{:S(2)}) %collective-permute-start.16) | collective-permute-done | bytes 8224 | tf_op jit(solution)/shard_map/ppermute | solution.py:239
  40.6 0.0 collective-permute-done.15.refs_5_
  40.6 2.3 %shard_map.85 = (f32[2048,512]{1,0:T(8,128)}, f32[16,128]{1,0:T(8,128)}) custom-call(f32[2048,512]{1,0:T(8,128)S(1)} %shard_map.82.refs_0_, f32[16,128]{1,0:T(8,128)S(1)} %get-tuple-element.56.refs_0_.refs_1_, f32[16,128]{1,0:T(8,128)S(1)} %get-tuple-element.69.refs_2_, f32[1,512]{1,0:T(1,128)S(1)} %get-tuple-element.70.refs_3_, f32[16,128]{1,0:T(8,128)S(1)} %add.7.refs_4_, ...), custom_call_target="tpu_custom_call" | custom-call | tf_op jit(solution)/shard_map/pallas_call | solution.py:348
  (3 shorter events, 0.0 us)
Async XLA Ops:
  0.6 9.8 %collective-permute-start.5 = (f32[64,128]{1,0:T(8,128)}, f32[64,128]{1,0:T(8,128)S(1)}, u32[]{:S(2)}, u32[]{:S(2)}) collective-permute-start(f32[64,128]{1,0:T(8,128)} %bitcast.14), channel_id=1, source_target_pairs={{0,4},{1,5},{2,6},{3,7},{4,0},{5,1},{6,2},{7,3},{8,12},{9,13},{10,... | collective-permute-start | bytes 98312 | tf_op jit(solution)/shard_map/ppermute | solution.py:239
  3.7 7.3 %collective-permute-start.4 = (f32[64,128]{1,0:T(8,128)}, f32[64,128]{1,0:T(8,128)S(1)}, u32[]{:S(2)}, u32[]{:S(2)}) collective-permute-start(f32[64,128]{1,0:T(8,128)} %bitcast.15), channel_id=1, source_target_pairs={{0,12},{1,13},{2,14},{3,15},{4,8},{5,9},{6,10},{7,11},{8,4},{9,5},... | collective-permute-start | bytes 98312 | tf_op jit(solution)/shard_map/ppermute | solution.py:239
  6.2 5.4 %collective-permute-start.3 = (f32[64,128]{1,0:T(8,128)}, f32[64,128]{1,0:T(8,128)S(1)}, u32[]{:S(2)}, u32[]{:S(2)}) collective-permute-start(f32[64,128]{1,0:T(8,128)} %bitcast.16), channel_id=1, source_target_pairs={{0,8},{1,9},{2,10},{3,11},{4,12},{5,13},{6,14},{7,15},{8,0},{9,1},... | collective-permute-start | bytes 98312 | tf_op jit(solution)/shard_map/ppermute | solution.py:239
  7.4 6.1 %collective-permute-start.2 = (f32[72,256]{1,0:T(8,128)S(1)}, f32[72,256]{1,0:T(8,128)S(1)}, u32[]{:S(2)}, u32[]{:S(2)}) collective-permute-start(f32[72,256]{1,0:T(8,128)S(1)} %get-tuple-element.39.refs_0_), channel_id=1, source_target_pairs={{0,20},{1,21},{2,22},{3,23},{4,16},{5,17},{6,18},{7,19},{8,28},{9,... | collective-permute-start | bytes 221192 | tf_op jit(solution)/shard_map/ppermute | solution.py:239
  10.2 4.4 %collective-permute-start.1 = (f32[72,256]{1,0:T(8,128)S(1)}, f32[72,256]{1,0:T(8,128)S(1)}, u32[]{:S(2)}, u32[]{:S(2)}) collective-permute-start(f32[72,256]{1,0:T(8,128)S(1)} %get-tuple-element.39.refs_0_), channel_id=1, source_target_pairs={{0,4},{1,5},{2,6},{3,7},{4,0},{5,1},{6,2},{7,3},{8,12},{9,13},{10,... | collective-permute-start | bytes 221192 | tf_op jit(solution)/shard_map/ppermute | solution.py:239
  10.5 4.4 %collective-permute-start = (f32[72,256]{1,0:T(8,128)S(1)}, f32[72,256]{1,0:T(8,128)S(1)}, u32[]{:S(2)}, u32[]{:S(2)}) collective-permute-start(f32[72,256]{1,0:T(8,128)S(1)} %get-tuple-element.39.refs_0_), channel_id=1, source_target_pairs={{0,16},{1,17},{2,18},{3,19},{4,20},{5,21},{6,22},{7,23},{8,24},{9,... | collective-permute-start | bytes 221192 | tf_op jit(solution)/shard_map/ppermute | solution.py:239
  11.6 5.0 %collective-permute-start.7 = (f32[4,64,128]{2,1,0:T(8,128)S(1)}, f32[4,64,128]{2,1,0:T(8,128)S(1)}, u32[]{:S(2)}, u32[]{:S(2)}) collective-permute-start(f32[4,64,128]{2,1,0:T(8,128)S(1)} %pad_maximum_fusion.refs_0_), channel_id=1, source_target_pairs={{0,2},{1,3},{2,0},{3,1},{4,6},{5,7},{6,4},{7,5},{8,10},{9,11},{10,... | collective-permute-start | bytes 393224 | tf_op jit(solution)/shard_map/ppermute | solution.py:239
  14.8 1.8 %collective-permute-start.6 = (f32[4,64,128]{2,1,0:T(8,128)S(1)}, f32[4,64,128]{2,1,0:T(8,128)S(1)}, u32[]{:S(2)}, u32[]{:S(2)}) collective-permute-start(f32[4,64,128]{2,1,0:T(8,128)S(1)} %pad_maximum_fusion.refs_0_), channel_id=1, source_target_pairs={{0,1},{1,0},{2,3},{3,2},{4,5},{5,4},{6,7},{7,6},{8,9},{9,8},{10,11... | collective-permute-start | bytes 393224 | tf_op jit(solution)/shard_map/ppermute | solution.py:239
  16.6 1.3 %collective-permute-start.8 = (f32[4,64,128]{2,1,0:T(8,128)S(1)}, f32[4,64,128]{2,1,0:T(8,128)S(1)}, u32[]{:S(2)}, u32[]{:S(2)}) collective-permute-start(f32[4,64,128]{2,1,0:T(8,128)S(1)} %collective-permute-done.7.refs_0_), channel_id=1, source_target_pairs={{0,1},{1,0},{2,3},{3,2},{4,5},{5,4},{6,7},{7,6},{8,9},{9,8},{10,11... | collective-permute-start | bytes 393224 | tf_op jit(solution)/shard_map/ppermute | solution.py:239
  18.4 4.6 %collective-permute-start.9 = (f32[16,128]{1,0:T(8,128)S(1)}, f32[16,128]{1,0:T(8,128)S(1)}, u32[]{:S(2)}, u32[]{:S(2)}) collective-permute-start(f32[16,128]{1,0:T(8,128)S(1)} %get-tuple-element.61), channel_id=1, source_target_pairs={{0,8},{1,9},{2,10},{3,11},{4,12},{5,13},{6,14},{7,15},{8,0},{9,1},... | collective-permute-start | bytes 24584 | tf_op jit(solution)/shard_map/ppermute | solution.py:239
  23.1 3.1 %collective-permute-start.12 = (f32[16,128]{1,0:T(8,128)S(1)}, f32[16,128]{1,0:T(8,128)S(1)}, u32[]{:S(2)}, u32[]{:S(2)}) collective-permute-start(f32[16,128]{1,0:T(8,128)S(1)} %add.6.refs_5_), channel_id=1, source_target_pairs={{0,3},{1,2},{2,1},{3,0},{4,7},{5,6},{6,5},{7,4},{8,11},{9,10},{10,... | collective-permute-start | bytes 24584 | tf_op jit(solution)/shard_map/ppermute | solution.py:239
  23.1 3.7 %collective-permute-start.11 = (f32[16,128]{1,0:T(8,128)S(1)}, f32[16,128]{1,0:T(8,128)S(1)}, u32[]{:S(2)}, u32[]{:S(2)}) collective-permute-start(f32[16,128]{1,0:T(8,128)S(1)} %add.6.refs_5_), channel_id=1, source_target_pairs={{0,2},{1,3},{2,0},{3,1},{4,6},{5,7},{6,4},{7,5},{8,10},{9,11},{10,... | collective-permute-start | bytes 24584 | tf_op jit(solution)/shard_map/ppermute | solution.py:239
  24.6 2.2 %collective-permute-start.10 = (f32[16,128]{1,0:T(8,128)S(1)}, f32[16,128]{1,0:T(8,128)S(1)}, u32[]{:S(2)}, u32[]{:S(2)}) collective-permute-start(f32[16,128]{1,0:T(8,128)S(1)} %add.6.refs_5_), channel_id=1, source_target_pairs={{0,1},{1,0},{2,3},{3,2},{4,5},{5,4},{6,7},{7,6},{8,9},{9,8},{10,11... | collective-permute-start | bytes 24584 | tf_op jit(solution)/shard_map/ppermute | solution.py:239
  27.7 3.7 %collective-permute-start.13 = (f32[8,128]{1,0:T(8,128)S(1)}, f32[8,128]{1,0:T(8,128)S(1)}, u32[]{:S(2)}, u32[]{:S(2)}) collective-permute-start(f32[8,128]{1,0:T(8,128)S(1)} %get-tuple-element.68.refs_7_), channel_id=1, source_target_pairs={{0,16},{16,0},{1,17},{17,1},{2,18},{18,2},{3,19},{19,3},{4,20},{20... | collective-permute-start | bytes 12296 | tf_op jit(solution)/shard_map/ppermute | solution.py:239
  32.3 4.6 %collective-permute-start.14 = (f32[16,128]{1,0:T(8,128)S(1)}, f32[16,128]{1,0:T(8,128)S(1)}, u32[]{:S(2)}, u32[]{:S(2)}) collective-permute-start(f32[16,128]{1,0:T(8,128)S(1)} %get-tuple-element.71), channel_id=1, source_target_pairs={{0,8},{1,9},{2,10},{3,11},{4,12},{5,13},{6,14},{7,15},{8,0},{9,1},... | collective-permute-start | bytes 24584 | tf_op jit(solution)/shard_map/ppermute | solution.py:239
  37.0 3.2 %collective-permute-start.17 = (f32[16,128]{1,0:T(8,128)S(1)}, f32[16,128]{1,0:T(8,128)S(1)}, u32[]{:S(2)}, u32[]{:S(2)}) collective-permute-start(f32[16,128]{1,0:T(8,128)S(1)} %add.7.refs_4_), channel_id=1, source_target_pairs={{0,3},{1,2},{2,1},{3,0},{4,7},{5,6},{6,5},{7,4},{8,11},{9,10},{10,... | collective-permute-start | bytes 24584 | tf_op jit(solution)/shard_map/ppermute | solution.py:239
  37.0 3.7 %collective-permute-start.16 = (f32[16,128]{1,0:T(8,128)S(1)}, f32[16,128]{1,0:T(8,128)S(1)}, u32[]{:S(2)}, u32[]{:S(2)}) collective-permute-start(f32[16,128]{1,0:T(8,128)S(1)} %add.7.refs_4_), channel_id=1, source_target_pairs={{0,2},{1,3},{2,0},{3,1},{4,6},{5,7},{6,4},{7,5},{8,10},{9,11},{10,... | collective-permute-start | bytes 24584 | tf_op jit(solution)/shard_map/ppermute | solution.py:239
  38.4 2.2 %collective-permute-start.15 = (f32[16,128]{1,0:T(8,128)S(1)}, f32[16,128]{1,0:T(8,128)S(1)}, u32[]{:S(2)}, u32[]{:S(2)}) collective-permute-start(f32[16,128]{1,0:T(8,128)S(1)} %add.7.refs_4_), channel_id=1, source_target_pairs={{0,1},{1,0},{2,3},{3,2},{4,5},{5,4},{6,7},{7,6},{8,9},{9,8},{10,11... | collective-permute-start | bytes 24584 | tf_op jit(solution)/shard_map/ppermute | solution.py:239

commit v5 on v4

--- a/solution.py
+++ b/solution.py
@@ -12,6 +12,7 @@
 SCORE_GAIN = 0.0875
 LOG2E = 1.4426950408889634
 OFF = 1e30
+SMALL = 2.0**-10
 EMB = 64
 DEPTH = 3 * EMB + 16
 F32, BF16 = jnp.float32, jnp.bfloat16
@@ -72,15 +73,12 @@
     rows, cols = class_ref.shape[0], elig_ref.shape[0]
     flags = elig_ref[...].astype(F32)
     allowance = limit / imps
-    totals = []
-    for c in range(cols):
-        total = jnp.zeros((1, BLOCK), F32)
-        for b in range(rows):
-            total = total + flags[c : c + 1, b : b + 1] * allowance[b : b + 1]
-        totals.append(jnp.broadcast_to(jnp.sum(total, axis=1, keepdims=True), (1, BLOCK)))
+    sums = jnp.concatenate([*pieces(allowance)], axis=1).astype(BF16)
+    sums = jnp.dot(flags.astype(BF16), sums, preferred_element_type=F32)
+    totals = jnp.broadcast_to(jnp.sum(sums, axis=1, keepdims=True), (cols, BLOCK))
     pack_ref[EMB : EMB + 8, :] = jnp.zeros((8, pack_ref.shape[1]), F32)
     for c in range(cols):
-        pack_ref[EMB + c // 2 : EMB + c // 2 + 1, c % 2 * BLOCK : (c % 2 + 1) * BLOCK] = totals[c]
+        pack_ref[EMB + c // 2 : EMB + c // 2 + 1, c % 2 * BLOCK : (c % 2 + 1) * BLOCK] = totals[c : c + 1]
     pack_ref[EMB + 4 : EMB + 4 + cols, 0:rows] = flags
 
 
@@ -173,23 +171,26 @@
     return [(ref, (rows, slice(lane, lane + BLOCK))) for ref in refs for lane in range(0, ref.shape[1], BLOCK)]
 
 
+def squares_kernel(parts, *refs):
+    for ref, out_ref in zip(refs[:parts], refs[parts:]):
+        out_ref[...] = (ref[...] * SMALL) * (ref[...] * SMALL)
+
+
 def prices_kernel(keys, parts, limit_ref, *refs):
-    gains, sum_refs, (part_ref, pacing_ref), bids = refs[:parts], refs[parts : -2 - parts], refs[-2 - parts : -parts], refs[-parts:]
+    gains, sum_refs, (part_ref, pacing_ref) = refs[:parts], refs[parts:-2], refs[-2:]
     m, _ = home()
     limit = limit_ref[...]
     pacing_ref[...] = limit / jnp.maximum(tree([ref[...] for ref in sum_refs]), limit)
     factors = [pacing_ref[pl.ds(m ^ k, 1), :] for k in keys]
     for c in range(part_ref.shape[0]):
         total = jnp.zeros((BLOCK, BLOCK), F32)
-        for (gain_ref, at), (bid_ref, _), factor in zip(tiles(gains, c), tiles(bids, c), factors):
-            bid = gain_ref[at] * factor
-            bid_ref[at] = bid
-            total = total + bid
+        for (ref, at), factor in zip(tiles(gains, c), factors):
+            total = total + ref[at] * factor
         part_ref[c : c + 1, :] = jnp.sum(total.T, axis=0, keepdims=True)
 
 
 def second_kernel(keys, parts, imps, limit_ref, pacing_ref, price_ref, *refs):
-    bids, part_refs, (sums_ref, prices_ref, factor_ref, change_ref) = refs[:parts], refs[parts:-4], refs[-4:]
+    squares, part_refs, (sums_ref, prices_ref, factor_ref, change_ref) = refs[:parts], refs[parts:-4], refs[-4:]
     m, w = home()
     prices = tree([ref[...] for ref in part_refs])
     changes = price_ref[...] / prices
@@ -202,12 +203,11 @@
     totals = [jnp.zeros((8, BLOCK), F32) for _ in keys]
     for c in range(2 * half):
         column = jnp.broadcast_to(changes[c : c + 1], (BLOCK, BLOCK)).T
-        for n, (ref, at) in enumerate(tiles(bids, c)):
-            bid = ref[at]
-            totals[n] = totals[n] + jnp.sum((bid * (bid * column)).reshape(BLOCK // 8, 8, BLOCK), axis=0)
+        for n, (ref, at) in enumerate(tiles(squares, c)):
+            totals[n] = totals[n] + jnp.sum((ref[at] * column).reshape(BLOCK // 8, 8, BLOCK), axis=0)
     for k, total in zip(keys, totals):
         sums_ref[pl.ds(m ^ k, 1), :] = jnp.sum(total, axis=0, keepdims=True)
-    sums_ref[...] = sums_ref[...] * (imps / (limit_ref[...] * pacing_ref[...]))
+    sums_ref[...] = sums_ref[...] * (factor_ref[...] / SMALL**2)
 
 
 def final_kernel(keys, advs, gain_ref, limit_ref, factor_ref, change_ref, *refs):
@@ -285,13 +285,13 @@
         ],
         compiler_params=PARAMS,
     )(*ins)
-    line = jnp.stack([own, *with_partners(adv_t, (8, 12, 4))[1:]])
+    line = jnp.stack([own, *with_partners(adv_t, (4, 12, 8))[1:]])
     down, side, cross = [swap(pack, ("adv", "imp"), k) for k in (16, 4, 20)]
     plane = swap(line, "imp", 2)
     plane, _ = lax.optimization_barrier((plane, (down, side, cross)))
     ready, _ = lax.optimization_barrier((line, (down, side, cross)))
     line_pair = swap(ready, "imp", 1)
-    at_line = (0, 8, 12, 4)
+    at_line = (0, 4, 12, 8)
     at_line_pair = tuple(k + 1 for k in at_line)
     at_plane = tuple(k + 2 for k in at_line)
     at_plane_pair = tuple(k + 3 for k in at_line)
@@ -330,18 +330,24 @@
     work(at_plane, plane)
     work(at_plane_pair, swap(plane, "imp", 1))
 
+    squares = call(
+        lambda *refs: squares_kernel(len(gains), *refs),
+        tuple(pltpu.VMEM(g.shape, F32) for g in gains),
+        gains,
+        cost=10**9,
+    )
     terms = over_impressions(sums[0], ((8,),(1,2,3)))
     (gain_rows,) = call(rows_kernel, (pltpu.VMEM((adv_count, imp_count), F32),), (lhs, *rhs), cost=10**9)
 
-    part, pacing, *bids = call(
+    part, pacing = call(
         lambda *refs: prices_kernel(keys, len(gains), *refs),
-        (shape(2 * cols, BLOCK), shape(rows, BLOCK), *(pltpu.VMEM(g.shape, F32) for g in gains)),
+        (shape(2 * cols, BLOCK), shape(rows, BLOCK)),
         (limit, *gains, *terms),
     )
     sums, prices, factor, change = call(
         lambda *refs: second_kernel(keys, len(gains), imps, *refs),
         (shape(rows, BLOCK), pltpu.VMEM((cols, BLOCK), F32), shape(rows, BLOCK), shape(1, imp_count)),
-        (limit, pacing, first_price, *bids, part, swap(part, "adv", 1)),
+        (limit, pacing, first_price, *squares, part, swap(part, "adv", 1)),
     )
 
     terms = over_impressions(sums, ((8,),(1,2,3)))

time: 43.1 us -> 42.4 us (0.984)
  waiting for transfers between devices: 12.8 us -> 10.7 us
  starting transfers between devices: 20.7 us -> 21.8 us
    ppermute x18, waiting for transfers between devices: 12.8 us -> 10.7 us  [swap(): lax.ppermute(x, axis, [(i, i ^ k) for i in range(lax.axis_size(axis))])]
    ppermute x18, starting transfers between devices: 20.7 us -> 21.8 us  [swap(): lax.ppermute(x, axis, [(i, i ^ k) for i in range(lax.axis_size(axis))])]
    pallas_call x8 -> x9, Pallas kernels: 4.74 us -> 4.96 us  [call(): pl.pallas_call(kernel, out_shape=out, in_specs=[VMEM] * len(operands), ou...]
  transfers between devices with their start and end apart: 18 -> 18, of which waited for: 12 -> 11; matrix products, arithmetic and copies ran while one was open for 1% -> 1% of each run, Pallas kernels for 8% -> 10%
where the time goes in v5:
time: 42.4 us; the launch traced here: 42.2 us
  starting transfers between devices  21.8 us (51%)
  waiting for transfers between devices  10.7 us (25%)
  Pallas kernels  8.39 us (20%)
  between operations  0.72 us (2%)
  local copies, waits for them, and re-layouts  0.58 us (1%)
    ppermute x18, starting transfers between devices, swap(): lax.ppermute(x, axis, [(i, i ^ k) for i in range(lax.axis_size(axis))])  21.8 us
    ppermute x18, waiting for transfers between devices, swap(): lax.ppermute(x, axis, [(i, i ^ k) for i in range(lax.axis_size(axis))])  10.7 us
    pallas_call x9, Pallas kernels, call(): pl.pallas_call(kernel, out_shape=out, in_specs=[VMEM] * len(operands), ou...  4.96 us
    pallas_call x1, Pallas kernels, staged(): pl.pallas_call(lambda *refs: final_kernel(keys, advs, *refs), out_shape=(...  2.29 us
    pallas_call x1, Pallas kernels, staged(): pl.pallas_call(lambda *refs: prepare_kernel(ratio, imps, *refs), out_shap...  1.15 us
  transfers between devices with their start and end apart: 18, of which 11 were waited for; matrix products, arithmetic and copies ran while one was open for 1% of the time, Pallas kernels for 10%

profile of v5, /device:TPU:0, one launch (start us, length us, event | category | flops | bytes accessed | tf_op | source)
XLA Modules:
  0.0 42.2 jit_solution(5657540742369572694)
XLA Ops:
  0.6 4.1 %collective-permute-start.5 = (f32[64,128]{1,0:T(8,128)}, f32[64,128]{1,0:T(8,128)S(1)}, u32[]{:S(2)}, u32[]{:S(2)}) collective-permute-start(f32[64,128]{1,0:T(8,128)} %bitcast.14), channel_id=1, source_target_pairs={{0,8},{1,9},{2,10},{3,11},{4,12},{5,13},{6,14},{7,15},{8,0},{9,1},... | collective-permute-start | bytes 98312 | tf_op jit(solution)/shard_map/ppermute | solution.py:239
  4.7 1.3 %collective-permute-start.4 = (f32[64,128]{1,0:T(8,128)}, f32[64,128]{1,0:T(8,128)S(1)}, u32[]{:S(2)}, u32[]{:S(2)}) collective-permute-start(f32[64,128]{1,0:T(8,128)} %bitcast.15), channel_id=1, source_target_pairs={{0,12},{1,13},{2,14},{3,15},{4,8},{5,9},{6,10},{7,11},{8,4},{9,5},... | collective-permute-start | bytes 98312 | tf_op jit(solution)/shard_map/ppermute | solution.py:239
  6.1 0.2 collective-permute-start.3
  6.3 1.1 %shard_map.76 = (f32[72,256]{1,0:T(8,128)S(1)}, f32[16,128]{1,0:T(8,128)S(1)}, f32[16,128]{1,0:T(8,128)S(1)}, f32[64,128]{1,0:T(8,128)S(1)}) custom-call(s32[4,16]{1,0:T(4,128)} %bitcast.23, s32[16,128]{1,0:T(8,128)} %bitcast.21, f32[16,128]{1,0:T(8,128)} %bitcast.22, f32[64,256]{1,0:T(8,128)} %bitcast.13, f32[64,128]{1,0:T(8,128)} %bitcast.17), custom_call_target="tpu_custom_call" | custom-call | tf_op jit(solution)/shard_map/pallas_call | solution.py:275
  7.5 2.8 %collective-permute-start.2 = (f32[72,256]{1,0:T(8,128)S(1)}, f32[72,256]{1,0:T(8,128)S(1)}, u32[]{:S(2)}, u32[]{:S(2)}) collective-permute-start(f32[72,256]{1,0:T(8,128)S(1)} %get-tuple-element.39.refs_0_), channel_id=1, source_target_pairs={{0,20},{1,21},{2,22},{3,23},{4,16},{5,17},{6,18},{7,19},{8,28},{9,... | collective-permute-start | bytes 221192 | tf_op jit(solution)/shard_map/ppermute | solution.py:239
  10.3 0.2 collective-permute-start.1
  10.5 0.0 collective-permute-done.5
  10.5 0.5 %collective-permute-start = (f32[72,256]{1,0:T(8,128)S(1)}, f32[72,256]{1,0:T(8,128)S(1)}, u32[]{:S(2)}, u32[]{:S(2)}) collective-permute-start(f32[72,256]{1,0:T(8,128)S(1)} %get-tuple-element.39.refs_0_), channel_id=1, source_target_pairs={{0,16},{1,17},{2,18},{3,19},{4,20},{5,21},{6,22},{7,23},{8,24},{9,... | collective-permute-start | bytes 221192 | tf_op jit(solution)/shard_map/ppermute | solution.py:239
  11.0 0.0 collective-permute-done.4
  11.0 0.0 collective-permute-done.3
  11.0 1.6 %collective-permute-start.7 = (f32[4,64,128]{2,1,0:T(8,128)S(1)}, f32[4,64,128]{2,1,0:T(8,128)S(1)}, u32[]{:S(2)}, u32[]{:S(2)}) collective-permute-start(f32[4,64,128]{2,1,0:T(8,128)S(1)} %pad_maximum_fusion.refs_0_), channel_id=1, source_target_pairs={{0,2},{1,3},{2,0},{3,1},{4,6},{5,7},{6,4},{7,5},{8,10},{9,11},{10,... | collective-permute-start | bytes 393224 | tf_op jit(solution)/shard_map/ppermute | solution.py:239
  12.6 0.8 %collective-permute-done.2.refs_3_ = f32[72,256]{1,0:T(8,128)S(1)} collective-permute-done((f32[72,256]{1,0:T(8,128)S(1)}, f32[72,256]{1,0:T(8,128)S(1)}, u32[]{:S(2)}, u32[]{:S(2)}) %collective-permute-start.2) | collective-permute-done | bytes 73760 | tf_op jit(solution)/shard_map/ppermute | solution.py:239
  13.4 1.2 %collective-permute-done.1.refs_2_ = f32[72,256]{1,0:T(8,128)S(1)} collective-permute-done((f32[72,256]{1,0:T(8,128)S(1)}, f32[72,256]{1,0:T(8,128)S(1)}, u32[]{:S(2)}, u32[]{:S(2)}) %collective-permute-start.1) | collective-permute-done | bytes 73760 | tf_op jit(solution)/shard_map/ppermute | solution.py:239
  14.6 0.2 collective-permute-done.refs_1_
  14.9 0.0 collective-permute-start.6
  14.9 0.3 shard_map.77
  15.2 0.5 %shard_map.78 = (f32[1024,512]{1,0:T(8,128)S(1)}, f32[16,128]{1,0:T(8,128)S(1)}, bf16[208,512]{1,0:T(8,128)(2,1)S(1)}) custom-call(f32[4,64,128]{2,1,0:T(8,128)S(1)} %pad_maximum_fusion.refs_0_, bf16[16,2048]{1,0:T(8,128)(2,1)S(1)} %get-tuple-element.43.refs_1_, bf16[1024,208]{1,0:T(8,128)(2,1)S(1)} %get-tuple-element.44.refs_2_), custom_call_target="tpu_custom_call" | custom-call | flops 400000000 | bytes 1562500 | tf_op jit(solution)/shard_map/pallas_call | solution.py:262
  15.6 0.4 %collective-permute-done.7.refs_0_ = f32[4,64,128]{2,1,0:T(8,128)S(1)} collective-permute-done((f32[4,64,128]{2,1,0:T(8,128)S(1)}, f32[4,64,128]{2,1,0:T(8,128)S(1)}, u32[]{:S(2)}, u32[]{:S(2)}) %collective-permute-start.7) | collective-permute-done | bytes 131104 | tf_op jit(solution)/shard_map/ppermute | solution.py:239
  16.1 0.1 collective-permute-start.8
  16.2 0.0 collective-permute-done.6.refs_0_
  16.2 0.5 %shard_map.79 = (f32[1024,512]{1,0:T(8,128)S(1)}, f32[16,128]{1,0:T(8,128)S(1)}, bf16[208,512]{1,0:T(8,128)(2,1)S(1)}) custom-call(f32[4,64,128]{2,1,0:T(8,128)S(1)} %collective-permute-done.6.refs_0_, bf16[16,2048]{1,0:T(8,128)(2,1)S(1)} %get-tuple-element.43.refs_1_, bf16[1024,208]{1,0:T(8,128)(2,1)S(1)} %get-tuple-element.44.refs_2_, ...), custom_call_target="tpu_custom_call" | custom-call | flops 400000000 | bytes 1562500 | tf_op jit(solution)/shard_map/pallas_call | solution.py:262
  16.7 0.5 %shard_map.80 = (f32[1024,512]{1,0:T(8,128)S(1)}, f32[16,128]{1,0:T(8,128)S(1)}, bf16[208,512]{1,0:T(8,128)(2,1)S(1)}) custom-call(f32[4,64,128]{2,1,0:T(8,128)S(1)} %collective-permute-done.7.refs_0_, bf16[16,2048]{1,0:T(8,128)(2,1)S(1)} %get-tuple-element.43.refs_1_, bf16[1024,208]{1,0:T(8,128)(2,1)S(1)} %get-tuple-element.44.refs_2_, ...), custom_call_target="tpu_custom_call" | custom-call | flops 400000000 | bytes 1562500 | tf_op jit(solution)/shard_map/pallas_call | solution.py:262
  17.1 0.3 collective-permute-done.8.refs_0_
  17.4 0.5 %shard_map.81 = (f32[1024,512]{1,0:T(8,128)S(1)}, f32[16,128]{1,0:T(8,128)S(1)}, bf16[208,512]{1,0:T(8,128)(2,1)S(1)}) custom-call(f32[4,64,128]{2,1,0:T(8,128)S(1)} %collective-permute-done.8.refs_0_, bf16[16,2048]{1,0:T(8,128)(2,1)S(1)} %get-tuple-element.43.refs_1_, bf16[1024,208]{1,0:T(8,128)(2,1)S(1)} %get-tuple-element.44.refs_2_, ...), custom_call_target="tpu_custom_call" | custom-call | flops 400000000 | bytes 1562500 | tf_op jit(solution)/shard_map/pallas_call | solution.py:262
  17.9 2.9 %collective-permute-start.9 = (f32[16,128]{1,0:T(8,128)S(1)}, f32[16,128]{1,0:T(8,128)S(1)}, u32[]{:S(2)}, u32[]{:S(2)}) collective-permute-start(f32[16,128]{1,0:T(8,128)S(1)} %get-tuple-element.61), channel_id=1, source_target_pairs={{0,8},{1,9},{2,10},{3,11},{4,12},{5,13},{6,14},{7,15},{8,0},{9,1},... | collective-permute-start | bytes 24584 | tf_op jit(solution)/shard_map/ppermute | solution.py:239
  20.8 1.7 %collective-permute-done.9 = f32[16,128]{1,0:T(8,128)S(1)} collective-permute-done((f32[16,128]{1,0:T(8,128)S(1)}, f32[16,128]{1,0:T(8,128)S(1)}, u32[]{:S(2)}, u32[]{:S(2)}) %collective-permute-start.9) | collective-permute-done | bytes 8224 | tf_op jit(solution)/shard_map/ppermute | solution.py:239
  22.5 0.3 collective-permute-start.12
  22.8 1.3 %collective-permute-start.11 = (f32[16,128]{1,0:T(8,128)S(1)}, f32[16,128]{1,0:T(8,128)S(1)}, u32[]{:S(2)}, u32[]{:S(2)}) collective-permute-start(f32[16,128]{1,0:T(8,128)S(1)} %add.6.refs_5_), channel_id=1, source_target_pairs={{0,2},{1,3},{2,0},{3,1},{4,6},{5,7},{6,4},{7,5},{8,10},{9,11},{10,... | collective-permute-start | bytes 24584 | tf_op jit(solution)/shard_map/ppermute | solution.py:239
  24.0 0.3 collective-permute-start.10
  24.4 1.3 %collective-permute-done.12.refs_8_ = f32[16,128]{1,0:T(8,128)S(1)} collective-permute-done((f32[16,128]{1,0:T(8,128)S(1)}, f32[16,128]{1,0:T(8,128)S(1)}, u32[]{:S(2)}, u32[]{:S(2)}) %collective-permute-start.12) | collective-permute-done | bytes 8224 | tf_op jit(solution)/shard_map/ppermute | solution.py:239
  25.6 0.8 %collective-permute-done.11.refs_7_ = f32[16,128]{1,0:T(8,128)S(1)} collective-permute-done((f32[16,128]{1,0:T(8,128)S(1)}, f32[16,128]{1,0:T(8,128)S(1)}, u32[]{:S(2)}, u32[]{:S(2)}) %collective-permute-start.11) | collective-permute-done | bytes 8224 | tf_op jit(solution)/shard_map/ppermute | solution.py:239
  26.4 0.0 collective-permute-done.10.refs_6_
  26.4 0.8 %shard_map.83 = (f32[8,128]{1,0:T(8,128)S(1)}, f32[16,128]{1,0:T(8,128)S(1)}) custom-call(f32[16,128]{1,0:T(8,128)S(1)} %get-tuple-element.56.refs_0_.refs_1_, f32[1024,512]{1,0:T(8,128)S(1)} %get-tuple-element.57.refs_1_.refs_0_, f32[1024,512]{1,0:T(8,128)S(1)} %get-tuple-element.58.refs_2_.refs_1_, f32[1024,512]{1,0:T(8,128)S(1)} %get-tuple-element.59.refs_3_.refs_2_, ...), custom_call_target="tpu_custom_call" | custom-call | tf_op jit(solution)/shard_map/pallas_call | solution.py:262
  27.2 1.6 %collective-permute-start.13 = (f32[8,128]{1,0:T(8,128)S(1)}, f32[8,128]{1,0:T(8,128)S(1)}, u32[]{:S(2)}, u32[]{:S(2)}) collective-permute-start(f32[8,128]{1,0:T(8,128)S(1)} %get-tuple-element.68.refs_7_), channel_id=1, source_target_pairs={{0,16},{16,0},{1,17},{17,1},{2,18},{18,2},{3,19},{19,3},{4,20},{20... | collective-permute-start | bytes 12296 | tf_op jit(solution)/shard_map/ppermute | solution.py:239
  28.8 0.5 %shard_map.84 = (f32[1024,512]{1,0:T(8,128)S(1)}, f32[1024,512]{1,0:T(8,128)S(1)}, f32[1024,512]{1,0:T(8,128)S(1)}, f32[1024,512]{1,0:T(8,128)S(1)}) custom-call(f32[1024,512]{1,0:T(8,128)S(1)} %get-tuple-element.57.refs_1_.refs_0_, f32[1024,512]{1,0:T(8,128)S(1)} %get-tuple-element.58.refs_2_.refs_1_, f32[1024,512]{1,0:T(8,128)S(1)} %get-tuple-element.59.refs_3_.refs_2_, ...), custom_call_target="tpu_custom_call" | custom-call | flops 1000000000 | bytes 3906250 | tf_op jit(solution)/shard_map/pallas_call | solution.py:262
  29.3 1.5 %collective-permute-done.13.refs_8_ = f32[8,128]{1,0:T(8,128)S(1)} collective-permute-done((f32[8,128]{1,0:T(8,128)S(1)}, f32[8,128]{1,0:T(8,128)S(1)}, u32[]{:S(2)}, u32[]{:S(2)}) %collective-permute-start.13) | collective-permute-done | bytes 4128 | tf_op jit(solution)/shard_map/ppermute | solution.py:239
  30.9 0.8 %shard_map.85 = (f32[16,128]{1,0:T(8,128)S(1)}, f32[4,128]{1,0:T(4,128)S(1)}, f32[16,128]{1,0:T(8,128)S(1)}, f32[1,512]{1,0:T(1,128)S(1)}) custom-call(f32[16,128]{1,0:T(8,128)S(1)} %get-tuple-element.56.refs_0_.refs_1_, f32[16,128]{1,0:T(8,128)S(1)} %get-tuple-element.62.refs_1_, f32[8,128]{1,0:T(8,128)S(1)} %get-tuple-element.63.refs_2_, ...), custom_call_target="tpu_custom_call" | custom-call | tf_op jit(solution)/shard_map/pallas_call | solution.py:262
  31.6 2.7 %collective-permute-start.14 = (f32[16,128]{1,0:T(8,128)S(1)}, f32[16,128]{1,0:T(8,128)S(1)}, u32[]{:S(2)}, u32[]{:S(2)}) collective-permute-start(f32[16,128]{1,0:T(8,128)S(1)} %get-tuple-element.71), channel_id=1, source_target_pairs={{0,8},{1,9},{2,10},{3,11},{4,12},{5,13},{6,14},{7,15},{8,0},{9,1},... | collective-permute-start | bytes 24584 | tf_op jit(solution)/shard_map/ppermute | solution.py:239
  34.4 1.9 %collective-permute-done.14 = f32[16,128]{1,0:T(8,128)S(1)} collective-permute-done((f32[16,128]{1,0:T(8,128)S(1)}, f32[16,128]{1,0:T(8,128)S(1)}, u32[]{:S(2)}, u32[]{:S(2)}) %collective-permute-start.14) | collective-permute-done | bytes 8224 | tf_op jit(solution)/shard_map/ppermute | solution.py:239
  36.2 0.0 collective-permute-start.17
  36.3 1.3 %collective-permute-start.16 = (f32[16,128]{1,0:T(8,128)S(1)}, f32[16,128]{1,0:T(8,128)S(1)}, u32[]{:S(2)}, u32[]{:S(2)}) collective-permute-start(f32[16,128]{1,0:T(8,128)S(1)} %add.7.refs_4_), channel_id=1, source_target_pairs={{0,2},{1,3},{2,0},{3,1},{4,6},{5,7},{6,4},{7,5},{8,10},{9,11},{10,... | collective-permute-start | bytes 24584 | tf_op jit(solution)/shard_map/ppermute | solution.py:239
  37.5 0.6 %collective-permute-start.15 = (f32[16,128]{1,0:T(8,128)S(1)}, f32[16,128]{1,0:T(8,128)S(1)}, u32[]{:S(2)}, u32[]{:S(2)}) collective-permute-start(f32[16,128]{1,0:T(8,128)S(1)} %add.7.refs_4_), channel_id=1, source_target_pairs={{0,1},{1,0},{2,3},{3,2},{4,5},{5,4},{6,7},{7,6},{8,9},{9,8},{10,11... | collective-permute-start | bytes 24584 | tf_op jit(solution)/shard_map/ppermute | solution.py:239
  38.1 0.8 %shard_map.82.refs_0_ = f32[2048,512]{1,0:T(8,128)S(1)} custom-call(bf16[208,1024]{1,0:T(8,128)(2,1)S(1)} %get-tuple-element.41.lhs_ref, bf16[208,512]{1,0:T(8,128)(2,1)S(1)} %get-tuple-element.45.refs_0_, bf16[208,512]{1,0:T(8,128)(2,1)S(1)} %get-tuple-element.50.refs_1_, bf16[208,512]{1,0:T(8,128)(2,1)S(1)} %get-tuple-element.53.refs_2_, ...), custom_call_target="tpu_custom_call" | custom-call | flops 1000000000 | bytes 3906250 | tf_op jit(solution)/shard_map/pallas_call | solution.py:262
  38.9 0.6 %copy.8 = f32[512]{0:T(512)} copy(f32[512]{0:T(512)S(1)} %bitcast.11) | data formatting | bytes 4096
  39.5 0.0 collective-permute-done.17.refs_7_
  39.5 0.4 %collective-permute-done.16.refs_6_ = f32[16,128]{1,0:T(8,128)S(1)} collective-permute-done((f32[16,128]{1,0:T(8,128)S(1)}, f32[16,128]{1,0:T(8,128)S(1)}, u32[]{:S(2)}, u32[]{:S(2)}) %collective-permute-start.16) | collective-permute-done | bytes 8224 | tf_op jit(solution)/shard_map/ppermute | solution.py:239
  39.9 0.0 collective-permute-done.15.refs_5_
  39.9 2.3 %shard_map.86 = (f32[2048,512]{1,0:T(8,128)}, f32[16,128]{1,0:T(8,128)}) custom-call(f32[2048,512]{1,0:T(8,128)S(1)} %shard_map.82.refs_0_, f32[16,128]{1,0:T(8,128)S(1)} %get-tuple-element.56.refs_0_.refs_1_, f32[16,128]{1,0:T(8,128)S(1)} %get-tuple-element.69.refs_2_, f32[1,512]{1,0:T(1,128)S(1)} %get-tuple-element.70.refs_3_, f32[16,128]{1,0:T(8,128)S(1)} %add.7.refs_4_, ...), custom_call_target="tpu_custom_call" | custom-call | tf_op jit(solution)/shard_map/pallas_call | solution.py:354
  (3 shorter events, 0.0 us)
Async XLA Ops:
  0.6 9.9 %collective-permute-start.5 = (f32[64,128]{1,0:T(8,128)}, f32[64,128]{1,0:T(8,128)S(1)}, u32[]{:S(2)}, u32[]{:S(2)}) collective-permute-start(f32[64,128]{1,0:T(8,128)} %bitcast.14), channel_id=1, source_target_pairs={{0,8},{1,9},{2,10},{3,11},{4,12},{5,13},{6,14},{7,15},{8,0},{9,1},... | collective-permute-start | bytes 98312 | tf_op jit(solution)/shard_map/ppermute | solution.py:239
  4.7 6.3 %collective-permute-start.4 = (f32[64,128]{1,0:T(8,128)}, f32[64,128]{1,0:T(8,128)S(1)}, u32[]{:S(2)}, u32[]{:S(2)}) collective-permute-start(f32[64,128]{1,0:T(8,128)} %bitcast.15), channel_id=1, source_target_pairs={{0,12},{1,13},{2,14},{3,15},{4,8},{5,9},{6,10},{7,11},{8,4},{9,5},... | collective-permute-start | bytes 98312 | tf_op jit(solution)/shard_map/ppermute | solution.py:239
  6.1 4.9 %collective-permute-start.3 = (f32[64,128]{1,0:T(8,128)}, f32[64,128]{1,0:T(8,128)S(1)}, u32[]{:S(2)}, u32[]{:S(2)}) collective-permute-start(f32[64,128]{1,0:T(8,128)} %bitcast.16), channel_id=1, source_target_pairs={{0,4},{1,5},{2,6},{3,7},{4,0},{5,1},{6,2},{7,3},{8,12},{9,13},{10,... | collective-permute-start | bytes 98312 | tf_op jit(solution)/shard_map/ppermute | solution.py:239
  7.5 5.9 %collective-permute-start.2 = (f32[72,256]{1,0:T(8,128)S(1)}, f32[72,256]{1,0:T(8,128)S(1)}, u32[]{:S(2)}, u32[]{:S(2)}) collective-permute-start(f32[72,256]{1,0:T(8,128)S(1)} %get-tuple-element.39.refs_0_), channel_id=1, source_target_pairs={{0,20},{1,21},{2,22},{3,23},{4,16},{5,17},{6,18},{7,19},{8,28},{9,... | collective-permute-start | bytes 221192 | tf_op jit(solution)/shard_map/ppermute | solution.py:239
  10.3 4.4 %collective-permute-start.1 = (f32[72,256]{1,0:T(8,128)S(1)}, f32[72,256]{1,0:T(8,128)S(1)}, u32[]{:S(2)}, u32[]{:S(2)}) collective-permute-start(f32[72,256]{1,0:T(8,128)S(1)} %get-tuple-element.39.refs_0_), channel_id=1, source_target_pairs={{0,4},{1,5},{2,6},{3,7},{4,0},{5,1},{6,2},{7,3},{8,12},{9,13},{10,... | collective-permute-start | bytes 221192 | tf_op jit(solution)/shard_map/ppermute | solution.py:239
  10.5 4.4 %collective-permute-start = (f32[72,256]{1,0:T(8,128)S(1)}, f32[72,256]{1,0:T(8,128)S(1)}, u32[]{:S(2)}, u32[]{:S(2)}) collective-permute-start(f32[72,256]{1,0:T(8,128)S(1)} %get-tuple-element.39.refs_0_), channel_id=1, source_target_pairs={{0,16},{1,17},{2,18},{3,19},{4,20},{5,21},{6,22},{7,23},{8,24},{9,... | collective-permute-start | bytes 221192 | tf_op jit(solution)/shard_map/ppermute | solution.py:239
  11.0 5.0 %collective-permute-start.7 = (f32[4,64,128]{2,1,0:T(8,128)S(1)}, f32[4,64,128]{2,1,0:T(8,128)S(1)}, u32[]{:S(2)}, u32[]{:S(2)}) collective-permute-start(f32[4,64,128]{2,1,0:T(8,128)S(1)} %pad_maximum_fusion.refs_0_), channel_id=1, source_target_pairs={{0,2},{1,3},{2,0},{3,1},{4,6},{5,7},{6,4},{7,5},{8,10},{9,11},{10,... | collective-permute-start | bytes 393224 | tf_op jit(solution)/shard_map/ppermute | solution.py:239
  14.9 1.3 %collective-permute-start.6 = (f32[4,64,128]{2,1,0:T(8,128)S(1)}, f32[4,64,128]{2,1,0:T(8,128)S(1)}, u32[]{:S(2)}, u32[]{:S(2)}) collective-permute-start(f32[4,64,128]{2,1,0:T(8,128)S(1)} %pad_maximum_fusion.refs_0_), channel_id=1, source_target_pairs={{0,1},{1,0},{2,3},{3,2},{4,5},{5,4},{6,7},{7,6},{8,9},{9,8},{10,11... | collective-permute-start | bytes 393224 | tf_op jit(solution)/shard_map/ppermute | solution.py:239
  16.1 1.3 %collective-permute-start.8 = (f32[4,64,128]{2,1,0:T(8,128)S(1)}, f32[4,64,128]{2,1,0:T(8,128)S(1)}, u32[]{:S(2)}, u32[]{:S(2)}) collective-permute-start(f32[4,64,128]{2,1,0:T(8,128)S(1)} %collective-permute-done.7.refs_0_), channel_id=1, source_target_pairs={{0,1},{1,0},{2,3},{3,2},{4,5},{5,4},{6,7},{7,6},{8,9},{9,8},{10,11... | collective-permute-start | bytes 393224 | tf_op jit(solution)/shard_map/ppermute | solution.py:239
  17.9 4.6 %collective-permute-start.9 = (f32[16,128]{1,0:T(8,128)S(1)}, f32[16,128]{1,0:T(8,128)S(1)}, u32[]{:S(2)}, u32[]{:S(2)}) collective-permute-start(f32[16,128]{1,0:T(8,128)S(1)} %get-tuple-element.61), channel_id=1, source_target_pairs={{0,8},{1,9},{2,10},{3,11},{4,12},{5,13},{6,14},{7,15},{8,0},{9,1},... | collective-permute-start | bytes 24584 | tf_op jit(solution)/shard_map/ppermute | solution.py:239
  22.5 3.1 %collective-permute-start.12 = (f32[16,128]{1,0:T(8,128)S(1)}, f32[16,128]{1,0:T(8,128)S(1)}, u32[]{:S(2)}, u32[]{:S(2)}) collective-permute-start(f32[16,128]{1,0:T(8,128)S(1)} %add.6.refs_5_), channel_id=1, source_target_pairs={{0,3},{1,2},{2,1},{3,0},{4,7},{5,6},{6,5},{7,4},{8,11},{9,10},{10,... | collective-permute-start | bytes 24584 | tf_op jit(solution)/shard_map/ppermute | solution.py:239
  22.8 3.7 %collective-permute-start.11 = (f32[16,128]{1,0:T(8,128)S(1)}, f32[16,128]{1,0:T(8,128)S(1)}, u32[]{:S(2)}, u32[]{:S(2)}) collective-permute-start(f32[16,128]{1,0:T(8,128)S(1)} %add.6.refs_5_), channel_id=1, source_target_pairs={{0,2},{1,3},{2,0},{3,1},{4,6},{5,7},{6,4},{7,5},{8,10},{9,11},{10,... | collective-permute-start | bytes 24584 | tf_op jit(solution)/shard_map/ppermute | solution.py:239
  24.0 2.4 %collective-permute-start.10 = (f32[16,128]{1,0:T(8,128)S(1)}, f32[16,128]{1,0:T(8,128)S(1)}, u32[]{:S(2)}, u32[]{:S(2)}) collective-permute-start(f32[16,128]{1,0:T(8,128)S(1)} %add.6.refs_5_), channel_id=1, source_target_pairs={{0,1},{1,0},{2,3},{3,2},{4,5},{5,4},{6,7},{7,6},{8,9},{9,8},{10,11... | collective-permute-start | bytes 24584 | tf_op jit(solution)/shard_map/ppermute | solution.py:239
  27.2 3.7 %collective-permute-start.13 = (f32[8,128]{1,0:T(8,128)S(1)}, f32[8,128]{1,0:T(8,128)S(1)}, u32[]{:S(2)}, u32[]{:S(2)}) collective-permute-start(f32[8,128]{1,0:T(8,128)S(1)} %get-tuple-element.68.refs_7_), channel_id=1, source_target_pairs={{0,16},{16,0},{1,17},{17,1},{2,18},{18,2},{3,19},{19,3},{4,20},{20... | collective-permute-start | bytes 12296 | tf_op jit(solution)/shard_map/ppermute | solution.py:239
  31.6 4.6 %collective-permute-start.14 = (f32[16,128]{1,0:T(8,128)S(1)}, f32[16,128]{1,0:T(8,128)S(1)}, u32[]{:S(2)}, u32[]{:S(2)}) collective-permute-start(f32[16,128]{1,0:T(8,128)S(1)} %get-tuple-element.71), channel_id=1, source_target_pairs={{0,8},{1,9},{2,10},{3,11},{4,12},{5,13},{6,14},{7,15},{8,0},{9,1},... | collective-permute-start | bytes 24584 | tf_op jit(solution)/shard_map/ppermute | solution.py:239
  36.2 3.2 %collective-permute-start.17 = (f32[16,128]{1,0:T(8,128)S(1)}, f32[16,128]{1,0:T(8,128)S(1)}, u32[]{:S(2)}, u32[]{:S(2)}) collective-permute-start(f32[16,128]{1,0:T(8,128)S(1)} %add.7.refs_4_), channel_id=1, source_target_pairs={{0,3},{1,2},{2,1},{3,0},{4,7},{5,6},{6,5},{7,4},{8,11},{9,10},{10,... | collective-permute-start | bytes 24584 | tf_op jit(solution)/shard_map/ppermute | solution.py:239
  36.3 3.7 %collective-permute-start.16 = (f32[16,128]{1,0:T(8,128)S(1)}, f32[16,128]{1,0:T(8,128)S(1)}, u32[]{:S(2)}, u32[]{:S(2)}) collective-permute-start(f32[16,128]{1,0:T(8,128)S(1)} %add.7.refs_4_), channel_id=1, source_target_pairs={{0,2},{1,3},{2,0},{3,1},{4,6},{5,7},{6,4},{7,5},{8,10},{9,11},{10,... | collective-permute-start | bytes 24584 | tf_op jit(solution)/shard_map/ppermute | solution.py:239
  37.5 2.4 %collective-permute-start.15 = (f32[16,128]{1,0:T(8,128)S(1)}, f32[16,128]{1,0:T(8,128)S(1)}, u32[]{:S(2)}, u32[]{:S(2)}) collective-permute-start(f32[16,128]{1,0:T(8,128)S(1)} %add.7.refs_4_), channel_id=1, source_target_pairs={{0,1},{1,0},{2,3},{3,2},{4,5},{5,4},{6,7},{7,6},{8,9},{9,8},{10,11... | collective-permute-start | bytes 24584 | tf_op jit(solution)/shard_map/ppermute | solution.py:239

commit v6 on v5

--- a/solution.py
+++ b/solution.py
@@ -64,6 +64,7 @@
     copies = [pltpu.make_async_copy(src, dst, sems.at[n]) for n, (src, dst) in enumerate(moves)]
     for copy in copies:
         copy.start()
+    pack_ref[EMB : EMB + 8, :] = jnp.zeros((8, pack_ref.shape[1]), F32)
     for copy in copies:
         copy.wait()
     exponent = 0.3 * class_ref[...].astype(F32) - 1.2
@@ -73,12 +74,8 @@
     rows, cols = class_ref.shape[0], elig_ref.shape[0]
     flags = elig_ref[...].astype(F32)
     allowance = limit / imps
-    sums = jnp.concatenate([*pieces(allowance)], axis=1).astype(BF16)
-    sums = jnp.dot(flags.astype(BF16), sums, preferred_element_type=F32)
-    totals = jnp.broadcast_to(jnp.sum(sums, axis=1, keepdims=True), (cols, BLOCK))
-    pack_ref[EMB : EMB + 8, :] = jnp.zeros((8, pack_ref.shape[1]), F32)
-    for c in range(cols):
-        pack_ref[EMB + c // 2 : EMB + c // 2 + 1, c % 2 * BLOCK : (c % 2 + 1) * BLOCK] = totals[c : c + 1]
+    sums = sum(jnp.dot(flags.astype(BF16), p.astype(BF16), preferred_element_type=F32) for p in pieces(allowance))
+    pack_ref[EMB : EMB + cols, 0:BLOCK] = sums
     pack_ref[EMB + 4 : EMB + 4 + cols, 0:rows] = flags
 
 
@@ -110,16 +107,15 @@
         lhs_ref[0:EMB, at] = high
         lhs_ref[EMB : 2 * EMB, at] = low
         lhs_ref[2 * EMB : 3 * EMB, at] = high
-    rows_of = [a[EMB : EMB + 2, :] + b[EMB : EMB + 2, :] for a, b in ((own_ref, down_ref), (side_ref, cross_ref))]
-    price = in_order(w, *rows_of)
-    price = jnp.concatenate([price[r : r + 1] for r in range(4)], axis=1)
+    lanes = [a[EMB : EMB + cols, 0:BLOCK] + b[EMB : EMB + cols, 0:BLOCK] for a, b in ((own_ref, down_ref), (side_ref, cross_ref))]
+    totals = jnp.sum(in_order(w, *lanes), axis=1, keepdims=True)
+    price_ref[...] = jnp.broadcast_to(totals, price_ref.shape)
+    price = jnp.concatenate([price_ref[c : c + 1, :] for c in range(2 * cols)], axis=1)
     column = lax.broadcasted_iota(jnp.int32, (2 * cols, count), 1) // BLOCK
     own = (column == lax.broadcasted_iota(jnp.int32, (2 * cols, count), 0)).astype(F32)
     ones = jnp.ones((1, count), F32)
     parts = [own, ones, ones, ones, *pieces(-jnp.log(price) * LOG2E), jnp.zeros((10 - 2 * cols, count), F32)]
     lhs_ref[3 * EMB :, :] = jnp.concatenate(parts, axis=0).astype(BF16)
-    for c in range(2 * cols):
-        price_ref[c : c + 1, :] = price[:, c * BLOCK : (c + 1) * BLOCK]
     lhs_t_ref[...] = lhs_ref[...].T
     flags = in_order(w, own_flags(own_ref, cols, rows), own_flags(side_ref, cols, rows))
     extra_ref[...] = extra_rows(flags, logs_ref[...])
@@ -184,8 +180,9 @@
     factors = [pacing_ref[pl.ds(m ^ k, 1), :] for k in keys]
     for c in range(part_ref.shape[0]):
         total = jnp.zeros((BLOCK, BLOCK), F32)
-        for (ref, at), factor in zip(tiles(gains, c), factors):
-            total = total + ref[at] * factor
+        paced = [ref[at] * factor for (ref, at), factor in zip(tiles(gains, c), factors)]
+        for one, two in zip(paced[::2], paced[1::2]):
+            total = total + (one + two)
         part_ref[c : c + 1, :] = jnp.sum(total.T, axis=0, keepdims=True)
 
 

time: 42.4 us -> 42.3 us (level)
  no operation moved by 1% of the time
where the time goes in v6:
time: 42.3 us; the launch traced here: 42.2 us
  starting transfers between devices  21.8 us (52%)
  waiting for transfers between devices  10.7 us (25%)
  Pallas kernels  8.34 us (20%)
  between operations  0.72 us (2%)
  local copies, waits for them, and re-layouts  0.58 us (1%)
    ppermute x18, starting transfers between devices, swap(): lax.ppermute(x, axis, [(i, i ^ k) for i in range(lax.axis_size(axis))])  21.8 us
    ppermute x18, waiting for transfers between devices, swap(): lax.ppermute(x, axis, [(i, i ^ k) for i in range(lax.axis_size(axis))])  10.7 us
    pallas_call x9, Pallas kernels, call(): pl.pallas_call(kernel, out_shape=out, in_specs=[VMEM] * len(operands), ou...  4.98 us
    pallas_call x1, Pallas kernels, staged(): pl.pallas_call(lambda *refs: final_kernel(keys, advs, *refs), out_shape=(...  2.29 us
    pallas_call x1, Pallas kernels, staged(): pl.pallas_call(lambda *refs: prepare_kernel(ratio, imps, *refs), out_shap...  1.07 us
  transfers between devices with their start and end apart: 18, of which 11 were waited for; matrix products, arithmetic and copies ran while one was open for 1% of the time, Pallas kernels for 10%

profile of v6, /device:TPU:0, one launch (start us, length us, event | category | flops | bytes accessed | tf_op | source)
XLA Modules:
  0.0 42.2 jit_solution(8919163128075083591)
XLA Ops:
  0.6 4.1 %collective-permute-start.5 = (f32[64,128]{1,0:T(8,128)}, f32[64,128]{1,0:T(8,128)S(1)}, u32[]{:S(2)}, u32[]{:S(2)}) collective-permute-start(f32[64,128]{1,0:T(8,128)} %bitcast.14), channel_id=1, source_target_pairs={{0,8},{1,9},{2,10},{3,11},{4,12},{5,13},{6,14},{7,15},{8,0},{9,1},... | collective-permute-start | bytes 98312 | tf_op jit(solution)/shard_map/ppermute | solution.py:236
  4.7 1.3 %collective-permute-start.4 = (f32[64,128]{1,0:T(8,128)}, f32[64,128]{1,0:T(8,128)S(1)}, u32[]{:S(2)}, u32[]{:S(2)}) collective-permute-start(f32[64,128]{1,0:T(8,128)} %bitcast.15), channel_id=1, source_target_pairs={{0,12},{1,13},{2,14},{3,15},{4,8},{5,9},{6,10},{7,11},{8,4},{9,5},... | collective-permute-start | bytes 98312 | tf_op jit(solution)/shard_map/ppermute | solution.py:236
  6.1 0.2 collective-permute-start.3
  6.3 1.1 %shard_map.76 = (f32[72,256]{1,0:T(8,128)S(1)}, f32[16,128]{1,0:T(8,128)S(1)}, f32[16,128]{1,0:T(8,128)S(1)}, f32[64,128]{1,0:T(8,128)S(1)}) custom-call(s32[4,16]{1,0:T(4,128)} %bitcast.23, s32[16,128]{1,0:T(8,128)} %bitcast.21, f32[16,128]{1,0:T(8,128)} %bitcast.22, f32[64,256]{1,0:T(8,128)} %bitcast.13, f32[64,128]{1,0:T(8,128)} %bitcast.17), custom_call_target="tpu_custom_call" | custom-call | tf_op jit(solution)/shard_map/pallas_call | solution.py:272
  7.4 2.8 %collective-permute-start.2 = (f32[72,256]{1,0:T(8,128)S(1)}, f32[72,256]{1,0:T(8,128)S(1)}, u32[]{:S(2)}, u32[]{:S(2)}) collective-permute-start(f32[72,256]{1,0:T(8,128)S(1)} %get-tuple-element.39.refs_0_), channel_id=1, source_target_pairs={{0,20},{1,21},{2,22},{3,23},{4,16},{5,17},{6,18},{7,19},{8,28},{9,... | collective-permute-start | bytes 221192 | tf_op jit(solution)/shard_map/ppermute | solution.py:236
  10.2 0.2 collective-permute-start.1
  10.4 0.0 collective-permute-done.5
  10.4 0.5 %collective-permute-start = (f32[72,256]{1,0:T(8,128)S(1)}, f32[72,256]{1,0:T(8,128)S(1)}, u32[]{:S(2)}, u32[]{:S(2)}) collective-permute-start(f32[72,256]{1,0:T(8,128)S(1)} %get-tuple-element.39.refs_0_), channel_id=1, source_target_pairs={{0,16},{1,17},{2,18},{3,19},{4,20},{5,21},{6,22},{7,23},{8,24},{9,... | collective-permute-start | bytes 221192 | tf_op jit(solution)/shard_map/ppermute | solution.py:236
  10.9 0.0 collective-permute-done.4
  11.0 0.0 collective-permute-done.3
  11.0 1.6 %collective-permute-start.7 = (f32[4,64,128]{2,1,0:T(8,128)S(1)}, f32[4,64,128]{2,1,0:T(8,128)S(1)}, u32[]{:S(2)}, u32[]{:S(2)}) collective-permute-start(f32[4,64,128]{2,1,0:T(8,128)S(1)} %pad_maximum_fusion.refs_0_), channel_id=1, source_target_pairs={{0,2},{1,3},{2,0},{3,1},{4,6},{5,7},{6,4},{7,5},{8,10},{9,11},{10,... | collective-permute-start | bytes 393224 | tf_op jit(solution)/shard_map/ppermute | solution.py:236
  12.5 0.8 %collective-permute-done.2.refs_3_ = f32[72,256]{1,0:T(8,128)S(1)} collective-permute-done((f32[72,256]{1,0:T(8,128)S(1)}, f32[72,256]{1,0:T(8,128)S(1)}, u32[]{:S(2)}, u32[]{:S(2)}) %collective-permute-start.2) | collective-permute-done | bytes 73760 | tf_op jit(solution)/shard_map/ppermute | solution.py:236
  13.3 1.2 %collective-permute-done.1.refs_2_ = f32[72,256]{1,0:T(8,128)S(1)} collective-permute-done((f32[72,256]{1,0:T(8,128)S(1)}, f32[72,256]{1,0:T(8,128)S(1)}, u32[]{:S(2)}, u32[]{:S(2)}) %collective-permute-start.1) | collective-permute-done | bytes 73760 | tf_op jit(solution)/shard_map/ppermute | solution.py:236
  14.6 0.2 collective-permute-done.refs_1_
  14.8 0.0 collective-permute-start.6
  14.8 0.3 shard_map.77
  15.1 0.5 %shard_map.78 = (f32[1024,512]{1,0:T(8,128)S(1)}, f32[16,128]{1,0:T(8,128)S(1)}, bf16[208,512]{1,0:T(8,128)(2,1)S(1)}) custom-call(f32[4,64,128]{2,1,0:T(8,128)S(1)} %pad_maximum_fusion.refs_0_, bf16[16,2048]{1,0:T(8,128)(2,1)S(1)} %get-tuple-element.43.refs_1_, bf16[1024,208]{1,0:T(8,128)(2,1)S(1)} %get-tuple-element.44.refs_2_), custom_call_target="tpu_custom_call" | custom-call | flops 400000000 | bytes 1562500 | tf_op jit(solution)/shard_map/pallas_call | solution.py:259
  15.6 0.4 %collective-permute-done.7.refs_0_ = f32[4,64,128]{2,1,0:T(8,128)S(1)} collective-permute-done((f32[4,64,128]{2,1,0:T(8,128)S(1)}, f32[4,64,128]{2,1,0:T(8,128)S(1)}, u32[]{:S(2)}, u32[]{:S(2)}) %collective-permute-start.7) | collective-permute-done | bytes 131104 | tf_op jit(solution)/shard_map/ppermute | solution.py:236
  16.0 0.2 collective-permute-start.8
  16.2 0.0 collective-permute-done.6.refs_0_
  16.2 0.5 %shard_map.79 = (f32[1024,512]{1,0:T(8,128)S(1)}, f32[16,128]{1,0:T(8,128)S(1)}, bf16[208,512]{1,0:T(8,128)(2,1)S(1)}) custom-call(f32[4,64,128]{2,1,0:T(8,128)S(1)} %collective-permute-done.6.refs_0_, bf16[16,2048]{1,0:T(8,128)(2,1)S(1)} %get-tuple-element.43.refs_1_, bf16[1024,208]{1,0:T(8,128)(2,1)S(1)} %get-tuple-element.44.refs_2_, ...), custom_call_target="tpu_custom_call" | custom-call | flops 400000000 | bytes 1562500 | tf_op jit(solution)/shard_map/pallas_call | solution.py:259
  16.6 0.5 %shard_map.80 = (f32[1024,512]{1,0:T(8,128)S(1)}, f32[16,128]{1,0:T(8,128)S(1)}, bf16[208,512]{1,0:T(8,128)(2,1)S(1)}) custom-call(f32[4,64,128]{2,1,0:T(8,128)S(1)} %collective-permute-done.7.refs_0_, bf16[16,2048]{1,0:T(8,128)(2,1)S(1)} %get-tuple-element.43.refs_1_, bf16[1024,208]{1,0:T(8,128)(2,1)S(1)} %get-tuple-element.44.refs_2_, ...), custom_call_target="tpu_custom_call" | custom-call | flops 400000000 | bytes 1562500 | tf_op jit(solution)/shard_map/pallas_call | solution.py:259
  17.1 0.3 collective-permute-done.8.refs_0_
  17.4 0.5 %shard_map.81 = (f32[1024,512]{1,0:T(8,128)S(1)}, f32[16,128]{1,0:T(8,128)S(1)}, bf16[208,512]{1,0:T(8,128)(2,1)S(1)}) custom-call(f32[4,64,128]{2,1,0:T(8,128)S(1)} %collective-permute-done.8.refs_0_, bf16[16,2048]{1,0:T(8,128)(2,1)S(1)} %get-tuple-element.43.refs_1_, bf16[1024,208]{1,0:T(8,128)(2,1)S(1)} %get-tuple-element.44.refs_2_, ...), custom_call_target="tpu_custom_call" | custom-call | flops 400000000 | bytes 1562500 | tf_op jit(solution)/shard_map/pallas_call | solution.py:259
  17.8 2.9 %collective-permute-start.9 = (f32[16,128]{1,0:T(8,128)S(1)}, f32[16,128]{1,0:T(8,128)S(1)}, u32[]{:S(2)}, u32[]{:S(2)}) collective-permute-start(f32[16,128]{1,0:T(8,128)S(1)} %get-tuple-element.61), channel_id=1, source_target_pairs={{0,8},{1,9},{2,10},{3,11},{4,12},{5,13},{6,14},{7,15},{8,0},{9,1},... | collective-permute-start | bytes 24584 | tf_op jit(solution)/shard_map/ppermute | solution.py:236
  20.7 1.7 %collective-permute-done.9 = f32[16,128]{1,0:T(8,128)S(1)} collective-permute-done((f32[16,128]{1,0:T(8,128)S(1)}, f32[16,128]{1,0:T(8,128)S(1)}, u32[]{:S(2)}, u32[]{:S(2)}) %collective-permute-start.9) | collective-permute-done | bytes 8224 | tf_op jit(solution)/shard_map/ppermute | solution.py:236
  22.4 0.3 collective-permute-start.12
  22.7 1.2 %collective-permute-start.11 = (f32[16,128]{1,0:T(8,128)S(1)}, f32[16,128]{1,0:T(8,128)S(1)}, u32[]{:S(2)}, u32[]{:S(2)}) collective-permute-start(f32[16,128]{1,0:T(8,128)S(1)} %add.6.refs_5_), channel_id=1, source_target_pairs={{0,2},{1,3},{2,0},{3,1},{4,6},{5,7},{6,4},{7,5},{8,10},{9,11},{10,... | collective-permute-start | bytes 24584 | tf_op jit(solution)/shard_map/ppermute | solution.py:236
  24.0 0.3 collective-permute-start.10
  24.3 1.3 %collective-permute-done.12.refs_8_ = f32[16,128]{1,0:T(8,128)S(1)} collective-permute-done((f32[16,128]{1,0:T(8,128)S(1)}, f32[16,128]{1,0:T(8,128)S(1)}, u32[]{:S(2)}, u32[]{:S(2)}) %collective-permute-start.12) | collective-permute-done | bytes 8224 | tf_op jit(solution)/shard_map/ppermute | solution.py:236
  25.6 0.8 %collective-permute-done.11.refs_7_ = f32[16,128]{1,0:T(8,128)S(1)} collective-permute-done((f32[16,128]{1,0:T(8,128)S(1)}, f32[16,128]{1,0:T(8,128)S(1)}, u32[]{:S(2)}, u32[]{:S(2)}) %collective-permute-start.11) | collective-permute-done | bytes 8224 | tf_op jit(solution)/shard_map/ppermute | solution.py:236
  26.4 0.0 collective-permute-done.10.refs_6_
  26.4 0.8 %shard_map.83 = (f32[8,128]{1,0:T(8,128)S(1)}, f32[16,128]{1,0:T(8,128)S(1)}) custom-call(f32[16,128]{1,0:T(8,128)S(1)} %get-tuple-element.56.refs_0_.refs_1_, f32[1024,512]{1,0:T(8,128)S(1)} %get-tuple-element.57.refs_1_.refs_0_, f32[1024,512]{1,0:T(8,128)S(1)} %get-tuple-element.58.refs_2_.refs_1_, f32[1024,512]{1,0:T(8,128)S(1)} %get-tuple-element.59.refs_3_.refs_2_, ...), custom_call_target="tpu_custom_call" | custom-call | tf_op jit(solution)/shard_map/pallas_call | solution.py:259
  27.1 1.6 %collective-permute-start.13 = (f32[8,128]{1,0:T(8,128)S(1)}, f32[8,128]{1,0:T(8,128)S(1)}, u32[]{:S(2)}, u32[]{:S(2)}) collective-permute-start(f32[8,128]{1,0:T(8,128)S(1)} %get-tuple-element.68.refs_7_), channel_id=1, source_target_pairs={{0,16},{16,0},{1,17},{17,1},{2,18},{18,2},{3,19},{19,3},{4,20},{20... | collective-permute-start | bytes 12296 | tf_op jit(solution)/shard_map/ppermute | solution.py:236
  28.7 0.5 %shard_map.84 = (f32[1024,512]{1,0:T(8,128)S(1)}, f32[1024,512]{1,0:T(8,128)S(1)}, f32[1024,512]{1,0:T(8,128)S(1)}, f32[1024,512]{1,0:T(8,128)S(1)}) custom-call(f32[1024,512]{1,0:T(8,128)S(1)} %get-tuple-element.57.refs_1_.refs_0_, f32[1024,512]{1,0:T(8,128)S(1)} %get-tuple-element.58.refs_2_.refs_1_, f32[1024,512]{1,0:T(8,128)S(1)} %get-tuple-element.59.refs_3_.refs_2_, ...), custom_call_target="tpu_custom_call" | custom-call | flops 1000000000 | bytes 3906250 | tf_op jit(solution)/shard_map/pallas_call | solution.py:259
  29.3 1.6 %collective-permute-done.13.refs_8_ = f32[8,128]{1,0:T(8,128)S(1)} collective-permute-done((f32[8,128]{1,0:T(8,128)S(1)}, f32[8,128]{1,0:T(8,128)S(1)}, u32[]{:S(2)}, u32[]{:S(2)}) %collective-permute-start.13) | collective-permute-done | bytes 4128 | tf_op jit(solution)/shard_map/ppermute | solution.py:236
  30.8 0.8 %shard_map.85 = (f32[16,128]{1,0:T(8,128)S(1)}, f32[4,128]{1,0:T(4,128)S(1)}, f32[16,128]{1,0:T(8,128)S(1)}, f32[1,512]{1,0:T(1,128)S(1)}) custom-call(f32[16,128]{1,0:T(8,128)S(1)} %get-tuple-element.56.refs_0_.refs_1_, f32[16,128]{1,0:T(8,128)S(1)} %get-tuple-element.62.refs_1_, f32[8,128]{1,0:T(8,128)S(1)} %get-tuple-element.63.refs_2_, ...), custom_call_target="tpu_custom_call" | custom-call | tf_op jit(solution)/shard_map/pallas_call | solution.py:259
  31.6 2.7 %collective-permute-start.14 = (f32[16,128]{1,0:T(8,128)S(1)}, f32[16,128]{1,0:T(8,128)S(1)}, u32[]{:S(2)}, u32[]{:S(2)}) collective-permute-start(f32[16,128]{1,0:T(8,128)S(1)} %get-tuple-element.71), channel_id=1, source_target_pairs={{0,8},{1,9},{2,10},{3,11},{4,12},{5,13},{6,14},{7,15},{8,0},{9,1},... | collective-permute-start | bytes 24584 | tf_op jit(solution)/shard_map/ppermute | solution.py:236
  34.3 1.9 %collective-permute-done.14 = f32[16,128]{1,0:T(8,128)S(1)} collective-permute-done((f32[16,128]{1,0:T(8,128)S(1)}, f32[16,128]{1,0:T(8,128)S(1)}, u32[]{:S(2)}, u32[]{:S(2)}) %collective-permute-start.14) | collective-permute-done | bytes 8224 | tf_op jit(solution)/shard_map/ppermute | solution.py:236
  36.2 0.0 collective-permute-start.17
  36.2 1.3 %collective-permute-start.16 = (f32[16,128]{1,0:T(8,128)S(1)}, f32[16,128]{1,0:T(8,128)S(1)}, u32[]{:S(2)}, u32[]{:S(2)}) collective-permute-start(f32[16,128]{1,0:T(8,128)S(1)} %add.7.refs_4_), channel_id=1, source_target_pairs={{0,2},{1,3},{2,0},{3,1},{4,6},{5,7},{6,4},{7,5},{8,10},{9,11},{10,... | collective-permute-start | bytes 24584 | tf_op jit(solution)/shard_map/ppermute | solution.py:236
  37.5 0.6 %collective-permute-start.15 = (f32[16,128]{1,0:T(8,128)S(1)}, f32[16,128]{1,0:T(8,128)S(1)}, u32[]{:S(2)}, u32[]{:S(2)}) collective-permute-start(f32[16,128]{1,0:T(8,128)S(1)} %add.7.refs_4_), channel_id=1, source_target_pairs={{0,1},{1,0},{2,3},{3,2},{4,5},{5,4},{6,7},{7,6},{8,9},{9,8},{10,11... | collective-permute-start | bytes 24584 | tf_op jit(solution)/shard_map/ppermute | solution.py:236
  38.0 0.8 %shard_map.82.refs_0_ = f32[2048,512]{1,0:T(8,128)S(1)} custom-call(bf16[208,1024]{1,0:T(8,128)(2,1)S(1)} %get-tuple-element.41.lhs_ref, bf16[208,512]{1,0:T(8,128)(2,1)S(1)} %get-tuple-element.45.refs_0_, bf16[208,512]{1,0:T(8,128)(2,1)S(1)} %get-tuple-element.50.refs_1_, bf16[208,512]{1,0:T(8,128)(2,1)S(1)} %get-tuple-element.53.refs_2_, ...), custom_call_target="tpu_custom_call" | custom-call | flops 1000000000 | bytes 3906250 | tf_op jit(solution)/shard_map/pallas_call | solution.py:259
  38.8 0.6 %copy.8 = f32[512]{0:T(512)} copy(f32[512]{0:T(512)S(1)} %bitcast.11) | data formatting | bytes 4096
  39.4 0.0 collective-permute-done.17.refs_7_
  39.4 0.4 %collective-permute-done.16.refs_6_ = f32[16,128]{1,0:T(8,128)S(1)} collective-permute-done((f32[16,128]{1,0:T(8,128)S(1)}, f32[16,128]{1,0:T(8,128)S(1)}, u32[]{:S(2)}, u32[]{:S(2)}) %collective-permute-start.16) | collective-permute-done | bytes 8224 | tf_op jit(solution)/shard_map/ppermute | solution.py:236
  39.9 0.0 collective-permute-done.15.refs_5_
  39.9 2.3 %shard_map.86 = (f32[2048,512]{1,0:T(8,128)}, f32[16,128]{1,0:T(8,128)}) custom-call(f32[2048,512]{1,0:T(8,128)S(1)} %shard_map.82.refs_0_, f32[16,128]{1,0:T(8,128)S(1)} %get-tuple-element.56.refs_0_.refs_1_, f32[16,128]{1,0:T(8,128)S(1)} %get-tuple-element.69.refs_2_, f32[1,512]{1,0:T(1,128)S(1)} %get-tuple-element.70.refs_3_, f32[16,128]{1,0:T(8,128)S(1)} %add.7.refs_4_, ...), custom_call_target="tpu_custom_call" | custom-call | tf_op jit(solution)/shard_map/pallas_call | solution.py:351
  (3 shorter events, 0.0 us)
Async XLA Ops:
  0.6 9.8 %collective-permute-start.5 = (f32[64,128]{1,0:T(8,128)}, f32[64,128]{1,0:T(8,128)S(1)}, u32[]{:S(2)}, u32[]{:S(2)}) collective-permute-start(f32[64,128]{1,0:T(8,128)} %bitcast.14), channel_id=1, source_target_pairs={{0,8},{1,9},{2,10},{3,11},{4,12},{5,13},{6,14},{7,15},{8,0},{9,1},... | collective-permute-start | bytes 98312 | tf_op jit(solution)/shard_map/ppermute | solution.py:236
  4.7 6.2 %collective-permute-start.4 = (f32[64,128]{1,0:T(8,128)}, f32[64,128]{1,0:T(8,128)S(1)}, u32[]{:S(2)}, u32[]{:S(2)}) collective-permute-start(f32[64,128]{1,0:T(8,128)} %bitcast.15), channel_id=1, source_target_pairs={{0,12},{1,13},{2,14},{3,15},{4,8},{5,9},{6,10},{7,11},{8,4},{9,5},... | collective-permute-start | bytes 98312 | tf_op jit(solution)/shard_map/ppermute | solution.py:236
  6.1 4.9 %collective-permute-start.3 = (f32[64,128]{1,0:T(8,128)}, f32[64,128]{1,0:T(8,128)S(1)}, u32[]{:S(2)}, u32[]{:S(2)}) collective-permute-start(f32[64,128]{1,0:T(8,128)} %bitcast.16), channel_id=1, source_target_pairs={{0,4},{1,5},{2,6},{3,7},{4,0},{5,1},{6,2},{7,3},{8,12},{9,13},{10,... | collective-permute-start | bytes 98312 | tf_op jit(solution)/shard_map/ppermute | solution.py:236
  7.4 5.9 %collective-permute-start.2 = (f32[72,256]{1,0:T(8,128)S(1)}, f32[72,256]{1,0:T(8,128)S(1)}, u32[]{:S(2)}, u32[]{:S(2)}) collective-permute-start(f32[72,256]{1,0:T(8,128)S(1)} %get-tuple-element.39.refs_0_), channel_id=1, source_target_pairs={{0,20},{1,21},{2,22},{3,23},{4,16},{5,17},{6,18},{7,19},{8,28},{9,... | collective-permute-start | bytes 221192 | tf_op jit(solution)/shard_map/ppermute | solution.py:236
  10.2 4.4 %collective-permute-start.1 = (f32[72,256]{1,0:T(8,128)S(1)}, f32[72,256]{1,0:T(8,128)S(1)}, u32[]{:S(2)}, u32[]{:S(2)}) collective-permute-start(f32[72,256]{1,0:T(8,128)S(1)} %get-tuple-element.39.refs_0_), channel_id=1, source_target_pairs={{0,4},{1,5},{2,6},{3,7},{4,0},{5,1},{6,2},{7,3},{8,12},{9,13},{10,... | collective-permute-start | bytes 221192 | tf_op jit(solution)/shard_map/ppermute | solution.py:236
  10.4 4.4 %collective-permute-start = (f32[72,256]{1,0:T(8,128)S(1)}, f32[72,256]{1,0:T(8,128)S(1)}, u32[]{:S(2)}, u32[]{:S(2)}) collective-permute-start(f32[72,256]{1,0:T(8,128)S(1)} %get-tuple-element.39.refs_0_), channel_id=1, source_target_pairs={{0,16},{1,17},{2,18},{3,19},{4,20},{5,21},{6,22},{7,23},{8,24},{9,... | collective-permute-start | bytes 221192 | tf_op jit(solution)/shard_map/ppermute | solution.py:236
  11.0 5.0 %collective-permute-start.7 = (f32[4,64,128]{2,1,0:T(8,128)S(1)}, f32[4,64,128]{2,1,0:T(8,128)S(1)}, u32[]{:S(2)}, u32[]{:S(2)}) collective-permute-start(f32[4,64,128]{2,1,0:T(8,128)S(1)} %pad_maximum_fusion.refs_0_), channel_id=1, source_target_pairs={{0,2},{1,3},{2,0},{3,1},{4,6},{5,7},{6,4},{7,5},{8,10},{9,11},{10,... | collective-permute-start | bytes 393224 | tf_op jit(solution)/shard_map/ppermute | solution.py:236
  14.8 1.4 %collective-permute-start.6 = (f32[4,64,128]{2,1,0:T(8,128)S(1)}, f32[4,64,128]{2,1,0:T(8,128)S(1)}, u32[]{:S(2)}, u32[]{:S(2)}) collective-permute-start(f32[4,64,128]{2,1,0:T(8,128)S(1)} %pad_maximum_fusion.refs_0_), channel_id=1, source_target_pairs={{0,1},{1,0},{2,3},{3,2},{4,5},{5,4},{6,7},{7,6},{8,9},{9,8},{10,11... | collective-permute-start | bytes 393224 | tf_op jit(solution)/shard_map/ppermute | solution.py:236
  16.0 1.3 %collective-permute-start.8 = (f32[4,64,128]{2,1,0:T(8,128)S(1)}, f32[4,64,128]{2,1,0:T(8,128)S(1)}, u32[]{:S(2)}, u32[]{:S(2)}) collective-permute-start(f32[4,64,128]{2,1,0:T(8,128)S(1)} %collective-permute-done.7.refs_0_), channel_id=1, source_target_pairs={{0,1},{1,0},{2,3},{3,2},{4,5},{5,4},{6,7},{7,6},{8,9},{9,8},{10,11... | collective-permute-start | bytes 393224 | tf_op jit(solution)/shard_map/ppermute | solution.py:236
  17.8 4.6 %collective-permute-start.9 = (f32[16,128]{1,0:T(8,128)S(1)}, f32[16,128]{1,0:T(8,128)S(1)}, u32[]{:S(2)}, u32[]{:S(2)}) collective-permute-start(f32[16,128]{1,0:T(8,128)S(1)} %get-tuple-element.61), channel_id=1, source_target_pairs={{0,8},{1,9},{2,10},{3,11},{4,12},{5,13},{6,14},{7,15},{8,0},{9,1},... | collective-permute-start | bytes 24584 | tf_op jit(solution)/shard_map/ppermute | solution.py:236
  22.4 3.1 %collective-permute-start.12 = (f32[16,128]{1,0:T(8,128)S(1)}, f32[16,128]{1,0:T(8,128)S(1)}, u32[]{:S(2)}, u32[]{:S(2)}) collective-permute-start(f32[16,128]{1,0:T(8,128)S(1)} %add.6.refs_5_), channel_id=1, source_target_pairs={{0,3},{1,2},{2,1},{3,0},{4,7},{5,6},{6,5},{7,4},{8,11},{9,10},{10,... | collective-permute-start | bytes 24584 | tf_op jit(solution)/shard_map/ppermute | solution.py:236
  22.7 3.7 %collective-permute-start.11 = (f32[16,128]{1,0:T(8,128)S(1)}, f32[16,128]{1,0:T(8,128)S(1)}, u32[]{:S(2)}, u32[]{:S(2)}) collective-permute-start(f32[16,128]{1,0:T(8,128)S(1)} %add.6.refs_5_), channel_id=1, source_target_pairs={{0,2},{1,3},{2,0},{3,1},{4,6},{5,7},{6,4},{7,5},{8,10},{9,11},{10,... | collective-permute-start | bytes 24584 | tf_op jit(solution)/shard_map/ppermute | solution.py:236
  24.0 2.4 %collective-permute-start.10 = (f32[16,128]{1,0:T(8,128)S(1)}, f32[16,128]{1,0:T(8,128)S(1)}, u32[]{:S(2)}, u32[]{:S(2)}) collective-permute-start(f32[16,128]{1,0:T(8,128)S(1)} %add.6.refs_5_), channel_id=1, source_target_pairs={{0,1},{1,0},{2,3},{3,2},{4,5},{5,4},{6,7},{7,6},{8,9},{9,8},{10,11... | collective-permute-start | bytes 24584 | tf_op jit(solution)/shard_map/ppermute | solution.py:236
  27.1 3.7 %collective-permute-start.13 = (f32[8,128]{1,0:T(8,128)S(1)}, f32[8,128]{1,0:T(8,128)S(1)}, u32[]{:S(2)}, u32[]{:S(2)}) collective-permute-start(f32[8,128]{1,0:T(8,128)S(1)} %get-tuple-element.68.refs_7_), channel_id=1, source_target_pairs={{0,16},{16,0},{1,17},{17,1},{2,18},{18,2},{3,19},{19,3},{4,20},{20... | collective-permute-start | bytes 12296 | tf_op jit(solution)/shard_map/ppermute | solution.py:236
  31.6 4.6 %collective-permute-start.14 = (f32[16,128]{1,0:T(8,128)S(1)}, f32[16,128]{1,0:T(8,128)S(1)}, u32[]{:S(2)}, u32[]{:S(2)}) collective-permute-start(f32[16,128]{1,0:T(8,128)S(1)} %get-tuple-element.71), channel_id=1, source_target_pairs={{0,8},{1,9},{2,10},{3,11},{4,12},{5,13},{6,14},{7,15},{8,0},{9,1},... | collective-permute-start | bytes 24584 | tf_op jit(solution)/shard_map/ppermute | solution.py:236
  36.2 3.2 %collective-permute-start.17 = (f32[16,128]{1,0:T(8,128)S(1)}, f32[16,128]{1,0:T(8,128)S(1)}, u32[]{:S(2)}, u32[]{:S(2)}) collective-permute-start(f32[16,128]{1,0:T(8,128)S(1)} %add.7.refs_4_), channel_id=1, source_target_pairs={{0,3},{1,2},{2,1},{3,0},{4,7},{5,6},{6,5},{7,4},{8,11},{9,10},{10,... | collective-permute-start | bytes 24584 | tf_op jit(solution)/shard_map/ppermute | solution.py:236
  36.2 3.7 %collective-permute-start.16 = (f32[16,128]{1,0:T(8,128)S(1)}, f32[16,128]{1,0:T(8,128)S(1)}, u32[]{:S(2)}, u32[]{:S(2)}) collective-permute-start(f32[16,128]{1,0:T(8,128)S(1)} %add.7.refs_4_), channel_id=1, source_target_pairs={{0,2},{1,3},{2,0},{3,1},{4,6},{5,7},{6,4},{7,5},{8,10},{9,11},{10,... | collective-permute-start | bytes 24584 | tf_op jit(solution)/shard_map/ppermute | solution.py:236
  37.5 2.4 %collective-permute-start.15 = (f32[16,128]{1,0:T(8,128)S(1)}, f32[16,128]{1,0:T(8,128)S(1)}, u32[]{:S(2)}, u32[]{:S(2)}) collective-permute-start(f32[16,128]{1,0:T(8,128)S(1)} %add.7.refs_4_), channel_id=1, source_target_pairs={{0,1},{1,0},{2,3},{3,2},{4,5},{5,4},{6,7},{7,6},{8,9},{9,8},{10,11... | collective-permute-start | bytes 24584 | tf_op jit(solution)/shard_map/ppermute | solution.py:236

commit v7 on v6

--- a/solution.py
+++ b/solution.py
@@ -52,7 +52,7 @@
 
 def prepare_kernel(
     ratio, imps, elig_hbm, class_hbm, scale_hbm, imp_hbm, adv_hbm,
-    pack_ref, logs_ref, limit_ref, own_ref, elig_ref, class_ref, scale_ref, sems,
+    pack_ref, class_ref, scale_ref, own_ref, elig_ref, sems,
 ):
     moves = (
         (elig_hbm, elig_ref),
@@ -67,10 +67,7 @@
     pack_ref[EMB : EMB + 8, :] = jnp.zeros((8, pack_ref.shape[1]), F32)
     for copy in copies:
         copy.wait()
-    exponent = 0.3 * class_ref[...].astype(F32) - 1.2
-    limit = ratio * jnp.exp(exponent)
-    limit_ref[...] = limit
-    logs_ref[...] = jnp.log(scale_ref[...]) * LOG2E + (exponent * LOG2E + math.log2(ratio / imps))
+    limit = ratio * jnp.exp(0.3 * class_ref[...].astype(F32) - 1.2)
     rows, cols = class_ref.shape[0], elig_ref.shape[0]
     flags = elig_ref[...].astype(F32)
     allowance = limit / imps
@@ -95,7 +92,10 @@
     return jnp.concatenate(parts, axis=0).astype(BF16)
 
 
-def impressions_kernel(cols, rows, own_ref, down_ref, side_ref, cross_ref, logs_ref, lhs_ref, lhs_t_ref, extra_ref, price_ref):
+def impressions_kernel(
+    cols, rows, ratio, imps, own_ref, down_ref, side_ref, cross_ref, class_ref, scale_ref,
+    lhs_ref, lhs_t_ref, extra_ref, price_ref, limit_ref,
+):
     _, w = home()
     half = lax.axis_index("adv")
     width = own_ref.shape[1]
@@ -118,7 +118,10 @@
     lhs_ref[3 * EMB :, :] = jnp.concatenate(parts, axis=0).astype(BF16)
     lhs_t_ref[...] = lhs_ref[...].T
     flags = in_order(w, own_flags(own_ref, cols, rows), own_flags(side_ref, cols, rows))
-    extra_ref[...] = extra_rows(flags, logs_ref[...])
+    exponent = 0.3 * class_ref[...].astype(F32) - 1.2
+    limit_ref[...] = ratio * jnp.exp(exponent)
+    logs = jnp.log(scale_ref[...]) * LOG2E + (exponent * LOG2E + math.log2(ratio / imps))
+    extra_ref[...] = extra_rows(flags, logs)
 
 
 def first_kernel(keys, adv_ref, extra_ref, lhs_t_ref, *refs):
@@ -149,17 +152,23 @@
             sums_ref[pl.ds(m ^ keys[n + p], 1), :] = sums[:, p * BLOCK : (p + 1) * BLOCK]
 
 
-def rows_kernel(lhs_ref, *refs):
-    *rhs_refs, gain_ref = refs
-    _, w = home()
-    width = gain_ref.shape[1]
+def as_column(row):
+    shape = (BLOCK, BLOCK)
+    diagonal = lax.broadcasted_iota(jnp.int32, shape, 0) == lax.broadcasted_iota(jnp.int32, shape, 1)
+    return jnp.sum(jnp.where(diagonal, row, 0.0), axis=1, keepdims=True)
+
+
+def rows_kernel(keys, advs, lhs_ref, factor_ref, change_ref, *refs):
+    *rhs_refs, out_ref = refs
+    m, w = home()
+    width = out_ref.shape[1]
     lhs = lhs_ref[:, pl.ds(pl.multiple_of(w * width, width), width)]
-    at = 0
-    for ref in rhs_refs:
-        for lane in range(0, ref.shape[1], BLOCK):
-            rhs = ref[:, lane : lane + BLOCK].T
-            gain_ref[at : at + BLOCK, :] = jnp.exp2(jnp.dot(rhs, lhs, preferred_element_type=F32))
-            at += BLOCK
+    change = change_ref[...]
+    blocks = [(ref, lane) for ref in rhs_refs for lane in range(0, ref.shape[1], BLOCK)]
+    for n, (ref, lane) in enumerate(blocks):
+        gain = jnp.exp2(jnp.dot(ref[:, lane : lane + BLOCK].T, lhs, preferred_element_type=F32))
+        factor = as_column(factor_ref[pl.ds(m ^ keys[n], 1), :] * advs)
+        out_ref[n * BLOCK : (n + 1) * BLOCK, :] = (gain * factor) * (gain * change)
 
 
 def tiles(refs, c):
@@ -207,27 +216,20 @@
     sums_ref[...] = sums_ref[...] * (factor_ref[...] / SMALL**2)
 
 
-def final_kernel(keys, advs, gain_ref, limit_ref, factor_ref, change_ref, *refs):
-    *sum_refs, out_ref, pacing_out, pacing_ref, scale_ref, block_ref, sems = refs
+def final_kernel(keys, gain_ref, limit_ref, *refs):
+    *sum_refs, out_ref, pacing_out, pacing_ref, block_ref, sems = refs
     m, _ = home()
     limit = limit_ref[...]
-    pacing = limit / jnp.maximum(tree([ref[...] for ref in sum_refs]), limit)
-    scale_ref[...] = pacing * factor_ref[...] * advs
-    pacing_ref[...] = pacing
-    copies = [pltpu.make_async_copy(pacing_ref, pacing_out, sems.at[len(keys)])]
-    copies[0].start()
-    change = change_ref[...]
-    shape = (BLOCK, BLOCK)
-    diagonal = lax.broadcasted_iota(jnp.int32, shape, 0) == lax.broadcasted_iota(jnp.int32, shape, 1)
+    pacing_ref[...] = limit / jnp.maximum(tree([ref[...] for ref in sum_refs]), limit)
+    copies = []
     for n, k in enumerate(keys):
         rows = slice(n * BLOCK, (n + 1) * BLOCK)
-        scale = jnp.sum(jnp.where(diagonal, scale_ref[pl.ds(m ^ k, 1), :], 0.0), axis=1, keepdims=True)
-        gain = gain_ref[rows, :]
-        block_ref[rows, :] = (gain * scale) * (gain * change)
+        block_ref[rows, :] = gain_ref[rows, :] * as_column(pacing_ref[pl.ds(m ^ k, 1), :])
         to = pl.ds(pl.multiple_of((m ^ k) * BLOCK, BLOCK), BLOCK)
-        copy = pltpu.make_async_copy(block_ref.at[rows], out_ref.at[to], sems.at[n])
-        copy.start()
-        copies.append(copy)
+        copies.append(pltpu.make_async_copy(block_ref.at[rows], out_ref.at[to], sems.at[n]))
+        copies[-1].start()
+    copies.append(pltpu.make_async_copy(pacing_ref, pacing_out, sems.at[len(keys)]))
+    copies[-1].start()
     for copy in copies:
         copy.wait()
 
@@ -269,15 +271,13 @@
     adv_t = adv_embed.T
     ins = (eligible.T, spend_class.reshape(rows, BLOCK), value_scale.reshape(rows, BLOCK), imp_embed.T, adv_t)
     ins = [pltpu.with_memory_space_constraint(x, pltpu.HBM) for x in ins]
-    pack, logs, limit, own = pl.pallas_call(
+    pack, classes, scales, own = pl.pallas_call(
         lambda *refs: prepare_kernel(ratio, imps, *refs),
-        out_shape=(shape(EMB + 8, imp_embed.shape[0]), shape(rows, BLOCK), shape(rows, BLOCK), shape(*adv_t.shape)),
+        out_shape=(shape(EMB + 8, imp_embed.shape[0]), shape(rows, BLOCK, dtype=jnp.int32), shape(rows, BLOCK), shape(*adv_t.shape)),
         in_specs=[HBM] * len(ins),
         out_specs=(VMEM,) * 4,
         scratch_shapes=[
             pltpu.VMEM((cols, rows), jnp.int32),
-            pltpu.VMEM((rows, BLOCK), jnp.int32),
-            pltpu.VMEM((rows, BLOCK), F32),
             pltpu.SemaphoreType.DMA((len(ins),)),
         ],
         compiler_params=PARAMS,
@@ -295,15 +295,16 @@
     keys = at_line + at_line_pair + at_plane + at_plane_pair
 
     count = 2 * imp_count
-    lhs, lhs_t, extra, first_price = call(
-        lambda *refs: impressions_kernel(cols, rows, *refs),
+    lhs, lhs_t, extra, first_price, limit = call(
+        lambda *refs: impressions_kernel(cols, rows, ratio, imps, *refs),
         (
             shape(DEPTH, count, dtype=BF16),
             shape(count, DEPTH, dtype=BF16),
             shape(16, adv_count, dtype=BF16),
             shape(2 * cols, BLOCK),
+            shape(rows, BLOCK),
         ),
-        (pack, down, side, cross, logs),
+        (pack, down, side, cross, classes, scales),
         cost=10**8,
     )
     gains, rhs, sums = [], [], ()
@@ -334,7 +335,6 @@
         cost=10**9,
     )
     terms = over_impressions(sums[0], ((8,),(1,2,3)))
-    (gain_rows,) = call(rows_kernel, (pltpu.VMEM((adv_count, imp_count), F32),), (lhs, *rhs), cost=10**9)
 
     part, pacing = call(
         lambda *refs: prices_kernel(keys, len(gains), *refs),
@@ -348,19 +348,24 @@
     )
 
     terms = over_impressions(sums, ((8,),(1,2,3)))
+    (gain_rows,) = call(
+        lambda *refs: rows_kernel(keys, advs, *refs),
+        (pltpu.VMEM((adv_count, imp_count), F32),),
+        (lhs, factor, change, *rhs),
+        cost=10**9,
+    )
     density, pacing = pl.pallas_call(
-        lambda *refs: final_kernel(keys, advs, *refs),
+        lambda *refs: final_kernel(keys, *refs),
         out_shape=(shape(adv_count, imp_count), shape(rows, BLOCK)),
-        in_specs=[VMEM] * (4 + len(terms)),
+        in_specs=[VMEM] * (2 + len(terms)),
         out_specs=(HBM, HBM),
         scratch_shapes=[
-            pltpu.VMEM((rows, BLOCK), F32),
             pltpu.VMEM((rows, BLOCK), F32),
             pltpu.VMEM((adv_count, imp_count), F32),
             pltpu.SemaphoreType.DMA((rows + 1,)),
         ],
         compiler_params=PARAMS,
-    )(gain_rows, limit, factor, change, *terms)
+    )(gain_rows, limit, *terms)
     return density, prices.reshape(imp_count), pacing.reshape(adv_count)
 
 

time: 42.3 us -> 42.3 us (level)
  no operation moved by 1% of the time
where the time goes in v7:
time: 42.3 us; the launch traced here: 42.1 us
  starting transfers between devices  21.8 us (52%)
  waiting for transfers between devices  10.4 us (25%)
  Pallas kernels  8.61 us (20%)
  between operations  0.72 us (2%)
  local copies, waits for them, and re-layouts  0.58 us (1%)
    ppermute x18, starting transfers between devices, swap(): lax.ppermute(x, axis, [(i, i ^ k) for i in range(lax.axis_size(axis))])  21.8 us
    ppermute x18, waiting for transfers between devices, swap(): lax.ppermute(x, axis, [(i, i ^ k) for i in range(lax.axis_size(axis))])  10.4 us
    pallas_call x9, Pallas kernels, call(): pl.pallas_call(kernel, out_shape=out, in_specs=[VMEM] * len(operands), ou...  5.29 us
    pallas_call x1, Pallas kernels, staged(): pl.pallas_call(lambda *refs: final_kernel(keys, *refs), out_shape=(shape(...  2.26 us
    pallas_call x1, Pallas kernels, staged(): pl.pallas_call(lambda *refs: prepare_kernel(ratio, imps, *refs), out_shap...  1.07 us
  transfers between devices with their start and end apart: 18, of which 11 were waited for; matrix products, arithmetic and copies ran while one was open for 1% of the time, Pallas kernels for 10%

profile of v7, /device:TPU:0, one launch (start us, length us, event | category | flops | bytes accessed | tf_op | source)
XLA Modules:
  0.0 42.1 jit_solution(1392651342362971585)
XLA Ops:
  0.6 4.1 %collective-permute-start.5 = (f32[64,128]{1,0:T(8,128)}, f32[64,128]{1,0:T(8,128)S(1)}, u32[]{:S(2)}, u32[]{:S(2)}) collective-permute-start(f32[64,128]{1,0:T(8,128)} %bitcast.14), channel_id=1, source_target_pairs={{0,8},{1,9},{2,10},{3,11},{4,12},{5,13},{6,14},{7,15},{8,0},{9,1},... | collective-permute-start | bytes 98312 | tf_op jit(solution)/shard_map/ppermute | solution.py:238
  4.7 1.3 %collective-permute-start.4 = (f32[64,128]{1,0:T(8,128)}, f32[64,128]{1,0:T(8,128)S(1)}, u32[]{:S(2)}, u32[]{:S(2)}) collective-permute-start(f32[64,128]{1,0:T(8,128)} %bitcast.15), channel_id=1, source_target_pairs={{0,12},{1,13},{2,14},{3,15},{4,8},{5,9},{6,10},{7,11},{8,4},{9,5},... | collective-permute-start | bytes 98312 | tf_op jit(solution)/shard_map/ppermute | solution.py:238
  6.1 0.2 collective-permute-start.3
  6.3 1.1 %shard_map.76 = (f32[72,256]{1,0:T(8,128)S(1)}, s32[16,128]{1,0:T(8,128)S(1)}, f32[16,128]{1,0:T(8,128)S(1)}, f32[64,128]{1,0:T(8,128)S(1)}) custom-call(s32[4,16]{1,0:T(4,128)} %bitcast.23, s32[16,128]{1,0:T(8,128)} %bitcast.21, f32[16,128]{1,0:T(8,128)} %bitcast.22, f32[64,256]{1,0:T(8,128)} %bitcast.13, f32[64,128]{1,0:T(8,128)} %bitcast.17), custom_call_target="tpu_custom_call" | custom-call | tf_op jit(solution)/shard_map/pallas_call | solution.py:274
  7.4 2.8 %collective-permute-start.2 = (f32[72,256]{1,0:T(8,128)S(1)}, f32[72,256]{1,0:T(8,128)S(1)}, u32[]{:S(2)}, u32[]{:S(2)}) collective-permute-start(f32[72,256]{1,0:T(8,128)S(1)} %get-tuple-element.40.refs_0_), channel_id=1, source_target_pairs={{0,20},{1,21},{2,22},{3,23},{4,16},{5,17},{6,18},{7,19},{8,28},{9,... | collective-permute-start | bytes 221192 | tf_op jit(solution)/shard_map/ppermute | solution.py:238
  10.2 0.2 collective-permute-start.1
  10.4 0.0 collective-permute-done.5
  10.4 0.5 %collective-permute-start = (f32[72,256]{1,0:T(8,128)S(1)}, f32[72,256]{1,0:T(8,128)S(1)}, u32[]{:S(2)}, u32[]{:S(2)}) collective-permute-start(f32[72,256]{1,0:T(8,128)S(1)} %get-tuple-element.40.refs_0_), channel_id=1, source_target_pairs={{0,16},{1,17},{2,18},{3,19},{4,20},{5,21},{6,22},{7,23},{8,24},{9,... | collective-permute-start | bytes 221192 | tf_op jit(solution)/shard_map/ppermute | solution.py:238
  10.9 0.0 collective-permute-done.4
  11.0 0.0 collective-permute-done.3
  11.0 1.6 %collective-permute-start.7 = (f32[4,64,128]{2,1,0:T(8,128)S(1)}, f32[4,64,128]{2,1,0:T(8,128)S(1)}, u32[]{:S(2)}, u32[]{:S(2)}) collective-permute-start(f32[4,64,128]{2,1,0:T(8,128)S(1)} %pad_maximum_fusion.refs_0_), channel_id=1, source_target_pairs={{0,2},{1,3},{2,0},{3,1},{4,6},{5,7},{6,4},{7,5},{8,10},{9,11},{10,... | collective-permute-start | bytes 393224 | tf_op jit(solution)/shard_map/ppermute | solution.py:238
  12.5 0.8 %collective-permute-done.2.refs_3_ = f32[72,256]{1,0:T(8,128)S(1)} collective-permute-done((f32[72,256]{1,0:T(8,128)S(1)}, f32[72,256]{1,0:T(8,128)S(1)}, u32[]{:S(2)}, u32[]{:S(2)}) %collective-permute-start.2) | collective-permute-done | bytes 73760 | tf_op jit(solution)/shard_map/ppermute | solution.py:238
  13.3 1.2 %collective-permute-done.1.refs_2_ = f32[72,256]{1,0:T(8,128)S(1)} collective-permute-done((f32[72,256]{1,0:T(8,128)S(1)}, f32[72,256]{1,0:T(8,128)S(1)}, u32[]{:S(2)}, u32[]{:S(2)}) %collective-permute-start.1) | collective-permute-done | bytes 73760 | tf_op jit(solution)/shard_map/ppermute | solution.py:238
  14.6 0.2 collective-permute-done.refs_1_
  14.8 0.0 collective-permute-start.6
  14.8 0.3 shard_map.77
  15.1 0.5 %shard_map.78 = (f32[1024,512]{1,0:T(8,128)S(1)}, f32[16,128]{1,0:T(8,128)S(1)}, bf16[208,512]{1,0:T(8,128)(2,1)S(1)}) custom-call(f32[4,64,128]{2,1,0:T(8,128)S(1)} %pad_maximum_fusion.refs_0_, bf16[16,2048]{1,0:T(8,128)(2,1)S(1)} %get-tuple-element.46.refs_1_, bf16[1024,208]{1,0:T(8,128)(2,1)S(1)} %get-tuple-element.47.refs_2_), custom_call_target="tpu_custom_call" | custom-call | flops 400000000 | bytes 1562500 | tf_op jit(solution)/shard_map/pallas_call | solution.py:261
  15.6 0.4 %collective-permute-done.7.refs_0_ = f32[4,64,128]{2,1,0:T(8,128)S(1)} collective-permute-done((f32[4,64,128]{2,1,0:T(8,128)S(1)}, f32[4,64,128]{2,1,0:T(8,128)S(1)}, u32[]{:S(2)}, u32[]{:S(2)}) %collective-permute-start.7) | collective-permute-done | bytes 131104 | tf_op jit(solution)/shard_map/ppermute | solution.py:238
  16.0 0.2 collective-permute-start.8
  16.2 0.0 collective-permute-done.6.refs_0_
  16.2 0.5 %shard_map.79 = (f32[1024,512]{1,0:T(8,128)S(1)}, f32[16,128]{1,0:T(8,128)S(1)}, bf16[208,512]{1,0:T(8,128)(2,1)S(1)}) custom-call(f32[4,64,128]{2,1,0:T(8,128)S(1)} %collective-permute-done.6.refs_0_, bf16[16,2048]{1,0:T(8,128)(2,1)S(1)} %get-tuple-element.46.refs_1_, bf16[1024,208]{1,0:T(8,128)(2,1)S(1)} %get-tuple-element.47.refs_2_, ...), custom_call_target="tpu_custom_call" | custom-call | flops 400000000 | bytes 1562500 | tf_op jit(solution)/shard_map/pallas_call | solution.py:261
  16.6 0.5 %shard_map.80 = (f32[1024,512]{1,0:T(8,128)S(1)}, f32[16,128]{1,0:T(8,128)S(1)}, bf16[208,512]{1,0:T(8,128)(2,1)S(1)}) custom-call(f32[4,64,128]{2,1,0:T(8,128)S(1)} %collective-permute-done.7.refs_0_, bf16[16,2048]{1,0:T(8,128)(2,1)S(1)} %get-tuple-element.46.refs_1_, bf16[1024,208]{1,0:T(8,128)(2,1)S(1)} %get-tuple-element.47.refs_2_, ...), custom_call_target="tpu_custom_call" | custom-call | flops 400000000 | bytes 1562500 | tf_op jit(solution)/shard_map/pallas_call | solution.py:261
  17.1 0.3 collective-permute-done.8.refs_0_
  17.4 0.5 %shard_map.81 = (f32[1024,512]{1,0:T(8,128)S(1)}, f32[16,128]{1,0:T(8,128)S(1)}, bf16[208,512]{1,0:T(8,128)(2,1)S(1)}) custom-call(f32[4,64,128]{2,1,0:T(8,128)S(1)} %collective-permute-done.8.refs_0_, bf16[16,2048]{1,0:T(8,128)(2,1)S(1)} %get-tuple-element.46.refs_1_, bf16[1024,208]{1,0:T(8,128)(2,1)S(1)} %get-tuple-element.47.refs_2_, ...), custom_call_target="tpu_custom_call" | custom-call | flops 400000000 | bytes 1562500 | tf_op jit(solution)/shard_map/pallas_call | solution.py:261
  17.8 2.9 %collective-permute-start.9 = (f32[16,128]{1,0:T(8,128)S(1)}, f32[16,128]{1,0:T(8,128)S(1)}, u32[]{:S(2)}, u32[]{:S(2)}) collective-permute-start(f32[16,128]{1,0:T(8,128)S(1)} %get-tuple-element.59), channel_id=1, source_target_pairs={{0,8},{1,9},{2,10},{3,11},{4,12},{5,13},{6,14},{7,15},{8,0},{9,1},... | collective-permute-start | bytes 24584 | tf_op jit(solution)/shard_map/ppermute | solution.py:238
  20.7 1.7 %collective-permute-done.9 = f32[16,128]{1,0:T(8,128)S(1)} collective-permute-done((f32[16,128]{1,0:T(8,128)S(1)}, f32[16,128]{1,0:T(8,128)S(1)}, u32[]{:S(2)}, u32[]{:S(2)}) %collective-permute-start.9) | collective-permute-done | bytes 8224 | tf_op jit(solution)/shard_map/ppermute | solution.py:238
  22.4 0.3 collective-permute-start.12
  22.7 1.2 %collective-permute-start.11 = (f32[16,128]{1,0:T(8,128)S(1)}, f32[16,128]{1,0:T(8,128)S(1)}, u32[]{:S(2)}, u32[]{:S(2)}) collective-permute-start(f32[16,128]{1,0:T(8,128)S(1)} %add.6.refs_5_), channel_id=1, source_target_pairs={{0,2},{1,3},{2,0},{3,1},{4,6},{5,7},{6,4},{7,5},{8,10},{9,11},{10,... | collective-permute-start | bytes 24584 | tf_op jit(solution)/shard_map/ppermute | solution.py:238
  24.0 0.3 collective-permute-start.10
  24.3 1.3 %collective-permute-done.12.refs_8_ = f32[16,128]{1,0:T(8,128)S(1)} collective-permute-done((f32[16,128]{1,0:T(8,128)S(1)}, f32[16,128]{1,0:T(8,128)S(1)}, u32[]{:S(2)}, u32[]{:S(2)}) %collective-permute-start.12) | collective-permute-done | bytes 8224 | tf_op jit(solution)/shard_map/ppermute | solution.py:238
  25.6 0.8 %collective-permute-done.11.refs_7_ = f32[16,128]{1,0:T(8,128)S(1)} collective-permute-done((f32[16,128]{1,0:T(8,128)S(1)}, f32[16,128]{1,0:T(8,128)S(1)}, u32[]{:S(2)}, u32[]{:S(2)}) %collective-permute-start.11) | collective-permute-done | bytes 8224 | tf_op jit(solution)/shard_map/ppermute | solution.py:238
  26.4 0.0 collective-permute-done.10.refs_6_
  26.4 0.7 %shard_map.82 = (f32[8,128]{1,0:T(8,128)S(1)}, f32[16,128]{1,0:T(8,128)S(1)}) custom-call(f32[16,128]{1,0:T(8,128)S(1)} %get-tuple-element.44.refs_0_.refs_1_, f32[1024,512]{1,0:T(8,128)S(1)} %get-tuple-element.48.refs_1_.refs_0_, f32[1024,512]{1,0:T(8,128)S(1)} %get-tuple-element.53.refs_2_.refs_1_, f32[1024,512]{1,0:T(8,128)S(1)} %get-tuple-element.56.refs_3_.refs_2_, ...), custom_call_target="tpu_custom_call" | custom-call | tf_op jit(solution)/shard_map/pallas_call | solution.py:261
  27.1 1.6 %collective-permute-start.13 = (f32[8,128]{1,0:T(8,128)S(1)}, f32[8,128]{1,0:T(8,128)S(1)}, u32[]{:S(2)}, u32[]{:S(2)}) collective-permute-start(f32[8,128]{1,0:T(8,128)S(1)} %get-tuple-element.66.refs_7_), channel_id=1, source_target_pairs={{0,16},{16,0},{1,17},{17,1},{2,18},{18,2},{3,19},{19,3},{4,20},{20... | collective-permute-start | bytes 12296 | tf_op jit(solution)/shard_map/ppermute | solution.py:238
  28.7 0.5 %shard_map.83 = (f32[1024,512]{1,0:T(8,128)S(1)}, f32[1024,512]{1,0:T(8,128)S(1)}, f32[1024,512]{1,0:T(8,128)S(1)}, f32[1024,512]{1,0:T(8,128)S(1)}) custom-call(f32[1024,512]{1,0:T(8,128)S(1)} %get-tuple-element.48.refs_1_.refs_0_, f32[1024,512]{1,0:T(8,128)S(1)} %get-tuple-element.53.refs_2_.refs_1_, f32[1024,512]{1,0:T(8,128)S(1)} %get-tuple-element.56.refs_3_.refs_2_, ...), custom_call_target="tpu_custom_call" | custom-call | flops 1000000000 | bytes 3906250 | tf_op jit(solution)/shard_map/pallas_call | solution.py:261
  29.2 1.6 %collective-permute-done.13.refs_8_ = f32[8,128]{1,0:T(8,128)S(1)} collective-permute-done((f32[8,128]{1,0:T(8,128)S(1)}, f32[8,128]{1,0:T(8,128)S(1)}, u32[]{:S(2)}, u32[]{:S(2)}) %collective-permute-start.13) | collective-permute-done | bytes 4128 | tf_op jit(solution)/shard_map/ppermute | solution.py:238
  30.8 0.8 %shard_map.84 = (f32[16,128]{1,0:T(8,128)S(1)}, f32[4,128]{1,0:T(4,128)S(1)}, f32[16,128]{1,0:T(8,128)S(1)}, f32[1,512]{1,0:T(1,128)S(1)}) custom-call(f32[16,128]{1,0:T(8,128)S(1)} %get-tuple-element.44.refs_0_.refs_1_, f32[16,128]{1,0:T(8,128)S(1)} %get-tuple-element.60.refs_1_, f32[8,128]{1,0:T(8,128)S(1)} %get-tuple-element.61.refs_2_, ...), custom_call_target="tpu_custom_call" | custom-call | tf_op jit(solution)/shard_map/pallas_call | solution.py:261
  31.5 2.7 %collective-permute-start.14 = (f32[16,128]{1,0:T(8,128)S(1)}, f32[16,128]{1,0:T(8,128)S(1)}, u32[]{:S(2)}, u32[]{:S(2)}) collective-permute-start(f32[16,128]{1,0:T(8,128)S(1)} %get-tuple-element.73), channel_id=1, source_target_pairs={{0,8},{1,9},{2,10},{3,11},{4,12},{5,13},{6,14},{7,15},{8,0},{9,1},... | collective-permute-start | bytes 24584 | tf_op jit(solution)/shard_map/ppermute | solution.py:238
  34.3 1.9 %collective-permute-done.14 = f32[16,128]{1,0:T(8,128)S(1)} collective-permute-done((f32[16,128]{1,0:T(8,128)S(1)}, f32[16,128]{1,0:T(8,128)S(1)}, u32[]{:S(2)}, u32[]{:S(2)}) %collective-permute-start.14) | collective-permute-done | bytes 8224 | tf_op jit(solution)/shard_map/ppermute | solution.py:238
  36.2 0.0 collective-permute-start.17
  36.2 1.3 %collective-permute-start.16 = (f32[16,128]{1,0:T(8,128)S(1)}, f32[16,128]{1,0:T(8,128)S(1)}, u32[]{:S(2)}, u32[]{:S(2)}) collective-permute-start(f32[16,128]{1,0:T(8,128)S(1)} %add.7.refs_2_), channel_id=1, source_target_pairs={{0,2},{1,3},{2,0},{3,1},{4,6},{5,7},{6,4},{7,5},{8,10},{9,11},{10,... | collective-permute-start | bytes 24584 | tf_op jit(solution)/shard_map/ppermute | solution.py:238
  37.4 0.6 %collective-permute-start.15 = (f32[16,128]{1,0:T(8,128)S(1)}, f32[16,128]{1,0:T(8,128)S(1)}, u32[]{:S(2)}, u32[]{:S(2)}) collective-permute-start(f32[16,128]{1,0:T(8,128)S(1)} %add.7.refs_2_), channel_id=1, source_target_pairs={{0,1},{1,0},{2,3},{3,2},{4,5},{5,4},{6,7},{7,6},{8,9},{9,8},{10,11... | collective-permute-start | bytes 24584 | tf_op jit(solution)/shard_map/ppermute | solution.py:238
  38.0 1.1 %shard_map.85.refs_0_ = f32[2048,512]{1,0:T(8,128)S(1)} custom-call(bf16[208,1024]{1,0:T(8,128)(2,1)S(1)} %get-tuple-element.43.refs_0_, f32[16,128]{1,0:T(8,128)S(1)} %get-tuple-element.67.refs_1_, f32[1,512]{1,0:T(1,128)S(1)} %get-tuple-element.68.refs_2_, bf16[208,512]{1,0:T(8,128)(2,1)S(1)} %get-tuple-element.69.refs_3_, ...), custom_call_target="tpu_custom_call" | custom-call | flops 1000000000 | bytes 3906250 | tf_op jit(solution)/shard_map/pallas_call | solution.py:261
  39.1 0.6 %copy.8 = f32[512]{0:T(512)} copy(f32[512]{0:T(512)S(1)} %bitcast.11) | data formatting | bytes 4096
  39.7 0.0 collective-permute-done.17.refs_5_
  39.7 0.1 collective-permute-done.16.refs_4_
  39.9 0.0 collective-permute-done.15.refs_3_
  39.9 2.3 %shard_map.86 = (f32[2048,512]{1,0:T(8,128)}, f32[16,128]{1,0:T(8,128)}) custom-call(f32[2048,512]{1,0:T(8,128)S(1)} %shard_map.85.refs_0_, f32[16,128]{1,0:T(8,128)S(1)} %get-tuple-element.44.refs_0_.refs_1_, f32[16,128]{1,0:T(8,128)S(1)} %add.7.refs_2_, f32[16,128]{1,0:T(8,128)S(1)} %collective-permute-done.15.refs_3_, ...), custom_call_target="tpu_custom_call" | custom-call | tf_op jit(solution)/shard_map/pallas_call | solution.py:357
  (3 shorter events, 0.0 us)
Async XLA Ops:
  0.6 9.8 %collective-permute-start.5 = (f32[64,128]{1,0:T(8,128)}, f32[64,128]{1,0:T(8,128)S(1)}, u32[]{:S(2)}, u32[]{:S(2)}) collective-permute-start(f32[64,128]{1,0:T(8,128)} %bitcast.14), channel_id=1, source_target_pairs={{0,8},{1,9},{2,10},{3,11},{4,12},{5,13},{6,14},{7,15},{8,0},{9,1},... | collective-permute-start | bytes 98312 | tf_op jit(solution)/shard_map/ppermute | solution.py:238
  4.7 6.2 %collective-permute-start.4 = (f32[64,128]{1,0:T(8,128)}, f32[64,128]{1,0:T(8,128)S(1)}, u32[]{:S(2)}, u32[]{:S(2)}) collective-permute-start(f32[64,128]{1,0:T(8,128)} %bitcast.15), channel_id=1, source_target_pairs={{0,12},{1,13},{2,14},{3,15},{4,8},{5,9},{6,10},{7,11},{8,4},{9,5},... | collective-permute-start | bytes 98312 | tf_op jit(solution)/shard_map/ppermute | solution.py:238
  6.1 4.9 %collective-permute-start.3 = (f32[64,128]{1,0:T(8,128)}, f32[64,128]{1,0:T(8,128)S(1)}, u32[]{:S(2)}, u32[]{:S(2)}) collective-permute-start(f32[64,128]{1,0:T(8,128)} %bitcast.16), channel_id=1, source_target_pairs={{0,4},{1,5},{2,6},{3,7},{4,0},{5,1},{6,2},{7,3},{8,12},{9,13},{10,... | collective-permute-start | bytes 98312 | tf_op jit(solution)/shard_map/ppermute | solution.py:238
  7.4 5.9 %collective-permute-start.2 = (f32[72,256]{1,0:T(8,128)S(1)}, f32[72,256]{1,0:T(8,128)S(1)}, u32[]{:S(2)}, u32[]{:S(2)}) collective-permute-start(f32[72,256]{1,0:T(8,128)S(1)} %get-tuple-element.40.refs_0_), channel_id=1, source_target_pairs={{0,20},{1,21},{2,22},{3,23},{4,16},{5,17},{6,18},{7,19},{8,28},{9,... | collective-permute-start | bytes 221192 | tf_op jit(solution)/shard_map/ppermute | solution.py:238
  10.2 4.4 %collective-permute-start.1 = (f32[72,256]{1,0:T(8,128)S(1)}, f32[72,256]{1,0:T(8,128)S(1)}, u32[]{:S(2)}, u32[]{:S(2)}) collective-permute-start(f32[72,256]{1,0:T(8,128)S(1)} %get-tuple-element.40.refs_0_), channel_id=1, source_target_pairs={{0,4},{1,5},{2,6},{3,7},{4,0},{5,1},{6,2},{7,3},{8,12},{9,13},{10,... | collective-permute-start | bytes 221192 | tf_op jit(solution)/shard_map/ppermute | solution.py:238
  10.4 4.4 %collective-permute-start = (f32[72,256]{1,0:T(8,128)S(1)}, f32[72,256]{1,0:T(8,128)S(1)}, u32[]{:S(2)}, u32[]{:S(2)}) collective-permute-start(f32[72,256]{1,0:T(8,128)S(1)} %get-tuple-element.40.refs_0_), channel_id=1, source_target_pairs={{0,16},{1,17},{2,18},{3,19},{4,20},{5,21},{6,22},{7,23},{8,24},{9,... | collective-permute-start | bytes 221192 | tf_op jit(solution)/shard_map/ppermute | solution.py:238
  11.0 5.0 %collective-permute-start.7 = (f32[4,64,128]{2,1,0:T(8,128)S(1)}, f32[4,64,128]{2,1,0:T(8,128)S(1)}, u32[]{:S(2)}, u32[]{:S(2)}) collective-permute-start(f32[4,64,128]{2,1,0:T(8,128)S(1)} %pad_maximum_fusion.refs_0_), channel_id=1, source_target_pairs={{0,2},{1,3},{2,0},{3,1},{4,6},{5,7},{6,4},{7,5},{8,10},{9,11},{10,... | collective-permute-start | bytes 393224 | tf_op jit(solution)/shard_map/ppermute | solution.py:238
  14.8 1.4 %collective-permute-start.6 = (f32[4,64,128]{2,1,0:T(8,128)S(1)}, f32[4,64,128]{2,1,0:T(8,128)S(1)}, u32[]{:S(2)}, u32[]{:S(2)}) collective-permute-start(f32[4,64,128]{2,1,0:T(8,128)S(1)} %pad_maximum_fusion.refs_0_), channel_id=1, source_target_pairs={{0,1},{1,0},{2,3},{3,2},{4,5},{5,4},{6,7},{7,6},{8,9},{9,8},{10,11... | collective-permute-start | bytes 393224 | tf_op jit(solution)/shard_map/ppermute | solution.py:238
  16.0 1.3 %collective-permute-start.8 = (f32[4,64,128]{2,1,0:T(8,128)S(1)}, f32[4,64,128]{2,1,0:T(8,128)S(1)}, u32[]{:S(2)}, u32[]{:S(2)}) collective-permute-start(f32[4,64,128]{2,1,0:T(8,128)S(1)} %collective-permute-done.7.refs_0_), channel_id=1, source_target_pairs={{0,1},{1,0},{2,3},{3,2},{4,5},{5,4},{6,7},{7,6},{8,9},{9,8},{10,11... | collective-permute-start | bytes 393224 | tf_op jit(solution)/shard_map/ppermute | solution.py:238
  17.8 4.6 %collective-permute-start.9 = (f32[16,128]{1,0:T(8,128)S(1)}, f32[16,128]{1,0:T(8,128)S(1)}, u32[]{:S(2)}, u32[]{:S(2)}) collective-permute-start(f32[16,128]{1,0:T(8,128)S(1)} %get-tuple-element.59), channel_id=1, source_target_pairs={{0,8},{1,9},{2,10},{3,11},{4,12},{5,13},{6,14},{7,15},{8,0},{9,1},... | collective-permute-start | bytes 24584 | tf_op jit(solution)/shard_map/ppermute | solution.py:238
  22.4 3.1 %collective-permute-start.12 = (f32[16,128]{1,0:T(8,128)S(1)}, f32[16,128]{1,0:T(8,128)S(1)}, u32[]{:S(2)}, u32[]{:S(2)}) collective-permute-start(f32[16,128]{1,0:T(8,128)S(1)} %add.6.refs_5_), channel_id=1, source_target_pairs={{0,3},{1,2},{2,1},{3,0},{4,7},{5,6},{6,5},{7,4},{8,11},{9,10},{10,... | collective-permute-start | bytes 24584 | tf_op jit(solution)/shard_map/ppermute | solution.py:238
  22.7 3.7 %collective-permute-start.11 = (f32[16,128]{1,0:T(8,128)S(1)}, f32[16,128]{1,0:T(8,128)S(1)}, u32[]{:S(2)}, u32[]{:S(2)}) collective-permute-start(f32[16,128]{1,0:T(8,128)S(1)} %add.6.refs_5_), channel_id=1, source_target_pairs={{0,2},{1,3},{2,0},{3,1},{4,6},{5,7},{6,4},{7,5},{8,10},{9,11},{10,... | collective-permute-start | bytes 24584 | tf_op jit(solution)/shard_map/ppermute | solution.py:238
  24.0 2.4 %collective-permute-start.10 = (f32[16,128]{1,0:T(8,128)S(1)}, f32[16,128]{1,0:T(8,128)S(1)}, u32[]{:S(2)}, u32[]{:S(2)}) collective-permute-start(f32[16,128]{1,0:T(8,128)S(1)} %add.6.refs_5_), channel_id=1, source_target_pairs={{0,1},{1,0},{2,3},{3,2},{4,5},{5,4},{6,7},{7,6},{8,9},{9,8},{10,11... | collective-permute-start | bytes 24584 | tf_op jit(solution)/shard_map/ppermute | solution.py:238
  27.1 3.7 %collective-permute-start.13 = (f32[8,128]{1,0:T(8,128)S(1)}, f32[8,128]{1,0:T(8,128)S(1)}, u32[]{:S(2)}, u32[]{:S(2)}) collective-permute-start(f32[8,128]{1,0:T(8,128)S(1)} %get-tuple-element.66.refs_7_), channel_id=1, source_target_pairs={{0,16},{16,0},{1,17},{17,1},{2,18},{18,2},{3,19},{19,3},{4,20},{20... | collective-permute-start | bytes 12296 | tf_op jit(solution)/shard_map/ppermute | solution.py:238
  31.5 4.6 %collective-permute-start.14 = (f32[16,128]{1,0:T(8,128)S(1)}, f32[16,128]{1,0:T(8,128)S(1)}, u32[]{:S(2)}, u32[]{:S(2)}) collective-permute-start(f32[16,128]{1,0:T(8,128)S(1)} %get-tuple-element.73), channel_id=1, source_target_pairs={{0,8},{1,9},{2,10},{3,11},{4,12},{5,13},{6,14},{7,15},{8,0},{9,1},... | collective-permute-start | bytes 24584 | tf_op jit(solution)/shard_map/ppermute | solution.py:238
  36.2 3.6 %collective-permute-start.17 = (f32[16,128]{1,0:T(8,128)S(1)}, f32[16,128]{1,0:T(8,128)S(1)}, u32[]{:S(2)}, u32[]{:S(2)}) collective-permute-start(f32[16,128]{1,0:T(8,128)S(1)} %add.7.refs_2_), channel_id=1, source_target_pairs={{0,3},{1,2},{2,1},{3,0},{4,7},{5,6},{6,5},{7,4},{8,11},{9,10},{10,... | collective-permute-start | bytes 24584 | tf_op jit(solution)/shard_map/ppermute | solution.py:238
  36.2 3.7 %collective-permute-start.16 = (f32[16,128]{1,0:T(8,128)S(1)}, f32[16,128]{1,0:T(8,128)S(1)}, u32[]{:S(2)}, u32[]{:S(2)}) collective-permute-start(f32[16,128]{1,0:T(8,128)S(1)} %add.7.refs_2_), channel_id=1, source_target_pairs={{0,2},{1,3},{2,0},{3,1},{4,6},{5,7},{6,4},{7,5},{8,10},{9,11},{10,... | collective-permute-start | bytes 24584 | tf_op jit(solution)/shard_map/ppermute | solution.py:238
  37.4 2.4 %collective-permute-start.15 = (f32[16,128]{1,0:T(8,128)S(1)}, f32[16,128]{1,0:T(8,128)S(1)}, u32[]{:S(2)}, u32[]{:S(2)}) collective-permute-start(f32[16,128]{1,0:T(8,128)S(1)} %add.7.refs_2_), channel_id=1, source_target_pairs={{0,1},{1,0},{2,3},{3,2},{4,5},{5,4},{6,7},{7,6},{8,9},{9,8},{10,11... | collective-permute-start | bytes 24584 | tf_op jit(solution)/shard_map/ppermute | solution.py:238

commit v8 on v6

--- a/solution.py
+++ b/solution.py
@@ -95,7 +95,7 @@
     return jnp.concatenate(parts, axis=0).astype(BF16)
 
 
-def impressions_kernel(cols, rows, own_ref, down_ref, side_ref, cross_ref, logs_ref, lhs_ref, lhs_t_ref, extra_ref, price_ref):
+def impressions_kernel(cols, rows, own_ref, side_ref, cross_ref, down_ref, logs_ref, lhs_ref, lhs_t_ref, extra_ref, price_ref):
     _, w = home()
     half = lax.axis_index("adv")
     width = own_ref.shape[1]
@@ -283,10 +283,10 @@
         compiler_params=PARAMS,
     )(*ins)
     line = jnp.stack([own, *with_partners(adv_t, (4, 12, 8))[1:]])
-    down, side, cross = [swap(pack, ("adv", "imp"), k) for k in (16, 4, 20)]
+    side, cross, down = [swap(pack, ("adv", "imp"), k) for k in (4, 20, 16)]
     plane = swap(line, "imp", 2)
-    plane, _ = lax.optimization_barrier((plane, (down, side, cross)))
-    ready, _ = lax.optimization_barrier((line, (down, side, cross)))
+    plane, _ = lax.optimization_barrier((plane, (side, cross, down)))
+    ready, _ = lax.optimization_barrier((line, (side, cross, down)))
     line_pair = swap(ready, "imp", 1)
     at_line = (0, 4, 12, 8)
     at_line_pair = tuple(k + 1 for k in at_line)
@@ -303,7 +303,7 @@
             shape(16, adv_count, dtype=BF16),
             shape(2 * cols, BLOCK),
         ),
-        (pack, down, side, cross, logs),
+        (pack, side, cross, down, logs),
         cost=10**8,
     )
     gains, rhs, sums = [], [], ()

time: 42.3 us -> 42.4 us (level)
  no operation moved by 1% of the time
where the time goes in v8:
time: 42.4 us; the launch traced here: 42.3 us
  starting transfers between devices  21.9 us (52%)
  waiting for transfers between devices  10.7 us (25%)
  Pallas kernels  8.34 us (20%)
  between operations  0.72 us (2%)
  local copies, waits for them, and re-layouts  0.58 us (1%)
    ppermute x18, starting transfers between devices, swap(): lax.ppermute(x, axis, [(i, i ^ k) for i in range(lax.axis_size(axis))])  21.9 us
    ppermute x18, waiting for transfers between devices, swap(): lax.ppermute(x, axis, [(i, i ^ k) for i in range(lax.axis_size(axis))])  10.7 us
    pallas_call x9, Pallas kernels, call(): pl.pallas_call(kernel, out_shape=out, in_specs=[VMEM] * len(operands), ou...  4.98 us
    pallas_call x1, Pallas kernels, staged(): pl.pallas_call(lambda *refs: final_kernel(keys, advs, *refs), out_shape=(...  2.29 us
    pallas_call x1, Pallas kernels, staged(): pl.pallas_call(lambda *refs: prepare_kernel(ratio, imps, *refs), out_shap...  1.07 us
  transfers between devices with their start and end apart: 18, of which 11 were waited for; matrix products, arithmetic and copies ran while one was open for 1% of the time, Pallas kernels for 10%

profile of v8, /device:TPU:0, one launch (start us, length us, event | category | flops | bytes accessed | tf_op | source)
XLA Modules:
  0.0 42.3 jit_solution(15824315620238394630)
XLA Ops:
  0.6 4.1 %collective-permute-start.5 = (f32[64,128]{1,0:T(8,128)}, f32[64,128]{1,0:T(8,128)S(1)}, u32[]{:S(2)}, u32[]{:S(2)}) collective-permute-start(f32[64,128]{1,0:T(8,128)} %bitcast.14), channel_id=1, source_target_pairs={{0,8},{1,9},{2,10},{3,11},{4,12},{5,13},{6,14},{7,15},{8,0},{9,1},... | collective-permute-start | bytes 98312 | tf_op jit(solution)/shard_map/ppermute | solution.py:236
  4.7 1.3 %collective-permute-start.4 = (f32[64,128]{1,0:T(8,128)}, f32[64,128]{1,0:T(8,128)S(1)}, u32[]{:S(2)}, u32[]{:S(2)}) collective-permute-start(f32[64,128]{1,0:T(8,128)} %bitcast.15), channel_id=1, source_target_pairs={{0,12},{1,13},{2,14},{3,15},{4,8},{5,9},{6,10},{7,11},{8,4},{9,5},... | collective-permute-start | bytes 98312 | tf_op jit(solution)/shard_map/ppermute | solution.py:236
  6.1 0.2 collective-permute-start.3
  6.3 1.1 %shard_map.76 = (f32[72,256]{1,0:T(8,128)S(1)}, f32[16,128]{1,0:T(8,128)S(1)}, f32[16,128]{1,0:T(8,128)S(1)}, f32[64,128]{1,0:T(8,128)S(1)}) custom-call(s32[4,16]{1,0:T(4,128)} %bitcast.23, s32[16,128]{1,0:T(8,128)} %bitcast.21, f32[16,128]{1,0:T(8,128)} %bitcast.22, f32[64,256]{1,0:T(8,128)} %bitcast.13, f32[64,128]{1,0:T(8,128)} %bitcast.17), custom_call_target="tpu_custom_call" | custom-call | tf_op jit(solution)/shard_map/pallas_call | solution.py:272
  7.4 1.6 %collective-permute-start.2 = (f32[72,256]{1,0:T(8,128)S(1)}, f32[72,256]{1,0:T(8,128)S(1)}, u32[]{:S(2)}, u32[]{:S(2)}) collective-permute-start(f32[72,256]{1,0:T(8,128)S(1)} %get-tuple-element.39.refs_0_), channel_id=1, source_target_pairs={{0,16},{1,17},{2,18},{3,19},{4,20},{5,21},{6,22},{7,23},{8,24},{9,... | collective-permute-start | bytes 221192 | tf_op jit(solution)/shard_map/ppermute | solution.py:236
  9.0 1.7 %collective-permute-start.1 = (f32[72,256]{1,0:T(8,128)S(1)}, f32[72,256]{1,0:T(8,128)S(1)}, u32[]{:S(2)}, u32[]{:S(2)}) collective-permute-start(f32[72,256]{1,0:T(8,128)S(1)} %get-tuple-element.39.refs_0_), channel_id=1, source_target_pairs={{0,20},{1,21},{2,22},{3,23},{4,16},{5,17},{6,18},{7,19},{8,28},{9,... | collective-permute-start | bytes 221192 | tf_op jit(solution)/shard_map/ppermute | solution.py:236
  10.7 0.0 collective-permute-done.5
  10.7 0.2 collective-permute-start
  10.9 0.0 collective-permute-done.4
  11.0 0.0 collective-permute-done.3
  11.0 1.6 %collective-permute-start.7 = (f32[4,64,128]{2,1,0:T(8,128)S(1)}, f32[4,64,128]{2,1,0:T(8,128)S(1)}, u32[]{:S(2)}, u32[]{:S(2)}) collective-permute-start(f32[4,64,128]{2,1,0:T(8,128)S(1)} %pad_maximum_fusion.refs_0_), channel_id=1, source_target_pairs={{0,2},{1,3},{2,0},{3,1},{4,6},{5,7},{6,4},{7,5},{8,10},{9,11},{10,... | collective-permute-start | bytes 393224 | tf_op jit(solution)/shard_map/ppermute | solution.py:236
  12.5 0.1 collective-permute-done.2.refs_3_
  12.6 1.7 %collective-permute-done.1.refs_2_ = f32[72,256]{1,0:T(8,128)S(1)} collective-permute-done((f32[72,256]{1,0:T(8,128)S(1)}, f32[72,256]{1,0:T(8,128)S(1)}, u32[]{:S(2)}, u32[]{:S(2)}) %collective-permute-start.1) | collective-permute-done | bytes 73760 | tf_op jit(solution)/shard_map/ppermute | solution.py:236
  14.3 0.8 %collective-permute-done.refs_1_ = f32[72,256]{1,0:T(8,128)S(1)} collective-permute-done((f32[72,256]{1,0:T(8,128)S(1)}, f32[72,256]{1,0:T(8,128)S(1)}, u32[]{:S(2)}, u32[]{:S(2)}) %collective-permute-start) | collective-permute-done | bytes 73760 | tf_op jit(solution)/shard_map/ppermute | solution.py:236
  15.1 0.0 collective-permute-start.6
  15.1 0.3 shard_map.77
  15.4 0.5 %shard_map.78 = (f32[1024,512]{1,0:T(8,128)S(1)}, f32[16,128]{1,0:T(8,128)S(1)}, bf16[208,512]{1,0:T(8,128)(2,1)S(1)}) custom-call(f32[4,64,128]{2,1,0:T(8,128)S(1)} %pad_maximum_fusion.refs_0_, bf16[16,2048]{1,0:T(8,128)(2,1)S(1)} %get-tuple-element.43.refs_1_, bf16[1024,208]{1,0:T(8,128)(2,1)S(1)} %get-tuple-element.44.refs_2_), custom_call_target="tpu_custom_call" | custom-call | flops 400000000 | bytes 1562500 | tf_op jit(solution)/shard_map/pallas_call | solution.py:259
  15.9 0.1 collective-permute-done.7.refs_0_
  16.0 0.4 %collective-permute-start.8 = (f32[4,64,128]{2,1,0:T(8,128)S(1)}, f32[4,64,128]{2,1,0:T(8,128)S(1)}, u32[]{:S(2)}, u32[]{:S(2)}) collective-permute-start(f32[4,64,128]{2,1,0:T(8,128)S(1)} %collective-permute-done.7.refs_0_), channel_id=1, source_target_pairs={{0,1},{1,0},{2,3},{3,2},{4,5},{5,4},{6,7},{7,6},{8,9},{9,8},{10,11... | collective-permute-start | bytes 393224 | tf_op jit(solution)/shard_map/ppermute | solution.py:236
  16.4 0.0 collective-permute-done.6.refs_0_
  16.4 0.5 %shard_map.79 = (f32[1024,512]{1,0:T(8,128)S(1)}, f32[16,128]{1,0:T(8,128)S(1)}, bf16[208,512]{1,0:T(8,128)(2,1)S(1)}) custom-call(f32[4,64,128]{2,1,0:T(8,128)S(1)} %collective-permute-done.6.refs_0_, bf16[16,2048]{1,0:T(8,128)(2,1)S(1)} %get-tuple-element.43.refs_1_, bf16[1024,208]{1,0:T(8,128)(2,1)S(1)} %get-tuple-element.44.refs_2_, ...), custom_call_target="tpu_custom_call" | custom-call | flops 400000000 | bytes 1562500 | tf_op jit(solution)/shard_map/pallas_call | solution.py:259
  16.9 0.5 %shard_map.80 = (f32[1024,512]{1,0:T(8,128)S(1)}, f32[16,128]{1,0:T(8,128)S(1)}, bf16[208,512]{1,0:T(8,128)(2,1)S(1)}) custom-call(f32[4,64,128]{2,1,0:T(8,128)S(1)} %collective-permute-done.7.refs_0_, bf16[16,2048]{1,0:T(8,128)(2,1)S(1)} %get-tuple-element.43.refs_1_, bf16[1024,208]{1,0:T(8,128)(2,1)S(1)} %get-tuple-element.44.refs_2_, ...), custom_call_target="tpu_custom_call" | custom-call | flops 400000000 | bytes 1562500 | tf_op jit(solution)/shard_map/pallas_call | solution.py:259
  17.4 0.1 collective-permute-done.8.refs_0_
  17.4 0.5 %shard_map.81 = (f32[1024,512]{1,0:T(8,128)S(1)}, f32[16,128]{1,0:T(8,128)S(1)}, bf16[208,512]{1,0:T(8,128)(2,1)S(1)}) custom-call(f32[4,64,128]{2,1,0:T(8,128)S(1)} %collective-permute-done.8.refs_0_, bf16[16,2048]{1,0:T(8,128)(2,1)S(1)} %get-tuple-element.43.refs_1_, bf16[1024,208]{1,0:T(8,128)(2,1)S(1)} %get-tuple-element.44.refs_2_, ...), custom_call_target="tpu_custom_call" | custom-call | flops 400000000 | bytes 1562500 | tf_op jit(solution)/shard_map/pallas_call | solution.py:259
  17.9 2.8 %collective-permute-start.9 = (f32[16,128]{1,0:T(8,128)S(1)}, f32[16,128]{1,0:T(8,128)S(1)}, u32[]{:S(2)}, u32[]{:S(2)}) collective-permute-start(f32[16,128]{1,0:T(8,128)S(1)} %get-tuple-element.61), channel_id=1, source_target_pairs={{0,8},{1,9},{2,10},{3,11},{4,12},{5,13},{6,14},{7,15},{8,0},{9,1},... | collective-permute-start | bytes 24584 | tf_op jit(solution)/shard_map/ppermute | solution.py:236
  20.7 1.8 %collective-permute-done.9 = f32[16,128]{1,0:T(8,128)S(1)} collective-permute-done((f32[16,128]{1,0:T(8,128)S(1)}, f32[16,128]{1,0:T(8,128)S(1)}, u32[]{:S(2)}, u32[]{:S(2)}) %collective-permute-start.9) | collective-permute-done | bytes 8224 | tf_op jit(solution)/shard_map/ppermute | solution.py:236
  22.5 0.3 collective-permute-start.12
  22.8 1.2 %collective-permute-start.11 = (f32[16,128]{1,0:T(8,128)S(1)}, f32[16,128]{1,0:T(8,128)S(1)}, u32[]{:S(2)}, u32[]{:S(2)}) collective-permute-start(f32[16,128]{1,0:T(8,128)S(1)} %add.6.refs_5_), channel_id=1, source_target_pairs={{0,2},{1,3},{2,0},{3,1},{4,6},{5,7},{6,4},{7,5},{8,10},{9,11},{10,... | collective-permute-start | bytes 24584 | tf_op jit(solution)/shard_map/ppermute | solution.py:236
  24.1 0.3 collective-permute-start.10
  24.4 1.2 %collective-permute-done.12.refs_8_ = f32[16,128]{1,0:T(8,128)S(1)} collective-permute-done((f32[16,128]{1,0:T(8,128)S(1)}, f32[16,128]{1,0:T(8,128)S(1)}, u32[]{:S(2)}, u32[]{:S(2)}) %collective-permute-start.12) | collective-permute-done | bytes 8224 | tf_op jit(solution)/shard_map/ppermute | solution.py:236
  25.6 0.8 %collective-permute-done.11.refs_7_ = f32[16,128]{1,0:T(8,128)S(1)} collective-permute-done((f32[16,128]{1,0:T(8,128)S(1)}, f32[16,128]{1,0:T(8,128)S(1)}, u32[]{:S(2)}, u32[]{:S(2)}) %collective-permute-start.11) | collective-permute-done | bytes 8224 | tf_op jit(solution)/shard_map/ppermute | solution.py:236
  26.5 0.0 collective-permute-done.10.refs_6_
  26.5 0.8 %shard_map.83 = (f32[8,128]{1,0:T(8,128)S(1)}, f32[16,128]{1,0:T(8,128)S(1)}) custom-call(f32[16,128]{1,0:T(8,128)S(1)} %get-tuple-element.56.refs_0_.refs_1_, f32[1024,512]{1,0:T(8,128)S(1)} %get-tuple-element.57.refs_1_.refs_0_, f32[1024,512]{1,0:T(8,128)S(1)} %get-tuple-element.58.refs_2_.refs_1_, f32[1024,512]{1,0:T(8,128)S(1)} %get-tuple-element.59.refs_3_.refs_2_, ...), custom_call_target="tpu_custom_call" | custom-call | tf_op jit(solution)/shard_map/pallas_call | solution.py:259
  27.2 1.6 %collective-permute-start.13 = (f32[8,128]{1,0:T(8,128)S(1)}, f32[8,128]{1,0:T(8,128)S(1)}, u32[]{:S(2)}, u32[]{:S(2)}) collective-permute-start(f32[8,128]{1,0:T(8,128)S(1)} %get-tuple-element.68.refs_7_), channel_id=1, source_target_pairs={{0,16},{16,0},{1,17},{17,1},{2,18},{18,2},{3,19},{19,3},{4,20},{20... | collective-permute-start | bytes 12296 | tf_op jit(solution)/shard_map/ppermute | solution.py:236
  28.8 0.5 %shard_map.84 = (f32[1024,512]{1,0:T(8,128)S(1)}, f32[1024,512]{1,0:T(8,128)S(1)}, f32[1024,512]{1,0:T(8,128)S(1)}, f32[1024,512]{1,0:T(8,128)S(1)}) custom-call(f32[1024,512]{1,0:T(8,128)S(1)} %get-tuple-element.57.refs_1_.refs_0_, f32[1024,512]{1,0:T(8,128)S(1)} %get-tuple-element.58.refs_2_.refs_1_, f32[1024,512]{1,0:T(8,128)S(1)} %get-tuple-element.59.refs_3_.refs_2_, ...), custom_call_target="tpu_custom_call" | custom-call | flops 1000000000 | bytes 3906250 | tf_op jit(solution)/shard_map/pallas_call | solution.py:259
  29.4 1.5 %collective-permute-done.13.refs_8_ = f32[8,128]{1,0:T(8,128)S(1)} collective-permute-done((f32[8,128]{1,0:T(8,128)S(1)}, f32[8,128]{1,0:T(8,128)S(1)}, u32[]{:S(2)}, u32[]{:S(2)}) %collective-permute-start.13) | collective-permute-done | bytes 4128 | tf_op jit(solution)/shard_map/ppermute | solution.py:236
  30.9 0.8 %shard_map.85 = (f32[16,128]{1,0:T(8,128)S(1)}, f32[4,128]{1,0:T(4,128)S(1)}, f32[16,128]{1,0:T(8,128)S(1)}, f32[1,512]{1,0:T(1,128)S(1)}) custom-call(f32[16,128]{1,0:T(8,128)S(1)} %get-tuple-element.56.refs_0_.refs_1_, f32[16,128]{1,0:T(8,128)S(1)} %get-tuple-element.62.refs_1_, f32[8,128]{1,0:T(8,128)S(1)} %get-tuple-element.63.refs_2_, ...), custom_call_target="tpu_custom_call" | custom-call | tf_op jit(solution)/shard_map/pallas_call | solution.py:259
  31.7 2.6 %collective-permute-start.14 = (f32[16,128]{1,0:T(8,128)S(1)}, f32[16,128]{1,0:T(8,128)S(1)}, u32[]{:S(2)}, u32[]{:S(2)}) collective-permute-start(f32[16,128]{1,0:T(8,128)S(1)} %get-tuple-element.71), channel_id=1, source_target_pairs={{0,8},{1,9},{2,10},{3,11},{4,12},{5,13},{6,14},{7,15},{8,0},{9,1},... | collective-permute-start | bytes 24584 | tf_op jit(solution)/shard_map/ppermute | solution.py:236
  34.3 2.0 %collective-permute-done.14 = f32[16,128]{1,0:T(8,128)S(1)} collective-permute-done((f32[16,128]{1,0:T(8,128)S(1)}, f32[16,128]{1,0:T(8,128)S(1)}, u32[]{:S(2)}, u32[]{:S(2)}) %collective-permute-start.14) | collective-permute-done | bytes 8224 | tf_op jit(solution)/shard_map/ppermute | solution.py:236
  36.3 0.0 collective-permute-start.17
  36.3 1.3 %collective-permute-start.16 = (f32[16,128]{1,0:T(8,128)S(1)}, f32[16,128]{1,0:T(8,128)S(1)}, u32[]{:S(2)}, u32[]{:S(2)}) collective-permute-start(f32[16,128]{1,0:T(8,128)S(1)} %add.7.refs_4_), channel_id=1, source_target_pairs={{0,2},{1,3},{2,0},{3,1},{4,6},{5,7},{6,4},{7,5},{8,10},{9,11},{10,... | collective-permute-start | bytes 24584 | tf_op jit(solution)/shard_map/ppermute | solution.py:236
  37.6 0.6 %collective-permute-start.15 = (f32[16,128]{1,0:T(8,128)S(1)}, f32[16,128]{1,0:T(8,128)S(1)}, u32[]{:S(2)}, u32[]{:S(2)}) collective-permute-start(f32[16,128]{1,0:T(8,128)S(1)} %add.7.refs_4_), channel_id=1, source_target_pairs={{0,1},{1,0},{2,3},{3,2},{4,5},{5,4},{6,7},{7,6},{8,9},{9,8},{10,11... | collective-permute-start | bytes 24584 | tf_op jit(solution)/shard_map/ppermute | solution.py:236
  38.1 0.8 %shard_map.82.refs_0_ = f32[2048,512]{1,0:T(8,128)S(1)} custom-call(bf16[208,1024]{1,0:T(8,128)(2,1)S(1)} %get-tuple-element.41.lhs_ref, bf16[208,512]{1,0:T(8,128)(2,1)S(1)} %get-tuple-element.45.refs_0_, bf16[208,512]{1,0:T(8,128)(2,1)S(1)} %get-tuple-element.50.refs_1_, bf16[208,512]{1,0:T(8,128)(2,1)S(1)} %get-tuple-element.53.refs_2_, ...), custom_call_target="tpu_custom_call" | custom-call | flops 1000000000 | bytes 3906250 | tf_op jit(solution)/shard_map/pallas_call | solution.py:259
  38.9 0.6 %copy.8 = f32[512]{0:T(512)} copy(f32[512]{0:T(512)S(1)} %bitcast.11) | data formatting | bytes 4096
  39.5 0.0 collective-permute-done.17.refs_7_
  39.5 0.4 %collective-permute-done.16.refs_6_ = f32[16,128]{1,0:T(8,128)S(1)} collective-permute-done((f32[16,128]{1,0:T(8,128)S(1)}, f32[16,128]{1,0:T(8,128)S(1)}, u32[]{:S(2)}, u32[]{:S(2)}) %collective-permute-start.16) | collective-permute-done | bytes 8224 | tf_op jit(solution)/shard_map/ppermute | solution.py:236
  40.0 0.0 collective-permute-done.15.refs_5_
  40.0 2.3 %shard_map.86 = (f32[2048,512]{1,0:T(8,128)}, f32[16,128]{1,0:T(8,128)}) custom-call(f32[2048,512]{1,0:T(8,128)S(1)} %shard_map.82.refs_0_, f32[16,128]{1,0:T(8,128)S(1)} %get-tuple-element.56.refs_0_.refs_1_, f32[16,128]{1,0:T(8,128)S(1)} %get-tuple-element.69.refs_2_, f32[1,512]{1,0:T(1,128)S(1)} %get-tuple-element.70.refs_3_, f32[16,128]{1,0:T(8,128)S(1)} %add.7.refs_4_, ...), custom_call_target="tpu_custom_call" | custom-call | tf_op jit(solution)/shard_map/pallas_call | solution.py:351
  (3 shorter events, 0.0 us)
Async XLA Ops:
  0.6 10.1 %collective-permute-start.5 = (f32[64,128]{1,0:T(8,128)}, f32[64,128]{1,0:T(8,128)S(1)}, u32[]{:S(2)}, u32[]{:S(2)}) collective-permute-start(f32[64,128]{1,0:T(8,128)} %bitcast.14), channel_id=1, source_target_pairs={{0,8},{1,9},{2,10},{3,11},{4,12},{5,13},{6,14},{7,15},{8,0},{9,1},... | collective-permute-start | bytes 98312 | tf_op jit(solution)/shard_map/ppermute | solution.py:236
  4.7 6.2 %collective-permute-start.4 = (f32[64,128]{1,0:T(8,128)}, f32[64,128]{1,0:T(8,128)S(1)}, u32[]{:S(2)}, u32[]{:S(2)}) collective-permute-start(f32[64,128]{1,0:T(8,128)} %bitcast.15), channel_id=1, source_target_pairs={{0,12},{1,13},{2,14},{3,15},{4,8},{5,9},{6,10},{7,11},{8,4},{9,5},... | collective-permute-start | bytes 98312 | tf_op jit(solution)/shard_map/ppermute | solution.py:236
  6.1 4.9 %collective-permute-start.3 = (f32[64,128]{1,0:T(8,128)}, f32[64,128]{1,0:T(8,128)S(1)}, u32[]{:S(2)}, u32[]{:S(2)}) collective-permute-start(f32[64,128]{1,0:T(8,128)} %bitcast.16), channel_id=1, source_target_pairs={{0,4},{1,5},{2,6},{3,7},{4,0},{5,1},{6,2},{7,3},{8,12},{9,13},{10,... | collective-permute-start | bytes 98312 | tf_op jit(solution)/shard_map/ppermute | solution.py:236
  7.4 5.2 %collective-permute-start.2 = (f32[72,256]{1,0:T(8,128)S(1)}, f32[72,256]{1,0:T(8,128)S(1)}, u32[]{:S(2)}, u32[]{:S(2)}) collective-permute-start(f32[72,256]{1,0:T(8,128)S(1)} %get-tuple-element.39.refs_0_), channel_id=1, source_target_pairs={{0,16},{1,17},{2,18},{3,19},{4,20},{5,21},{6,22},{7,23},{8,24},{9,... | collective-permute-start | bytes 221192 | tf_op jit(solution)/shard_map/ppermute | solution.py:236
  9.0 5.3 %collective-permute-start.1 = (f32[72,256]{1,0:T(8,128)S(1)}, f32[72,256]{1,0:T(8,128)S(1)}, u32[]{:S(2)}, u32[]{:S(2)}) collective-permute-start(f32[72,256]{1,0:T(8,128)S(1)} %get-tuple-element.39.refs_0_), channel_id=1, source_target_pairs={{0,20},{1,21},{2,22},{3,23},{4,16},{5,17},{6,18},{7,19},{8,28},{9,... | collective-permute-start | bytes 221192 | tf_op jit(solution)/shard_map/ppermute | solution.py:236
  10.7 4.4 %collective-permute-start = (f32[72,256]{1,0:T(8,128)S(1)}, f32[72,256]{1,0:T(8,128)S(1)}, u32[]{:S(2)}, u32[]{:S(2)}) collective-permute-start(f32[72,256]{1,0:T(8,128)S(1)} %get-tuple-element.39.refs_0_), channel_id=1, source_target_pairs={{0,4},{1,5},{2,6},{3,7},{4,0},{5,1},{6,2},{7,3},{8,12},{9,13},{10,... | collective-permute-start | bytes 221192 | tf_op jit(solution)/shard_map/ppermute | solution.py:236
  11.0 5.0 %collective-permute-start.7 = (f32[4,64,128]{2,1,0:T(8,128)S(1)}, f32[4,64,128]{2,1,0:T(8,128)S(1)}, u32[]{:S(2)}, u32[]{:S(2)}) collective-permute-start(f32[4,64,128]{2,1,0:T(8,128)S(1)} %pad_maximum_fusion.refs_0_), channel_id=1, source_target_pairs={{0,2},{1,3},{2,0},{3,1},{4,6},{5,7},{6,4},{7,5},{8,10},{9,11},{10,... | collective-permute-start | bytes 393224 | tf_op jit(solution)/shard_map/ppermute | solution.py:236
  15.1 1.4 %collective-permute-start.6 = (f32[4,64,128]{2,1,0:T(8,128)S(1)}, f32[4,64,128]{2,1,0:T(8,128)S(1)}, u32[]{:S(2)}, u32[]{:S(2)}) collective-permute-start(f32[4,64,128]{2,1,0:T(8,128)S(1)} %pad_maximum_fusion.refs_0_), channel_id=1, source_target_pairs={{0,1},{1,0},{2,3},{3,2},{4,5},{5,4},{6,7},{7,6},{8,9},{9,8},{10,11... | collective-permute-start | bytes 393224 | tf_op jit(solution)/shard_map/ppermute | solution.py:236
  16.0 1.4 %collective-permute-start.8 = (f32[4,64,128]{2,1,0:T(8,128)S(1)}, f32[4,64,128]{2,1,0:T(8,128)S(1)}, u32[]{:S(2)}, u32[]{:S(2)}) collective-permute-start(f32[4,64,128]{2,1,0:T(8,128)S(1)} %collective-permute-done.7.refs_0_), channel_id=1, source_target_pairs={{0,1},{1,0},{2,3},{3,2},{4,5},{5,4},{6,7},{7,6},{8,9},{9,8},{10,11... | collective-permute-start | bytes 393224 | tf_op jit(solution)/shard_map/ppermute | solution.py:236
  17.9 4.6 %collective-permute-start.9 = (f32[16,128]{1,0:T(8,128)S(1)}, f32[16,128]{1,0:T(8,128)S(1)}, u32[]{:S(2)}, u32[]{:S(2)}) collective-permute-start(f32[16,128]{1,0:T(8,128)S(1)} %get-tuple-element.61), channel_id=1, source_target_pairs={{0,8},{1,9},{2,10},{3,11},{4,12},{5,13},{6,14},{7,15},{8,0},{9,1},... | collective-permute-start | bytes 24584 | tf_op jit(solution)/shard_map/ppermute | solution.py:236
  22.5 3.1 %collective-permute-start.12 = (f32[16,128]{1,0:T(8,128)S(1)}, f32[16,128]{1,0:T(8,128)S(1)}, u32[]{:S(2)}, u32[]{:S(2)}) collective-permute-start(f32[16,128]{1,0:T(8,128)S(1)} %add.6.refs_5_), channel_id=1, source_target_pairs={{0,3},{1,2},{2,1},{3,0},{4,7},{5,6},{6,5},{7,4},{8,11},{9,10},{10,... | collective-permute-start | bytes 24584 | tf_op jit(solution)/shard_map/ppermute | solution.py:236
  22.8 3.7 %collective-permute-start.11 = (f32[16,128]{1,0:T(8,128)S(1)}, f32[16,128]{1,0:T(8,128)S(1)}, u32[]{:S(2)}, u32[]{:S(2)}) collective-permute-start(f32[16,128]{1,0:T(8,128)S(1)} %add.6.refs_5_), channel_id=1, source_target_pairs={{0,2},{1,3},{2,0},{3,1},{4,6},{5,7},{6,4},{7,5},{8,10},{9,11},{10,... | collective-permute-start | bytes 24584 | tf_op jit(solution)/shard_map/ppermute | solution.py:236
  24.1 2.4 %collective-permute-start.10 = (f32[16,128]{1,0:T(8,128)S(1)}, f32[16,128]{1,0:T(8,128)S(1)}, u32[]{:S(2)}, u32[]{:S(2)}) collective-permute-start(f32[16,128]{1,0:T(8,128)S(1)} %add.6.refs_5_), channel_id=1, source_target_pairs={{0,1},{1,0},{2,3},{3,2},{4,5},{5,4},{6,7},{7,6},{8,9},{9,8},{10,11... | collective-permute-start | bytes 24584 | tf_op jit(solution)/shard_map/ppermute | solution.py:236
  27.2 3.7 %collective-permute-start.13 = (f32[8,128]{1,0:T(8,128)S(1)}, f32[8,128]{1,0:T(8,128)S(1)}, u32[]{:S(2)}, u32[]{:S(2)}) collective-permute-start(f32[8,128]{1,0:T(8,128)S(1)} %get-tuple-element.68.refs_7_), channel_id=1, source_target_pairs={{0,16},{16,0},{1,17},{17,1},{2,18},{18,2},{3,19},{19,3},{4,20},{20... | collective-permute-start | bytes 12296 | tf_op jit(solution)/shard_map/ppermute | solution.py:236
  31.7 4.6 %collective-permute-start.14 = (f32[16,128]{1,0:T(8,128)S(1)}, f32[16,128]{1,0:T(8,128)S(1)}, u32[]{:S(2)}, u32[]{:S(2)}) collective-permute-start(f32[16,128]{1,0:T(8,128)S(1)} %get-tuple-element.71), channel_id=1, source_target_pairs={{0,8},{1,9},{2,10},{3,11},{4,12},{5,13},{6,14},{7,15},{8,0},{9,1},... | collective-permute-start | bytes 24584 | tf_op jit(solution)/shard_map/ppermute | solution.py:236
  36.3 3.2 %collective-permute-start.17 = (f32[16,128]{1,0:T(8,128)S(1)}, f32[16,128]{1,0:T(8,128)S(1)}, u32[]{:S(2)}, u32[]{:S(2)}) collective-permute-start(f32[16,128]{1,0:T(8,128)S(1)} %add.7.refs_4_), channel_id=1, source_target_pairs={{0,3},{1,2},{2,1},{3,0},{4,7},{5,6},{6,5},{7,4},{8,11},{9,10},{10,... | collective-permute-start | bytes 24584 | tf_op jit(solution)/shard_map/ppermute | solution.py:236
  36.3 3.7 %collective-permute-start.16 = (f32[16,128]{1,0:T(8,128)S(1)}, f32[16,128]{1,0:T(8,128)S(1)}, u32[]{:S(2)}, u32[]{:S(2)}) collective-permute-start(f32[16,128]{1,0:T(8,128)S(1)} %add.7.refs_4_), channel_id=1, source_target_pairs={{0,2},{1,3},{2,0},{3,1},{4,6},{5,7},{6,4},{7,5},{8,10},{9,11},{10,... | collective-permute-start | bytes 24584 | tf_op jit(solution)/shard_map/ppermute | solution.py:236
  37.6 2.4 %collective-permute-start.15 = (f32[16,128]{1,0:T(8,128)S(1)}, f32[16,128]{1,0:T(8,128)S(1)}, u32[]{:S(2)}, u32[]{:S(2)}) collective-permute-start(f32[16,128]{1,0:T(8,128)S(1)} %add.7.refs_4_), channel_id=1, source_target_pairs={{0,1},{1,0},{2,3},{3,2},{4,5},{5,4},{6,7},{7,6},{8,9},{9,8},{10,11... | collective-permute-start | bytes 24584 | tf_op jit(solution)/shard_map/ppermute | solution.py:236

commit v9 on v7

--- a/solution.py
+++ b/solution.py
@@ -52,7 +52,7 @@
 
 def prepare_kernel(
     ratio, imps, elig_hbm, class_hbm, scale_hbm, imp_hbm, adv_hbm,
-    pack_ref, class_ref, scale_ref, own_ref, elig_ref, sems,
+    pack_ref, logs_ref, limit_ref, own_ref, elig_ref, class_ref, scale_ref, sems,
 ):
     moves = (
         (elig_hbm, elig_ref),
@@ -67,7 +67,10 @@
     pack_ref[EMB : EMB + 8, :] = jnp.zeros((8, pack_ref.shape[1]), F32)
     for copy in copies:
         copy.wait()
-    limit = ratio * jnp.exp(0.3 * class_ref[...].astype(F32) - 1.2)
+    exponent = 0.3 * class_ref[...].astype(F32) - 1.2
+    limit = ratio * jnp.exp(exponent)
+    limit_ref[...] = limit
+    logs_ref[...] = jnp.log(scale_ref[...]) * LOG2E + (exponent * LOG2E + math.log2(ratio / imps))
     rows, cols = class_ref.shape[0], elig_ref.shape[0]
     flags = elig_ref[...].astype(F32)
     allowance = limit / imps
@@ -92,10 +95,7 @@
     return jnp.concatenate(parts, axis=0).astype(BF16)
 
 
-def impressions_kernel(
-    cols, rows, ratio, imps, own_ref, down_ref, side_ref, cross_ref, class_ref, scale_ref,
-    lhs_ref, lhs_t_ref, extra_ref, price_ref, limit_ref,
-):
+def impressions_kernel(cols, rows, own_ref, down_ref, side_ref, cross_ref, logs_ref, lhs_ref, lhs_t_ref, extra_ref, price_ref):
     _, w = home()
     half = lax.axis_index("adv")
     width = own_ref.shape[1]
@@ -118,10 +118,7 @@
     lhs_ref[3 * EMB :, :] = jnp.concatenate(parts, axis=0).astype(BF16)
     lhs_t_ref[...] = lhs_ref[...].T
     flags = in_order(w, own_flags(own_ref, cols, rows), own_flags(side_ref, cols, rows))
-    exponent = 0.3 * class_ref[...].astype(F32) - 1.2
-    limit_ref[...] = ratio * jnp.exp(exponent)
-    logs = jnp.log(scale_ref[...]) * LOG2E + (exponent * LOG2E + math.log2(ratio / imps))
-    extra_ref[...] = extra_rows(flags, logs)
+    extra_ref[...] = extra_rows(flags, logs_ref[...])
 
 
 def first_kernel(keys, adv_ref, extra_ref, lhs_t_ref, *refs):
@@ -223,12 +220,15 @@
     pacing_ref[...] = limit / jnp.maximum(tree([ref[...] for ref in sum_refs]), limit)
     copies = []
     for n, k in enumerate(keys):
-        rows = slice(n * BLOCK, (n + 1) * BLOCK)
-        block_ref[rows, :] = gain_ref[rows, :] * as_column(pacing_ref[pl.ds(m ^ k, 1), :])
-        to = pl.ds(pl.multiple_of((m ^ k) * BLOCK, BLOCK), BLOCK)
-        copies.append(pltpu.make_async_copy(block_ref.at[rows], out_ref.at[to], sems.at[n]))
-        copies[-1].start()
-    copies.append(pltpu.make_async_copy(pacing_ref, pacing_out, sems.at[len(keys)]))
+        column = as_column(pacing_ref[pl.ds(m ^ k, 1), :])
+        step = BLOCK // 4 if n == 0 else BLOCK
+        for part in range(0, BLOCK, step):
+            rows = slice(n * BLOCK + part, n * BLOCK + part + step)
+            block_ref[rows, :] = gain_ref[rows, :] * column[part : part + step]
+            to = pl.ds(pl.multiple_of((m ^ k) * BLOCK + part, step), step)
+            copies.append(pltpu.make_async_copy(block_ref.at[rows], out_ref.at[to], sems.at[len(copies)]))
+            copies[-1].start()
+    copies.append(pltpu.make_async_copy(pacing_ref, pacing_out, sems.at[len(copies)]))
     copies[-1].start()
     for copy in copies:
         copy.wait()
@@ -271,13 +271,15 @@
     adv_t = adv_embed.T
     ins = (eligible.T, spend_class.reshape(rows, BLOCK), value_scale.reshape(rows, BLOCK), imp_embed.T, adv_t)
     ins = [pltpu.with_memory_space_constraint(x, pltpu.HBM) for x in ins]
-    pack, classes, scales, own = pl.pallas_call(
+    pack, logs, limit, own = pl.pallas_call(
         lambda *refs: prepare_kernel(ratio, imps, *refs),
-        out_shape=(shape(EMB + 8, imp_embed.shape[0]), shape(rows, BLOCK, dtype=jnp.int32), shape(rows, BLOCK), shape(*adv_t.shape)),
+        out_shape=(shape(EMB + 8, imp_embed.shape[0]), shape(rows, BLOCK), shape(rows, BLOCK), shape(*adv_t.shape)),
         in_specs=[HBM] * len(ins),
         out_specs=(VMEM,) * 4,
         scratch_shapes=[
             pltpu.VMEM((cols, rows), jnp.int32),
+            pltpu.VMEM((rows, BLOCK), jnp.int32),
+            pltpu.VMEM((rows, BLOCK), F32),
             pltpu.SemaphoreType.DMA((len(ins),)),
         ],
         compiler_params=PARAMS,
@@ -295,16 +297,15 @@
     keys = at_line + at_line_pair + at_plane + at_plane_pair
 
     count = 2 * imp_count
-    lhs, lhs_t, extra, first_price, limit = call(
-        lambda *refs: impressions_kernel(cols, rows, ratio, imps, *refs),
+    lhs, lhs_t, extra, first_price = call(
+        lambda *refs: impressions_kernel(cols, rows, *refs),
         (
             shape(DEPTH, count, dtype=BF16),
             shape(count, DEPTH, dtype=BF16),
             shape(16, adv_count, dtype=BF16),
             shape(2 * cols, BLOCK),
-            shape(rows, BLOCK),
         ),
-        (pack, down, side, cross, classes, scales),
+        (pack, down, side, cross, logs),
         cost=10**8,
     )
     gains, rhs, sums = [], [], ()
@@ -362,7 +363,7 @@
         scratch_shapes=[
             pltpu.VMEM((rows, BLOCK), F32),
             pltpu.VMEM((adv_count, imp_count), F32),
-            pltpu.SemaphoreType.DMA((rows + 1,)),
+            pltpu.SemaphoreType.DMA((rows + 4,)),
         ],
         compiler_params=PARAMS,
     )(gain_rows, limit, *terms)

time: 42.3 us -> 42.3 us (level)
  no operation moved by 1% of the time
where the time goes in v9:
time: 42.3 us; the launch traced here: 42.1 us
  starting transfers between devices  21.8 us (52%)
  waiting for transfers between devices  10.4 us (25%)
  Pallas kernels  8.62 us (20%)
  between operations  0.72 us (2%)
  local copies, waits for them, and re-layouts  0.58 us (1%)
    ppermute x18, starting transfers between devices, swap(): lax.ppermute(x, axis, [(i, i ^ k) for i in range(lax.axis_size(axis))])  21.8 us
    ppermute x18, waiting for transfers between devices, swap(): lax.ppermute(x, axis, [(i, i ^ k) for i in range(lax.axis_size(axis))])  10.4 us
    pallas_call x9, Pallas kernels, call(): pl.pallas_call(kernel, out_shape=out, in_specs=[VMEM] * len(operands), ou...  5.29 us
    pallas_call x1, Pallas kernels, staged(): pl.pallas_call(lambda *refs: final_kernel(keys, *refs), out_shape=(shape(...  2.27 us
    pallas_call x1, Pallas kernels, staged(): pl.pallas_call(lambda *refs: prepare_kernel(ratio, imps, *refs), out_shap...  1.07 us
  transfers between devices with their start and end apart: 18, of which 11 were waited for; matrix products, arithmetic and copies ran while one was open for 1% of the time, Pallas kernels for 10%

profile of v9, /device:TPU:0, one launch (start us, length us, event | category | flops | bytes accessed | tf_op | source)
XLA Modules:
  0.0 42.1 jit_solution(3986400828889293258)
XLA Ops:
  0.6 4.1 %collective-permute-start.5 = (f32[64,128]{1,0:T(8,128)}, f32[64,128]{1,0:T(8,128)S(1)}, u32[]{:S(2)}, u32[]{:S(2)}) collective-permute-start(f32[64,128]{1,0:T(8,128)} %bitcast.14), channel_id=1, source_target_pairs={{0,8},{1,9},{2,10},{3,11},{4,12},{5,13},{6,14},{7,15},{8,0},{9,1},... | collective-permute-start | bytes 98312 | tf_op jit(solution)/shard_map/ppermute | solution.py:238
  4.7 1.3 %collective-permute-start.4 = (f32[64,128]{1,0:T(8,128)}, f32[64,128]{1,0:T(8,128)S(1)}, u32[]{:S(2)}, u32[]{:S(2)}) collective-permute-start(f32[64,128]{1,0:T(8,128)} %bitcast.15), channel_id=1, source_target_pairs={{0,12},{1,13},{2,14},{3,15},{4,8},{5,9},{6,10},{7,11},{8,4},{9,5},... | collective-permute-start | bytes 98312 | tf_op jit(solution)/shard_map/ppermute | solution.py:238
  6.1 0.2 collective-permute-start.3
  6.3 1.1 %shard_map.76 = (f32[72,256]{1,0:T(8,128)S(1)}, f32[16,128]{1,0:T(8,128)S(1)}, f32[16,128]{1,0:T(8,128)S(1)}, f32[64,128]{1,0:T(8,128)S(1)}) custom-call(s32[4,16]{1,0:T(4,128)} %bitcast.23, s32[16,128]{1,0:T(8,128)} %bitcast.21, f32[16,128]{1,0:T(8,128)} %bitcast.22, f32[64,256]{1,0:T(8,128)} %bitcast.13, f32[64,128]{1,0:T(8,128)} %bitcast.17), custom_call_target="tpu_custom_call" | custom-call | tf_op jit(solution)/shard_map/pallas_call | solution.py:274
  7.4 2.8 %collective-permute-start.2 = (f32[72,256]{1,0:T(8,128)S(1)}, f32[72,256]{1,0:T(8,128)S(1)}, u32[]{:S(2)}, u32[]{:S(2)}) collective-permute-start(f32[72,256]{1,0:T(8,128)S(1)} %get-tuple-element.39.refs_0_), channel_id=1, source_target_pairs={{0,20},{1,21},{2,22},{3,23},{4,16},{5,17},{6,18},{7,19},{8,28},{9,... | collective-permute-start | bytes 221192 | tf_op jit(solution)/shard_map/ppermute | solution.py:238
  10.2 0.2 collective-permute-start.1
  10.4 0.0 collective-permute-done.5
  10.4 0.5 %collective-permute-start = (f32[72,256]{1,0:T(8,128)S(1)}, f32[72,256]{1,0:T(8,128)S(1)}, u32[]{:S(2)}, u32[]{:S(2)}) collective-permute-start(f32[72,256]{1,0:T(8,128)S(1)} %get-tuple-element.39.refs_0_), channel_id=1, source_target_pairs={{0,16},{1,17},{2,18},{3,19},{4,20},{5,21},{6,22},{7,23},{8,24},{9,... | collective-permute-start | bytes 221192 | tf_op jit(solution)/shard_map/ppermute | solution.py:238
  10.9 0.0 collective-permute-done.4
  11.0 0.0 collective-permute-done.3
  11.0 1.6 %collective-permute-start.7 = (f32[4,64,128]{2,1,0:T(8,128)S(1)}, f32[4,64,128]{2,1,0:T(8,128)S(1)}, u32[]{:S(2)}, u32[]{:S(2)}) collective-permute-start(f32[4,64,128]{2,1,0:T(8,128)S(1)} %pad_maximum_fusion.refs_0_), channel_id=1, source_target_pairs={{0,2},{1,3},{2,0},{3,1},{4,6},{5,7},{6,4},{7,5},{8,10},{9,11},{10,... | collective-permute-start | bytes 393224 | tf_op jit(solution)/shard_map/ppermute | solution.py:238
  12.5 0.8 %collective-permute-done.2.refs_3_ = f32[72,256]{1,0:T(8,128)S(1)} collective-permute-done((f32[72,256]{1,0:T(8,128)S(1)}, f32[72,256]{1,0:T(8,128)S(1)}, u32[]{:S(2)}, u32[]{:S(2)}) %collective-permute-start.2) | collective-permute-done | bytes 73760 | tf_op jit(solution)/shard_map/ppermute | solution.py:238
  13.3 1.2 %collective-permute-done.1.refs_2_ = f32[72,256]{1,0:T(8,128)S(1)} collective-permute-done((f32[72,256]{1,0:T(8,128)S(1)}, f32[72,256]{1,0:T(8,128)S(1)}, u32[]{:S(2)}, u32[]{:S(2)}) %collective-permute-start.1) | collective-permute-done | bytes 73760 | tf_op jit(solution)/shard_map/ppermute | solution.py:238
  14.6 0.2 collective-permute-done.refs_1_
  14.8 0.0 collective-permute-start.6
  14.8 0.3 shard_map.77
  15.1 0.5 %shard_map.78 = (f32[1024,512]{1,0:T(8,128)S(1)}, f32[16,128]{1,0:T(8,128)S(1)}, bf16[208,512]{1,0:T(8,128)(2,1)S(1)}) custom-call(f32[4,64,128]{2,1,0:T(8,128)S(1)} %pad_maximum_fusion.refs_0_, bf16[16,2048]{1,0:T(8,128)(2,1)S(1)} %get-tuple-element.44.refs_1_, bf16[1024,208]{1,0:T(8,128)(2,1)S(1)} %get-tuple-element.45.refs_2_), custom_call_target="tpu_custom_call" | custom-call | flops 400000000 | bytes 1562500 | tf_op jit(solution)/shard_map/pallas_call | solution.py:261
  15.6 0.4 %collective-permute-done.7.refs_0_ = f32[4,64,128]{2,1,0:T(8,128)S(1)} collective-permute-done((f32[4,64,128]{2,1,0:T(8,128)S(1)}, f32[4,64,128]{2,1,0:T(8,128)S(1)}, u32[]{:S(2)}, u32[]{:S(2)}) %collective-permute-start.7) | collective-permute-done | bytes 131104 | tf_op jit(solution)/shard_map/ppermute | solution.py:238
  16.0 0.2 collective-permute-start.8
  16.2 0.0 collective-permute-done.6.refs_0_
  16.2 0.5 %shard_map.79 = (f32[1024,512]{1,0:T(8,128)S(1)}, f32[16,128]{1,0:T(8,128)S(1)}, bf16[208,512]{1,0:T(8,128)(2,1)S(1)}) custom-call(f32[4,64,128]{2,1,0:T(8,128)S(1)} %collective-permute-done.6.refs_0_, bf16[16,2048]{1,0:T(8,128)(2,1)S(1)} %get-tuple-element.44.refs_1_, bf16[1024,208]{1,0:T(8,128)(2,1)S(1)} %get-tuple-element.45.refs_2_, ...), custom_call_target="tpu_custom_call" | custom-call | flops 400000000 | bytes 1562500 | tf_op jit(solution)/shard_map/pallas_call | solution.py:261
  16.6 0.5 %shard_map.80 = (f32[1024,512]{1,0:T(8,128)S(1)}, f32[16,128]{1,0:T(8,128)S(1)}, bf16[208,512]{1,0:T(8,128)(2,1)S(1)}) custom-call(f32[4,64,128]{2,1,0:T(8,128)S(1)} %collective-permute-done.7.refs_0_, bf16[16,2048]{1,0:T(8,128)(2,1)S(1)} %get-tuple-element.44.refs_1_, bf16[1024,208]{1,0:T(8,128)(2,1)S(1)} %get-tuple-element.45.refs_2_, ...), custom_call_target="tpu_custom_call" | custom-call | flops 400000000 | bytes 1562500 | tf_op jit(solution)/shard_map/pallas_call | solution.py:261
  17.1 0.3 collective-permute-done.8.refs_0_
  17.4 0.5 %shard_map.81 = (f32[1024,512]{1,0:T(8,128)S(1)}, f32[16,128]{1,0:T(8,128)S(1)}, bf16[208,512]{1,0:T(8,128)(2,1)S(1)}) custom-call(f32[4,64,128]{2,1,0:T(8,128)S(1)} %collective-permute-done.8.refs_0_, bf16[16,2048]{1,0:T(8,128)(2,1)S(1)} %get-tuple-element.44.refs_1_, bf16[1024,208]{1,0:T(8,128)(2,1)S(1)} %get-tuple-element.45.refs_2_, ...), custom_call_target="tpu_custom_call" | custom-call | flops 400000000 | bytes 1562500 | tf_op jit(solution)/shard_map/pallas_call | solution.py:261
  17.8 2.9 %collective-permute-start.9 = (f32[16,128]{1,0:T(8,128)S(1)}, f32[16,128]{1,0:T(8,128)S(1)}, u32[]{:S(2)}, u32[]{:S(2)}) collective-permute-start(f32[16,128]{1,0:T(8,128)S(1)} %get-tuple-element.57), channel_id=1, source_target_pairs={{0,8},{1,9},{2,10},{3,11},{4,12},{5,13},{6,14},{7,15},{8,0},{9,1},... | collective-permute-start | bytes 24584 | tf_op jit(solution)/shard_map/ppermute | solution.py:238
  20.7 1.7 %collective-permute-done.9 = f32[16,128]{1,0:T(8,128)S(1)} collective-permute-done((f32[16,128]{1,0:T(8,128)S(1)}, f32[16,128]{1,0:T(8,128)S(1)}, u32[]{:S(2)}, u32[]{:S(2)}) %collective-permute-start.9) | collective-permute-done | bytes 8224 | tf_op jit(solution)/shard_map/ppermute | solution.py:238
  22.4 0.3 collective-permute-start.12
  22.7 1.2 %collective-permute-start.11 = (f32[16,128]{1,0:T(8,128)S(1)}, f32[16,128]{1,0:T(8,128)S(1)}, u32[]{:S(2)}, u32[]{:S(2)}) collective-permute-start(f32[16,128]{1,0:T(8,128)S(1)} %add.6.refs_5_), channel_id=1, source_target_pairs={{0,2},{1,3},{2,0},{3,1},{4,6},{5,7},{6,4},{7,5},{8,10},{9,11},{10,... | collective-permute-start | bytes 24584 | tf_op jit(solution)/shard_map/ppermute | solution.py:238
  24.0 0.3 collective-permute-start.10
  24.3 1.3 %collective-permute-done.12.refs_8_ = f32[16,128]{1,0:T(8,128)S(1)} collective-permute-done((f32[16,128]{1,0:T(8,128)S(1)}, f32[16,128]{1,0:T(8,128)S(1)}, u32[]{:S(2)}, u32[]{:S(2)}) %collective-permute-start.12) | collective-permute-done | bytes 8224 | tf_op jit(solution)/shard_map/ppermute | solution.py:238
  25.6 0.8 %collective-permute-done.11.refs_7_ = f32[16,128]{1,0:T(8,128)S(1)} collective-permute-done((f32[16,128]{1,0:T(8,128)S(1)}, f32[16,128]{1,0:T(8,128)S(1)}, u32[]{:S(2)}, u32[]{:S(2)}) %collective-permute-start.11) | collective-permute-done | bytes 8224 | tf_op jit(solution)/shard_map/ppermute | solution.py:238
  26.4 0.0 collective-permute-done.10.refs_6_
  26.4 0.7 %shard_map.82 = (f32[8,128]{1,0:T(8,128)S(1)}, f32[16,128]{1,0:T(8,128)S(1)}) custom-call(f32[16,128]{1,0:T(8,128)S(1)} %get-tuple-element.42.refs_0_.refs_1_, f32[1024,512]{1,0:T(8,128)S(1)} %get-tuple-element.46.refs_1_.refs_0_, f32[1024,512]{1,0:T(8,128)S(1)} %get-tuple-element.51.refs_2_.refs_1_, f32[1024,512]{1,0:T(8,128)S(1)} %get-tuple-element.54.refs_3_.refs_2_, ...), custom_call_target="tpu_custom_call" | custom-call | tf_op jit(solution)/shard_map/pallas_call | solution.py:261
  27.1 1.6 %collective-permute-start.13 = (f32[8,128]{1,0:T(8,128)S(1)}, f32[8,128]{1,0:T(8,128)S(1)}, u32[]{:S(2)}, u32[]{:S(2)}) collective-permute-start(f32[8,128]{1,0:T(8,128)S(1)} %get-tuple-element.64.refs_7_), channel_id=1, source_target_pairs={{0,16},{16,0},{1,17},{17,1},{2,18},{18,2},{3,19},{19,3},{4,20},{20... | collective-permute-start | bytes 12296 | tf_op jit(solution)/shard_map/ppermute | solution.py:238
  28.7 0.5 %shard_map.83 = (f32[1024,512]{1,0:T(8,128)S(1)}, f32[1024,512]{1,0:T(8,128)S(1)}, f32[1024,512]{1,0:T(8,128)S(1)}, f32[1024,512]{1,0:T(8,128)S(1)}) custom-call(f32[1024,512]{1,0:T(8,128)S(1)} %get-tuple-element.46.refs_1_.refs_0_, f32[1024,512]{1,0:T(8,128)S(1)} %get-tuple-element.51.refs_2_.refs_1_, f32[1024,512]{1,0:T(8,128)S(1)} %get-tuple-element.54.refs_3_.refs_2_, ...), custom_call_target="tpu_custom_call" | custom-call | flops 1000000000 | bytes 3906250 | tf_op jit(solution)/shard_map/pallas_call | solution.py:261
  29.2 1.6 %collective-permute-done.13.refs_8_ = f32[8,128]{1,0:T(8,128)S(1)} collective-permute-done((f32[8,128]{1,0:T(8,128)S(1)}, f32[8,128]{1,0:T(8,128)S(1)}, u32[]{:S(2)}, u32[]{:S(2)}) %collective-permute-start.13) | collective-permute-done | bytes 4128 | tf_op jit(solution)/shard_map/ppermute | solution.py:238
  30.8 0.8 %shard_map.84 = (f32[16,128]{1,0:T(8,128)S(1)}, f32[4,128]{1,0:T(4,128)S(1)}, f32[16,128]{1,0:T(8,128)S(1)}, f32[1,512]{1,0:T(1,128)S(1)}) custom-call(f32[16,128]{1,0:T(8,128)S(1)} %get-tuple-element.42.refs_0_.refs_1_, f32[16,128]{1,0:T(8,128)S(1)} %get-tuple-element.58.refs_1_, f32[8,128]{1,0:T(8,128)S(1)} %get-tuple-element.59.refs_2_, ...), custom_call_target="tpu_custom_call" | custom-call | tf_op jit(solution)/shard_map/pallas_call | solution.py:261
  31.5 2.7 %collective-permute-start.14 = (f32[16,128]{1,0:T(8,128)S(1)}, f32[16,128]{1,0:T(8,128)S(1)}, u32[]{:S(2)}, u32[]{:S(2)}) collective-permute-start(f32[16,128]{1,0:T(8,128)S(1)} %get-tuple-element.71), channel_id=1, source_target_pairs={{0,8},{1,9},{2,10},{3,11},{4,12},{5,13},{6,14},{7,15},{8,0},{9,1},... | collective-permute-start | bytes 24584 | tf_op jit(solution)/shard_map/ppermute | solution.py:238
  34.3 1.9 %collective-permute-done.14 = f32[16,128]{1,0:T(8,128)S(1)} collective-permute-done((f32[16,128]{1,0:T(8,128)S(1)}, f32[16,128]{1,0:T(8,128)S(1)}, u32[]{:S(2)}, u32[]{:S(2)}) %collective-permute-start.14) | collective-permute-done | bytes 8224 | tf_op jit(solution)/shard_map/ppermute | solution.py:238
  36.2 0.0 collective-permute-start.17
  36.2 1.3 %collective-permute-start.16 = (f32[16,128]{1,0:T(8,128)S(1)}, f32[16,128]{1,0:T(8,128)S(1)}, u32[]{:S(2)}, u32[]{:S(2)}) collective-permute-start(f32[16,128]{1,0:T(8,128)S(1)} %add.7.refs_2_), channel_id=1, source_target_pairs={{0,2},{1,3},{2,0},{3,1},{4,6},{5,7},{6,4},{7,5},{8,10},{9,11},{10,... | collective-permute-start | bytes 24584 | tf_op jit(solution)/shard_map/ppermute | solution.py:238
  37.4 0.6 %collective-permute-start.15 = (f32[16,128]{1,0:T(8,128)S(1)}, f32[16,128]{1,0:T(8,128)S(1)}, u32[]{:S(2)}, u32[]{:S(2)}) collective-permute-start(f32[16,128]{1,0:T(8,128)S(1)} %add.7.refs_2_), channel_id=1, source_target_pairs={{0,1},{1,0},{2,3},{3,2},{4,5},{5,4},{6,7},{7,6},{8,9},{9,8},{10,11... | collective-permute-start | bytes 24584 | tf_op jit(solution)/shard_map/ppermute | solution.py:238
  38.0 1.1 %shard_map.85.refs_0_ = f32[2048,512]{1,0:T(8,128)S(1)} custom-call(bf16[208,1024]{1,0:T(8,128)(2,1)S(1)} %get-tuple-element.41.refs_0_, f32[16,128]{1,0:T(8,128)S(1)} %get-tuple-element.65.refs_1_, f32[1,512]{1,0:T(1,128)S(1)} %get-tuple-element.66.refs_2_, bf16[208,512]{1,0:T(8,128)(2,1)S(1)} %get-tuple-element.67.refs_3_, ...), custom_call_target="tpu_custom_call" | custom-call | flops 1000000000 | bytes 3906250 | tf_op jit(solution)/shard_map/pallas_call | solution.py:261
  39.1 0.6 %copy.8 = f32[512]{0:T(512)} copy(f32[512]{0:T(512)S(1)} %bitcast.11) | data formatting | bytes 4096
  39.7 0.0 collective-permute-done.17.refs_5_
  39.7 0.1 collective-permute-done.16.refs_4_
  39.8 0.0 collective-permute-done.15.refs_3_
  39.9 2.3 %shard_map.86 = (f32[2048,512]{1,0:T(8,128)}, f32[16,128]{1,0:T(8,128)}) custom-call(f32[2048,512]{1,0:T(8,128)S(1)} %shard_map.85.refs_0_, f32[16,128]{1,0:T(8,128)S(1)} %get-tuple-element.42.refs_0_.refs_1_, f32[16,128]{1,0:T(8,128)S(1)} %add.7.refs_2_, f32[16,128]{1,0:T(8,128)S(1)} %collective-permute-done.15.refs_3_, ...), custom_call_target="tpu_custom_call" | custom-call | tf_op jit(solution)/shard_map/pallas_call | solution.py:358
  (3 shorter events, 0.0 us)
Async XLA Ops:
  0.6 9.8 %collective-permute-start.5 = (f32[64,128]{1,0:T(8,128)}, f32[64,128]{1,0:T(8,128)S(1)}, u32[]{:S(2)}, u32[]{:S(2)}) collective-permute-start(f32[64,128]{1,0:T(8,128)} %bitcast.14), channel_id=1, source_target_pairs={{0,8},{1,9},{2,10},{3,11},{4,12},{5,13},{6,14},{7,15},{8,0},{9,1},... | collective-permute-start | bytes 98312 | tf_op jit(solution)/shard_map/ppermute | solution.py:238
  4.7 6.2 %collective-permute-start.4 = (f32[64,128]{1,0:T(8,128)}, f32[64,128]{1,0:T(8,128)S(1)}, u32[]{:S(2)}, u32[]{:S(2)}) collective-permute-start(f32[64,128]{1,0:T(8,128)} %bitcast.15), channel_id=1, source_target_pairs={{0,12},{1,13},{2,14},{3,15},{4,8},{5,9},{6,10},{7,11},{8,4},{9,5},... | collective-permute-start | bytes 98312 | tf_op jit(solution)/shard_map/ppermute | solution.py:238
  6.1 4.9 %collective-permute-start.3 = (f32[64,128]{1,0:T(8,128)}, f32[64,128]{1,0:T(8,128)S(1)}, u32[]{:S(2)}, u32[]{:S(2)}) collective-permute-start(f32[64,128]{1,0:T(8,128)} %bitcast.16), channel_id=1, source_target_pairs={{0,4},{1,5},{2,6},{3,7},{4,0},{5,1},{6,2},{7,3},{8,12},{9,13},{10,... | collective-permute-start | bytes 98312 | tf_op jit(solution)/shard_map/ppermute | solution.py:238
  7.4 5.9 %collective-permute-start.2 = (f32[72,256]{1,0:T(8,128)S(1)}, f32[72,256]{1,0:T(8,128)S(1)}, u32[]{:S(2)}, u32[]{:S(2)}) collective-permute-start(f32[72,256]{1,0:T(8,128)S(1)} %get-tuple-element.39.refs_0_), channel_id=1, source_target_pairs={{0,20},{1,21},{2,22},{3,23},{4,16},{5,17},{6,18},{7,19},{8,28},{9,... | collective-permute-start | bytes 221192 | tf_op jit(solution)/shard_map/ppermute | solution.py:238
  10.2 4.4 %collective-permute-start.1 = (f32[72,256]{1,0:T(8,128)S(1)}, f32[72,256]{1,0:T(8,128)S(1)}, u32[]{:S(2)}, u32[]{:S(2)}) collective-permute-start(f32[72,256]{1,0:T(8,128)S(1)} %get-tuple-element.39.refs_0_), channel_id=1, source_target_pairs={{0,4},{1,5},{2,6},{3,7},{4,0},{5,1},{6,2},{7,3},{8,12},{9,13},{10,... | collective-permute-start | bytes 221192 | tf_op jit(solution)/shard_map/ppermute | solution.py:238
  10.4 4.4 %collective-permute-start = (f32[72,256]{1,0:T(8,128)S(1)}, f32[72,256]{1,0:T(8,128)S(1)}, u32[]{:S(2)}, u32[]{:S(2)}) collective-permute-start(f32[72,256]{1,0:T(8,128)S(1)} %get-tuple-element.39.refs_0_), channel_id=1, source_target_pairs={{0,16},{1,17},{2,18},{3,19},{4,20},{5,21},{6,22},{7,23},{8,24},{9,... | collective-permute-start | bytes 221192 | tf_op jit(solution)/shard_map/ppermute | solution.py:238
  11.0 5.0 %collective-permute-start.7 = (f32[4,64,128]{2,1,0:T(8,128)S(1)}, f32[4,64,128]{2,1,0:T(8,128)S(1)}, u32[]{:S(2)}, u32[]{:S(2)}) collective-permute-start(f32[4,64,128]{2,1,0:T(8,128)S(1)} %pad_maximum_fusion.refs_0_), channel_id=1, source_target_pairs={{0,2},{1,3},{2,0},{3,1},{4,6},{5,7},{6,4},{7,5},{8,10},{9,11},{10,... | collective-permute-start | bytes 393224 | tf_op jit(solution)/shard_map/ppermute | solution.py:238
  14.8 1.4 %collective-permute-start.6 = (f32[4,64,128]{2,1,0:T(8,128)S(1)}, f32[4,64,128]{2,1,0:T(8,128)S(1)}, u32[]{:S(2)}, u32[]{:S(2)}) collective-permute-start(f32[4,64,128]{2,1,0:T(8,128)S(1)} %pad_maximum_fusion.refs_0_), channel_id=1, source_target_pairs={{0,1},{1,0},{2,3},{3,2},{4,5},{5,4},{6,7},{7,6},{8,9},{9,8},{10,11... | collective-permute-start | bytes 393224 | tf_op jit(solution)/shard_map/ppermute | solution.py:238
  16.0 1.3 %collective-permute-start.8 = (f32[4,64,128]{2,1,0:T(8,128)S(1)}, f32[4,64,128]{2,1,0:T(8,128)S(1)}, u32[]{:S(2)}, u32[]{:S(2)}) collective-permute-start(f32[4,64,128]{2,1,0:T(8,128)S(1)} %collective-permute-done.7.refs_0_), channel_id=1, source_target_pairs={{0,1},{1,0},{2,3},{3,2},{4,5},{5,4},{6,7},{7,6},{8,9},{9,8},{10,11... | collective-permute-start | bytes 393224 | tf_op jit(solution)/shard_map/ppermute | solution.py:238
  17.8 4.6 %collective-permute-start.9 = (f32[16,128]{1,0:T(8,128)S(1)}, f32[16,128]{1,0:T(8,128)S(1)}, u32[]{:S(2)}, u32[]{:S(2)}) collective-permute-start(f32[16,128]{1,0:T(8,128)S(1)} %get-tuple-element.57), channel_id=1, source_target_pairs={{0,8},{1,9},{2,10},{3,11},{4,12},{5,13},{6,14},{7,15},{8,0},{9,1},... | collective-permute-start | bytes 24584 | tf_op jit(solution)/shard_map/ppermute | solution.py:238
  22.4 3.1 %collective-permute-start.12 = (f32[16,128]{1,0:T(8,128)S(1)}, f32[16,128]{1,0:T(8,128)S(1)}, u32[]{:S(2)}, u32[]{:S(2)}) collective-permute-start(f32[16,128]{1,0:T(8,128)S(1)} %add.6.refs_5_), channel_id=1, source_target_pairs={{0,3},{1,2},{2,1},{3,0},{4,7},{5,6},{6,5},{7,4},{8,11},{9,10},{10,... | collective-permute-start | bytes 24584 | tf_op jit(solution)/shard_map/ppermute | solution.py:238
  22.7 3.7 %collective-permute-start.11 = (f32[16,128]{1,0:T(8,128)S(1)}, f32[16,128]{1,0:T(8,128)S(1)}, u32[]{:S(2)}, u32[]{:S(2)}) collective-permute-start(f32[16,128]{1,0:T(8,128)S(1)} %add.6.refs_5_), channel_id=1, source_target_pairs={{0,2},{1,3},{2,0},{3,1},{4,6},{5,7},{6,4},{7,5},{8,10},{9,11},{10,... | collective-permute-start | bytes 24584 | tf_op jit(solution)/shard_map/ppermute | solution.py:238
  24.0 2.4 %collective-permute-start.10 = (f32[16,128]{1,0:T(8,128)S(1)}, f32[16,128]{1,0:T(8,128)S(1)}, u32[]{:S(2)}, u32[]{:S(2)}) collective-permute-start(f32[16,128]{1,0:T(8,128)S(1)} %add.6.refs_5_), channel_id=1, source_target_pairs={{0,1},{1,0},{2,3},{3,2},{4,5},{5,4},{6,7},{7,6},{8,9},{9,8},{10,11... | collective-permute-start | bytes 24584 | tf_op jit(solution)/shard_map/ppermute | solution.py:238
  27.1 3.7 %collective-permute-start.13 = (f32[8,128]{1,0:T(8,128)S(1)}, f32[8,128]{1,0:T(8,128)S(1)}, u32[]{:S(2)}, u32[]{:S(2)}) collective-permute-start(f32[8,128]{1,0:T(8,128)S(1)} %get-tuple-element.64.refs_7_), channel_id=1, source_target_pairs={{0,16},{16,0},{1,17},{17,1},{2,18},{18,2},{3,19},{19,3},{4,20},{20... | collective-permute-start | bytes 12296 | tf_op jit(solution)/shard_map/ppermute | solution.py:238
  31.5 4.6 %collective-permute-start.14 = (f32[16,128]{1,0:T(8,128)S(1)}, f32[16,128]{1,0:T(8,128)S(1)}, u32[]{:S(2)}, u32[]{:S(2)}) collective-permute-start(f32[16,128]{1,0:T(8,128)S(1)} %get-tuple-element.71), channel_id=1, source_target_pairs={{0,8},{1,9},{2,10},{3,11},{4,12},{5,13},{6,14},{7,15},{8,0},{9,1},... | collective-permute-start | bytes 24584 | tf_op jit(solution)/shard_map/ppermute | solution.py:238
  36.2 3.6 %collective-permute-start.17 = (f32[16,128]{1,0:T(8,128)S(1)}, f32[16,128]{1,0:T(8,128)S(1)}, u32[]{:S(2)}, u32[]{:S(2)}) collective-permute-start(f32[16,128]{1,0:T(8,128)S(1)} %add.7.refs_2_), channel_id=1, source_target_pairs={{0,3},{1,2},{2,1},{3,0},{4,7},{5,6},{6,5},{7,4},{8,11},{9,10},{10,... | collective-permute-start | bytes 24584 | tf_op jit(solution)/shard_map/ppermute | solution.py:238
  36.2 3.7 %collective-permute-start.16 = (f32[16,128]{1,0:T(8,128)S(1)}, f32[16,128]{1,0:T(8,128)S(1)}, u32[]{:S(2)}, u32[]{:S(2)}) collective-permute-start(f32[16,128]{1,0:T(8,128)S(1)} %add.7.refs_2_), channel_id=1, source_target_pairs={{0,2},{1,3},{2,0},{3,1},{4,6},{5,7},{6,4},{7,5},{8,10},{9,11},{10,... | collective-permute-start | bytes 24584 | tf_op jit(solution)/shard_map/ppermute | solution.py:238
  37.4 2.4 %collective-permute-start.15 = (f32[16,128]{1,0:T(8,128)S(1)}, f32[16,128]{1,0:T(8,128)S(1)}, u32[]{:S(2)}, u32[]{:S(2)}) collective-permute-start(f32[16,128]{1,0:T(8,128)S(1)} %add.7.refs_2_), channel_id=1, source_target_pairs={{0,1},{1,0},{2,3},{3,2},{4,5},{5,4},{6,7},{7,6},{8,9},{9,8},{10,11... | collective-permute-start | bytes 24584 | tf_op jit(solution)/shard_map/ppermute | solution.py:238
